TPU v7x, 32 devices: a whole 2x2x4 slice. The times are simulated.
32 devices in a mesh: dp: 4 (over x, core), seq: 4 (over z), tensor: 2 (over y).
Axes of the slice: x: 2, y: 2, z: 4, core: 2. Of those that a mesh axis runs over, the one named last changes fastest.
Arguments:
- inputs: bfloat16 [2, 4, 512, 2048], P(None, 'dp', 'seq'), may hold values from -20 to 20
- skip_mask: int32 [2, 4], P(None, 'dp'), may hold values 0 or 1
- block_order: int32 [2, 4, 8], P(None, 'dp'), may hold values from 0 to 7, as said below
- norm1_gain: bfloat16 [2048], replicated, may hold values from 0.3 to 3
- query_weight: bfloat16 [2048, 2048], P(None, 'tensor'), may hold values from -0.125 to 0.125
- key_weight: bfloat16 [2048, 1024], P(None, 'tensor'), may hold values from -0.125 to 0.125
- value_weight: bfloat16 [2048, 1024], P(None, 'tensor'), may hold values from -0.125 to 0.125
- w_out: bfloat16 [2048, 2048], P('tensor'), may hold values from -0.5 to 0.5
- norm2_gain: bfloat16 [2048], replicated, may hold values from 0.25 to 1.75
- w_gate: bfloat16 [2048, 5632], P(None, 'tensor'), may hold values from -0.125 to 0.125
- w_up: bfloat16 [2048, 5632], P(None, 'tensor'), may hold values from -0.125 to 0.125
- w_down: bfloat16 [5632, 2048], P('tensor'), may hold values from -0.078125 to 0.078125
- out_grad: bfloat16 [2, 4, 512, 2048], P(None, 'dp', 'seq'), may hold values from -6 to 6
Outputs:
- output: bfloat16 [2, 4, 512, 2048], P(None, 'dp', 'seq', 'tensor')
- input_grad: float32 [2, 4, 512, 2048], P(None, 'dp', 'seq', 'tensor')
- grad_norm1: float32 [2048], P('tensor')
- grad_query: float32 [2048, 2048], P(None, 'tensor')
- grad_key: float32 [2048, 1024], P(None, 'tensor')
- grad_value: float32 [2048, 1024], P(None, 'tensor')
- grad_out: float32 [2048, 2048], P('tensor')
- grad_norm2: float32 [2048], P('tensor')
- grad_gate: float32 [2048, 5632], P(None, 'tensor')
- grad_up: float32 [2048, 5632], P(None, 'tensor')
- grad_down: float32 [5632, 2048], P('tensor')
Inputs may be any that keep to these rules, and one draw needn't show every extreme that they name: `skip_mask`: 1 marks a sample that passes through unchanged. `block_order`: each row is a permutation of the 8 position blocks in which stored blocks 2 s and 2 s + 1 hold position blocks r and 7 - r for some r, in either order, so each seq device holds one early and one late block.
All inputs are finite; a program needn't handle non-finite values. No bound on the sum of `skip_mask` on one device may be relied on, other than what follows from the above.
Results may differ from a plain program's by a relative error of at most 0.014.
The roundings to bfloat16 on the way count: a program that leaves them out, or rounds other values in their place, can miss the bound.
Values may be sent and summed in bfloat16 or wider, within the bound.
No kernel may reach another device: no remote copies, remote signals or barrier semaphores. Data moves between devices by JAX's collectives and lax.ppermute only.
A program may use at most 512 MiB of HBM per device.

v0:
```python
import jax
import jax.numpy as jnp
from jax import lax
from jax.sharding import PartitionSpec as P

QUERY_HEADS = 16
KEY_VALUE_HEADS = 8
HEAD_DIMENSION = 128


EPSILON = 1e-05
NEGATIVE = -1e30


def angles(positions, head_width):
    frequency = jnp.exp(
        jnp.arange(head_width // 2, dtype=jnp.float32) * (-2.0 / head_width) * jnp.log(10000.0)
    )
    phases = positions.astype(jnp.float32)[:, None] * frequency[None, :]
    return (jnp.cos(phases), jnp.sin(phases))


def rotate(values, cos_table, sine_table, direction):
    half_width = values.shape[-1] // 2
    lower_half = values[..., :half_width]
    upper_half = values[..., half_width:]
    return jnp.concatenate(
        [
            lower_half * cos_table - direction * upper_half * sine_table,
            upper_half * cos_table + direction * lower_half * sine_table,
        ],
        axis=-1,
    )


def scores_of(query_b, key_all, local_pos, all_pos):
    raw_scores = jnp.einsum("rkgd,lkd->kgrl", query_b, key_all, preferred_element_type=jnp.float32)
    allowed = all_pos[None, :] <= local_pos[:, None]
    return jnp.where(allowed[None, None], raw_scores * HEAD_DIMENSION ** (-0.5), NEGATIVE)


def on_device(
    inputs,
    skip_mask,
    block_order,
    norm1_gain,
    query_weight,
    key_weight,
    value_weight,
    w_out,
    norm2_gain,
    w_gate,
    w_up,
    w_down,
    out_grad,
):
    tensor_count = lax.axis_size("tensor")
    tensor_rank = lax.axis_index("tensor")
    seq_rank = lax.axis_index("seq")
    micro_count = inputs.shape[0]
    row_count = inputs.shape[2]
    model_width = inputs.shape[3]
    slice_width = model_width // tensor_count
    kv_local = key_weight.shape[1] // HEAD_DIMENSION
    heads_per_group = QUERY_HEADS // KEY_VALUE_HEADS
    block_rows = row_count // 2
    col_start = tensor_rank * slice_width
    gain_one = norm1_gain.astype(jnp.float32)
    gain_two = norm2_gain.astype(jnp.float32)
    gain_one_s = lax.dynamic_slice_in_dim(gain_one, col_start, slice_width)
    acc_gain_one = jnp.zeros((slice_width,), jnp.float32)
    acc_gain_two = jnp.zeros((slice_width,), jnp.float32)
    acc_query = jnp.zeros(query_weight.shape, jnp.float32)
    acc_key = jnp.zeros(key_weight.shape, jnp.float32)
    acc_value = jnp.zeros(value_weight.shape, jnp.float32)
    acc_out = jnp.zeros(w_out.shape, jnp.float32)
    acc_gate = jnp.zeros(w_gate.shape, jnp.float32)
    acc_up = jnp.zeros(w_up.shape, jnp.float32)
    acc_down = jnp.zeros(w_down.shape, jnp.float32)
    out_list = []
    grad_list = []
    for micro in range(micro_count):
        in_f = inputs[micro, 0].astype(jnp.float32)
        in_slice = lax.dynamic_slice_in_dim(in_f, col_start, slice_width, 1)
        grad_f = out_grad[micro, 0].astype(jnp.float32)
        active = (1 - skip_mask[micro, 0]).astype(jnp.float32)
        order_row = block_order[micro, 0]
        offsets = jnp.arange(block_rows, dtype=jnp.int32)
        all_pos = (order_row[:, None] * block_rows + offsets[None, :]).reshape(-1)
        my_blocks = lax.dynamic_slice_in_dim(order_row, 2 * seq_rank, 2)
        local_pos = (my_blocks[:, None] * block_rows + offsets[None, :]).reshape(-1)
        cos_table, sine_table = angles(local_pos, HEAD_DIMENSION)
        scale_one = lax.rsqrt(jnp.mean(in_f * in_f, axis=-1, keepdims=True) + EPSILON)
        first_normalized = (in_f * scale_one * gain_one).astype(jnp.bfloat16)
        query_unrotated = jnp.dot(
            first_normalized, query_weight, preferred_element_type=jnp.float32
        ).reshape(row_count, kv_local, heads_per_group, HEAD_DIMENSION)
        key_unrotated = jnp.dot(
            first_normalized, key_weight, preferred_element_type=jnp.float32
        ).reshape(row_count, kv_local, HEAD_DIMENSION)
        value_b = (
            jnp.dot(first_normalized, value_weight, preferred_element_type=jnp.float32)
            .astype(jnp.bfloat16)
            .reshape(row_count, kv_local, HEAD_DIMENSION)
        )
        query_b = rotate(
            query_unrotated, cos_table[:, None, None, :], sine_table[:, None, None, :], 1.0
        ).astype(jnp.bfloat16)
        key_b = rotate(key_unrotated, cos_table[:, None, :], sine_table[:, None, :], 1.0).astype(
            jnp.bfloat16
        )
        key_all, value_all = (
            lax.all_gather(key_b, "seq", axis=0, tiled=True),
            lax.all_gather(value_b, "seq", axis=0, tiled=True),
        )
        scores = scores_of(query_b, key_all, local_pos, all_pos)
        top_score = jnp.max(scores, axis=-1, keepdims=True)
        expd = jnp.exp(scores - top_score)
        totals = jnp.sum(expd, axis=-1, keepdims=True)
        attn_b = (expd / totals).astype(jnp.bfloat16)
        log_total = top_score + jnp.log(totals)
        attended = jnp.einsum(
            "kgrl,lkd->rkgd", attn_b, value_all, preferred_element_type=jnp.float32
        )
        attended_b = attended.reshape(row_count, -1).astype(jnp.bfloat16)
        mixed_part = jnp.dot(attended_b, w_out, preferred_element_type=jnp.float32)
        mixed_full = lax.psum(mixed_part, "tensor")
        hidden = in_f + active * mixed_full
        scale_two = lax.rsqrt(jnp.mean(hidden * hidden, axis=-1, keepdims=True) + EPSILON)
        normed_two = (hidden * scale_two * gain_two).astype(jnp.bfloat16)
        hidden_s = lax.dynamic_slice_in_dim(hidden, col_start, slice_width, 1)
        gate_rows = jnp.dot(normed_two, w_gate, preferred_element_type=jnp.float32)
        up_rows = jnp.dot(normed_two, w_up, preferred_element_type=jnp.float32)
        sigmoid_g = jax.nn.sigmoid(gate_rows)
        silu_g = gate_rows * sigmoid_g
        gated = (silu_g * up_rows).astype(jnp.bfloat16)
        branch_part = jnp.dot(gated, w_down, preferred_element_type=jnp.float32)
        branch_s = lax.psum_scatter(
            branch_part.astype(jnp.bfloat16), "tensor", scatter_dimension=1, tiled=True
        ).astype(jnp.float32)
        out_list.append((hidden_s + active * branch_s).astype(jnp.bfloat16))
        branch_grad = (active * grad_f).astype(jnp.bfloat16)
        acc_down = acc_down + jnp.einsum(
            "rf,rd->fd", gated, branch_grad, preferred_element_type=jnp.float32
        )
        d_gated = jnp.einsum("rd,fd->rf", branch_grad, w_down, preferred_element_type=jnp.float32)
        d_gate = (d_gated * up_rows * sigmoid_g * (1.0 + gate_rows * (1.0 - sigmoid_g))).astype(
            jnp.bfloat16
        )
        d_up = (d_gated * silu_g).astype(jnp.bfloat16)
        acc_gate = acc_gate + jnp.einsum(
            "rd,rf->df", normed_two, d_gate, preferred_element_type=jnp.float32
        )
        acc_up = acc_up + jnp.einsum(
            "rd,rf->df", normed_two, d_up, preferred_element_type=jnp.float32
        )
        norm_two_part = jnp.einsum(
            "rf,df->rd", d_gate, w_gate, preferred_element_type=jnp.float32
        ) + jnp.einsum("rf,df->rd", d_up, w_up, preferred_element_type=jnp.float32)
        d_norm = lax.psum(norm_two_part, "tensor")
        d_scaled = d_norm * gain_two
        inner_two = jnp.mean(d_scaled * hidden, axis=-1, keepdims=True)
        d_hidden = grad_f + scale_two * d_scaled - hidden * scale_two**3 * inner_two
        gain_terms = jnp.sum(d_norm * hidden * scale_two, axis=0)
        acc_gain_two = acc_gain_two + lax.dynamic_slice_in_dim(gain_terms, col_start, slice_width)
        d_hidden_s = lax.dynamic_slice_in_dim(d_hidden, col_start, slice_width, 1)
        d_mixed = (active * d_hidden).astype(jnp.bfloat16)
        acc_out = acc_out + jnp.einsum(
            "rk,rd->kd", attended_b, d_mixed, preferred_element_type=jnp.float32
        )
        d_attended = jnp.einsum("rd,kd->rk", d_mixed, w_out, preferred_element_type=jnp.float32)
        d_att_b = d_attended.astype(jnp.bfloat16).reshape(
            row_count, kv_local, heads_per_group, HEAD_DIMENSION
        )
        scores = scores_of(query_b, key_all, local_pos, all_pos)
        attn_weights = jnp.exp(scores - log_total)
        attn_again = attn_weights.astype(jnp.bfloat16)
        d_prob = jnp.einsum(
            "rkgd,lkd->kgrl", d_att_b, value_all, preferred_element_type=jnp.float32
        )
        row_inner = jnp.sum(attn_weights * d_prob, axis=-1, keepdims=True)
        d_score = (attn_weights * (d_prob - row_inner) * HEAD_DIMENSION ** (-0.5)).astype(
            jnp.bfloat16
        )
        d_query = jnp.einsum("kgrl,lkd->rkgd", d_score, key_all, preferred_element_type=jnp.float32)
        d_key_all = jnp.einsum(
            "kgrl,rkgd->lkd", d_score, query_b, preferred_element_type=jnp.float32
        )
        d_value_all = jnp.einsum(
            "kgrl,rkgd->lkd", attn_again, d_att_b, preferred_element_type=jnp.float32
        )
        d_key, d_value = (
            lax.psum_scatter(d_key_all, "seq", scatter_dimension=0, tiled=True),
            lax.psum_scatter(d_value_all, "seq", scatter_dimension=0, tiled=True),
        )
        d_query_b = (
            rotate(d_query, cos_table[:, None, None, :], sine_table[:, None, None, :], -1.0)
            .reshape(row_count, -1)
            .astype(jnp.bfloat16)
        )
        d_key_b = (
            rotate(d_key, cos_table[:, None, :], sine_table[:, None, :], -1.0)
            .reshape(row_count, -1)
            .astype(jnp.bfloat16)
        )
        d_value_b = d_value.reshape(row_count, -1).astype(jnp.bfloat16)
        acc_query = acc_query + jnp.einsum(
            "rd,rk->dk", first_normalized, d_query_b, preferred_element_type=jnp.float32
        )
        acc_key = acc_key + jnp.einsum(
            "rd,rk->dk", first_normalized, d_key_b, preferred_element_type=jnp.float32
        )
        acc_value = acc_value + jnp.einsum(
            "rd,rk->dk", first_normalized, d_value_b, preferred_element_type=jnp.float32
        )
        norm_one_part = jnp.einsum(
            "rk,dk->rd", d_query_b, query_weight, preferred_element_type=jnp.float32
        )
        norm_one_part = norm_one_part + jnp.einsum(
            "rk,dk->rd", d_key_b, key_weight, preferred_element_type=jnp.float32
        )
        norm_one_part = norm_one_part + jnp.einsum(
            "rk,dk->rd", d_value_b, value_weight, preferred_element_type=jnp.float32
        )
        d_norm_one = lax.psum_scatter(norm_one_part, "tensor", scatter_dimension=1, tiled=True)
        d_scaled_one = d_norm_one * gain_one_s
        inner_one = lax.psum(jnp.sum(d_scaled_one * in_slice, axis=-1), "tensor")
        d_input = (
            d_hidden_s
            + scale_one * d_scaled_one
            - in_slice * scale_one**3 * (inner_one / model_width)[:, None]
        )
        acc_gain_one = acc_gain_one + jnp.sum(d_norm_one * in_slice * scale_one, axis=0)
        grad_list.append(d_input)
    summed = lax.psum(
        (
            acc_gain_one,
            acc_query,
            acc_key,
            acc_value,
            acc_out,
            acc_gain_two,
            acc_gate,
            acc_up,
            acc_down,
        ),
        ("dp", "seq"),
    )
    output = jnp.stack(out_list)[:, None]
    input_grad = jnp.stack(grad_list)[:, None]
    return (
        output,
        input_grad,
        summed[0],
        summed[1],
        summed[2],
        summed[3],
        summed[4],
        summed[5],
        summed[6],
        summed[7],
        summed[8],
    )


def solution(mesh):
    return jax.shard_map(
        on_device,
        mesh=mesh,
        in_specs=(
            P(None, "dp", "seq", None),
            P(None, "dp"),
            P(None, "dp", None),
            P(),
            P(None, "tensor"),
            P(None, "tensor"),
            P(None, "tensor"),
            P("tensor", None),
            P(),
            P(None, "tensor"),
            P(None, "tensor"),
            P("tensor", None),
            P(None, "dp", "seq", None),
        ),
        out_specs=(
            P(None, "dp", "seq", "tensor"),
            P(None, "dp", "seq", "tensor"),
            P("tensor"),
            P(None, "tensor"),
            P(None, "tensor"),
            P(None, "tensor"),
            P("tensor", None),
            P("tensor"),
            P(None, "tensor"),
            P(None, "tensor"),
            P("tensor", None),
        ),
        check_vma=False,
    )
```

profile of v0, /device:TPU:0, one launch (start us, length us, event | category | flops | bytes accessed | tf_op | source)
XLA Modules:
  0.0 2157.4 jit_solution(14588341741385188119)
XLA Ops:
  37.3 16.8 all_gather.12
  54.1 14.7 all_gather.14
  70.8 14.3 all_gather.13
  85.2 14.4 all_gather.15
  111.9 59.3 %all-reduce.13.cloned.1.call-done = (f32[128,2048]{1,0:T(8,128)}, f32[128,2048]{1,0:T(8,128)}) async-done(((f32[128,2048]{1,0:T(8,128)}, f32[128,2048]{1,0:T(8,128)}), (f32[128,2048]{1,0:T(8,128)}, f32[128,2048]{1,0:T(8,128)})) %all-reduce.13.cloned.1.call-update) | async-done | bytes 2097168 | tf_op jit(solution)/shard_map/psum | solution.py:127
  191.9 10.7 multiply_convert_fusion.2
  208.4 10.9 multiply_convert_fusion
  224.4 9.1 convolution_add_fusion.12
  233.5 9.0 convolution_add_fusion.11
  242.6 63.2 %all-reduce.11.cloned.1.call-done = (f32[128,2048]{1,0:T(8,128)}, f32[128,2048]{1,0:T(8,128)}) async-done(((f32[128,2048]{1,0:T(8,128)}, f32[128,2048]{1,0:T(8,128)}), (f32[128,2048]{1,0:T(8,128)}, f32[128,2048]{1,0:T(8,128)})) %all-reduce.11.cloned.1.call-update) | async-done | bytes 2097168 | tf_op jit(solution)/shard_map/psum | solution.py:160
  327.1 12.8 fusion.137
  344.8 15.7 convolution_add_fusion.1
  360.6 9.9 fusion.136
  385.3 12.7 fusion.98
  398.1 19.5 convolution_add_fusion
  417.6 15.4 convolution_add_fusion.2
  476.7 8.1 convolution_add_fusion.3
  491.7 8.2 convolution_add_fusion.4
  520.5 35.7 %all-reduce = (f32[1024]{0:T(1024)}, f32[1024]{0:T(1024)}) all-reduce(f32[1024]{0:T(1024)S(1)} %add.364, f32[1024]{0:T(1024)S(1)} %dynamic-slice_add_fusion), channel_id=1, replica_groups=mesh['dp'=4,'seq'=4,'tensor'=2] {'dp','seq'}, use_global_device_ids=true, to_apply=%region_30.31 | all-reduce | flops 2048 | bytes 16384 | tf_op jit(solution)/shard_map/psum | solution.py:235
  559.4 1526.4 %all-reduce.9.cloned.1.call-done = (f32[2048,1024]{1,0:T(8,128)}, f32[2048,512]{1,0:T(8,128)}, f32[2048,512]{1,0:T(8,128)}, f32[1024,2048]{1,0:T(8,128)}, f32[20...) async-done(((f32[2048,1024]{1,0:T(8,128)}, f32[2048,512]{1,0:T(8,128)}, f32[2048,512]{1,0:T(8,128)}, f32[1024,2048]{1,0:T(8,128)}, ...) | async-done | bytes 94371856 | tf_op jit(solution)/shard_map/psum | solution.py:235
  2085.7 8.6 copy.99
  2105.6 18.6 copy.103
  2124.2 17.9 copy.104
  2142.2 8.2 copy.105
  (336 shorter events, 200.6 us)
Async XLA Ops:
  7.2 164.0 %all-reduce.13.cloned.1.call-start = ((), (), s32[]{:S(2)}) async-start(), calls=%async_computation.18 | async-start | bytes 4194304 | tf_op jit(solution)/shard_map/psum | solution.py:127
  37.2 47.9 %copy-start.67 = (f32[128,4,128]{0,2,1:T(8,128)S(1)}, f32[128,4,128]{0,2,1:T(8,128)}, u32[]{:S(2)}) copy-start(f32[128,4,128]{0,2,1:T(8,128)} %fusion.58) | copy-start | bytes 786436
  37.2 62.3 %copy-start.61 = (f32[128,4,2,128]{0,3,2,1:T(8,128)S(1)}, f32[128,4,2,128]{0,3,2,1:T(8,128)}, u32[]{:S(2)}) copy-start(f32[128,4,2,128]{0,3,2,1:T(8,128)} %fusion.63) | copy-start | bytes 1572868
  54.1 46.7 %copy-start.37 = (bf16[512,4,128]{0,2,1:T(8,128)(2,1)}, bf16[512,4,128]{0,2,1:T(8,128)(2,1)S(1)}, u32[]{:S(2)}) copy-start(bf16[512,4,128]{0,2,1:T(8,128)(2,1)S(1)} %all_gather.12) | copy-start | bytes 1572868
  54.1 45.6 %copy-start.60 = (f32[128,4,2,128]{0,3,2,1:T(8,128)S(1)}, f32[128,4,2,128]{0,3,2,1:T(8,128)}, u32[]{:S(2)}) copy-start(f32[128,4,2,128]{0,3,2,1:T(8,128)} %fusion.56) | copy-start | bytes 1572868
  68.8 37.2 %copy-start.35 = (bf16[512,4,128]{0,2,1:T(8,128)(2,1)}, bf16[512,4,128]{0,2,1:T(8,128)(2,1)S(1)}, u32[]{:S(2)}) copy-start(bf16[512,4,128]{0,2,1:T(8,128)(2,1)S(1)} %all_gather.14) | copy-start | bytes 1572868
  69.7 30.0 %copy-start.48 = (f32[128,64]{0,1:T(8,128)}, f32[128,64]{0,1:T(8,128)S(1)}, u32[]{:S(2)}) copy-start(f32[128,64]{0,1:T(8,128)S(1)} %get-tuple-element.102) | copy-start | bytes 98308
  69.7 30.0 %copy-start.50 = (f32[128,64]{0,1:T(8,128)}, f32[128,64]{0,1:T(8,128)S(1)}, u32[]{:S(2)}) copy-start(f32[128,64]{0,1:T(8,128)S(1)} %get-tuple-element.89) | copy-start | bytes 98308
  109.4 196.4 %all-reduce.11.cloned.1.call-start = ((), (), s32[]{:S(2)}) async-start(), calls=%async_computation.17 | async-start | bytes 4194304 | tf_op jit(solution)/shard_map/psum | solution.py:160
  242.5 221.7 %reduce-scatter.15.cloned.1.call-start = ((), (), s32[]{:S(2)}) async-start(), calls=%async_computation.11 | async-start | bytes 1310720 | tf_op jit(solution)/shard_map/reduce_scatter | solution.py:194
  318.0 147.1 %reduce-scatter.13.cloned.1.call-start = ((), (), s32[]{:S(2)}) async-start(), calls=%async_computation.10 | async-start | bytes 1310720 | tf_op jit(solution)/shard_map/reduce_scatter | solution.py:193
  327.0 157.7 %reduce-scatter.21.cloned.1.call-start = ((), (), s32[]{:S(2)}) async-start(), calls=%async_computation.14 | async-start | bytes 1310720 | tf_op jit(solution)/shard_map/reduce_scatter | solution.py:194
  344.8 141.0 %reduce-scatter.19.cloned.1.call-start = ((), (), s32[]{:S(2)}) async-start(), calls=%async_computation.13 | async-start | bytes 1310720 | tf_op jit(solution)/shard_map/reduce_scatter | solution.py:193
  377.9 131.7 %reduce-scatter.9.cloned.1.call-start = ((), (), s32[]{:S(2)}) async-start(), calls=%async_computation.8 | async-start | bytes 786432 | tf_op jit(solution)/shard_map/reduce_scatter | solution.py:138
  398.0 112.8 %reduce-scatter.11.cloned.1.call-start = ((), (), s32[]{:S(2)}) async-start(), calls=%async_computation.9 | async-start | bytes 786432 | tf_op jit(solution)/shard_map/reduce_scatter | solution.py:138
  440.2 72.8 %reduce-scatter.17.cloned.1.call-start = ((), (), s32[]{:S(2)}) async-start(), calls=%async_computation.12 | async-start | bytes 1572864 | tf_op jit(solution)/shard_map/reduce_scatter | solution.py:225
  470.9 42.9 %reduce-scatter.23.cloned.1.call-start = ((), (), s32[]{:S(2)}) async-start(), calls=%async_computation.15 | async-start | bytes 1572864 | tf_op jit(solution)/shard_map/reduce_scatter | solution.py:225
  491.4 1594.3 %all-reduce.9.cloned.1.call-start = ((), (), s32[]{:S(2)}) async-start(), calls=%async_computation.16 | async-start | bytes 188743680 | tf_op jit(solution)/shard_map/psum | solution.py:235
  510.8 45.5 %copy-start.17 = (f32[128,2048]{1,0:T(8,128)S(1)}, f32[128,2048]{1,0:T(8,128)}, u32[]{:S(2)}) copy-start(f32[128,2048]{1,0:T(8,128)} %copy-done.15) | copy-start | bytes 3145732
  510.8 45.5 %copy-start.78 = (f32[128]{0:T(128)S(1)}, f32[128]{0:T(128)}, u32[]{:S(2)}) copy-start(f32[128]{0:T(128)} %get-tuple-element.99) | copy-start | bytes 1540
  510.8 45.5 %copy-start.79 = (f32[128]{0:T(128)S(1)}, f32[128]{0:T(128)}, u32[]{:S(2)}) copy-start(f32[128]{0:T(128)} %get-tuple-element.115) | copy-start | bytes 1540
  2105.6 36.5 %slice-start.6 = ((s8[23068672]{0:T(1024)(128)(4,1)}), s8[4194304]{0:T(1024)(128)(4,1)S(1)}, s32[]{:S(2)}) async-start(s8[23068672]{0:T(1024)(128)(4,1)} %bitcast.359), calls=%async_computation.25 | async-start | bytes 8388608
  2105.6 36.5 %slice-start.7 = ((s8[23068672]{0:T(1024)(128)(4,1)}), s8[4194304]{0:T(1024)(128)(4,1)S(1)}, s32[]{:S(2)}) async-start(s8[23068672]{0:T(1024)(128)(4,1)} %bitcast.359), calls=%async_computation.26 | async-start | bytes 8388608
  2105.6 36.5 %slice-start.8 = ((s8[23068672]{0:T(1024)(128)(4,1)}), s8[4194304]{0:T(1024)(128)(4,1)S(1)}, s32[]{:S(2)}) async-start(s8[23068672]{0:T(1024)(128)(4,1)} %bitcast.359), calls=%async_computation.27 | async-start | bytes 8388608
  (82 other events, 536.5 us)
Sparse Core Ops, SparseCore 0:
  109.5 61.6 all-reduce.12
  242.6 63.0 all-reduce.10
  318.2 27.1 reduce-scatter.14
  347.6 25.7 reduce-scatter.12
  375.6 25.7 reduce-scatter.20
  403.6 25.8 reduce-scatter.18
  431.7 13.1 reduce-scatter.8
  447.8 14.5 reduce-scatter.10
  471.0 20.1 reduce-scatter.16
  493.4 20.3 reduce-scatter.22
  520.8 1564.9 all-reduce.8
where the time goes:
time: 2170 us; the launch traced here: 2160 us
  waiting for transfers between devices  1650 us (76%)
  matrix products  272 us (13%)
  blocking collectives  101 us (5%)
  local copies, waits for them, and re-layouts  85.2 us (4%)
  other arithmetic  31.2 us (1%)
    psum x1, waiting for transfers between devices, on_device(): lax.psum((acc_gain_one, acc_query, acc_key, acc_value, acc_out, acc_gain_...  1530 us
    unnamed x197, local copies, waits for them, and re-layouts  72.5 us
    psum x1, waiting for transfers between devices, on_device(): d_norm = lax.psum(norm_two_part, 'tensor')  63.2 us
    psum x1, waiting for transfers between devices, on_device(): mixed_full = lax.psum(mixed_part, 'tensor')  59.3 us
  transfers between devices with their start and end apart: 11, of which 4 were waited for; matrix products, arithmetic and copies ran while one was open for 9% of the time, Pallas kernels for 0%

commit v1 on v0

v1 whole, which is shorter than its diff:
```python
import jax
import jax.numpy as jnp
from jax import lax
from jax.sharding import PartitionSpec as P

HEAD_DIMENSION = 128
EPSILON = 1e-05
NEGATIVE = -1e30
BF = jnp.bfloat16
F32 = jnp.float32


def angles(positions, head_width):
    frequency = jnp.exp(
        jnp.arange(head_width // 2, dtype=F32) * (-2.0 / head_width) * jnp.log(10000.0)
    )
    phases = positions.astype(F32)[:, None] * frequency[None, :]
    return (jnp.cos(phases), jnp.sin(phases))


def rotate(values, cos_table, sine_table, direction):
    half_width = values.shape[-1] // 2
    lower_half = values[..., :half_width]
    upper_half = values[..., half_width:]
    return jnp.concatenate(
        [
            lower_half * cos_table - direction * upper_half * sine_table,
            upper_half * cos_table + direction * lower_half * sine_table,
        ],
        axis=-1,
    )


def dot(a, b):
    return jnp.dot(a, b, preferred_element_type=F32)


def dot_t(a, b):
    return lax.dot_general(a, b, (((1,), (1,)), ((), ())), preferred_element_type=F32)


def dot_rows(a, b):
    return lax.dot_general(a, b, (((0,), (0,)), ((), ())), preferred_element_type=F32)


def sum_tensor(part):
    sent = part.astype(BF)
    if lax.axis_size("tensor") == 2:
        other = lax.ppermute(sent, "tensor", [(0, 1), (1, 0)])
        return sent.astype(F32) + other.astype(F32)
    return lax.psum(sent.astype(F32), "tensor")


def half(values, index):
    width = values.shape[1] // 2
    return lax.dynamic_slice_in_dim(values, index * width, width, 1)


def spread(by_core, by_chip):
    count = lax.axis_size("dp")
    me = lax.axis_index("dp")
    blocks = []
    for mask in range(count):
        target = jnp.bitwise_xor(me, mask)
        block = jnp.concatenate(
            [half(v, target % 2) for v in by_core] + [half(v, target // 2) for v in by_chip], axis=1
        )
        if mask:
            block = lax.ppermute(block, "dp", [(i, i ^ mask) for i in range(count)])
        blocks.append(block)
    return jnp.concatenate(blocks, axis=0)


def finish(quarter, row_by_core):
    part = lax.psum_scatter(quarter.astype(BF), "seq", scatter_dimension=0, tiled=True)
    every = lax.all_gather(part, ("dp", "seq"), axis=0, tiled=False)
    seq = lax.axis_size("seq")
    every = every.reshape(2, 2, seq, part.shape[0], part.shape[1])
    return every, row_by_core


def assemble(every, row_by_core, start, stop):
    every = every[..., start:stop]
    order = (1, 2, 3, 0, 4) if row_by_core else (0, 2, 3, 1, 4)
    _, _, seq, rows, cols = every.shape
    return every.transpose(order).reshape(2 * seq * rows, 2 * cols).astype(F32)


def on_device(
    inputs,
    skip_mask,
    block_order,
    norm1_gain,
    query_weight,
    key_weight,
    value_weight,
    w_out,
    norm2_gain,
    w_gate,
    w_up,
    w_down,
    out_grad,
):
    tensor_count = lax.axis_size("tensor")
    tensor_rank = lax.axis_index("tensor")
    seq_rank = lax.axis_index("seq")
    micro, _, length, width = inputs.shape
    rows = micro * length
    slice_width = width // tensor_count
    kv = key_weight.shape[1] // HEAD_DIMENSION
    group = query_weight.shape[1] // key_weight.shape[1]
    block_rows = length // 2
    col_start = tensor_rank * slice_width

    def mine(values):
        return lax.dynamic_slice_in_dim(values, col_start, slice_width, values.ndim - 1)

    gain_one = norm1_gain.astype(F32)
    gain_two = norm2_gain.astype(F32)
    gain_one_s = mine(gain_one)

    in_f = inputs.reshape(rows, width).astype(F32)
    grad_f = out_grad.reshape(rows, width).astype(F32)
    active = jnp.repeat((1 - skip_mask[:, 0]).astype(F32), length)[:, None]
    offsets = jnp.arange(block_rows, dtype=jnp.int32)
    order = block_order[:, 0]
    all_pos = (order[:, :, None] * block_rows + offsets).reshape(micro, -1)
    my_blocks = lax.dynamic_slice_in_dim(order, 2 * seq_rank, 2, 1)
    local_pos = (my_blocks[:, :, None] * block_rows + offsets).reshape(micro, length)
    cos_table, sine_table = angles(local_pos.reshape(-1), HEAD_DIMENSION)
    cos_table, sine_table = cos_table[:, None, :], sine_table[:, None, :]
    allowed = all_pos[:, None, :] <= local_pos[:, :, None]

    scale_one = lax.rsqrt(jnp.mean(in_f * in_f, axis=-1, keepdims=True) + EPSILON)
    hn1 = (in_f * scale_one * gain_one).astype(BF)
    df = (active * grad_f).astype(BF)
    early = spread([hn1, df], [])

    q = rotate(dot(hn1, query_weight).reshape(rows, -1, HEAD_DIMENSION), cos_table, sine_table, 1.0)
    k = rotate(dot(hn1, key_weight).reshape(rows, -1, HEAD_DIMENSION), cos_table, sine_table, 1.0)
    v = dot(hn1, value_weight).astype(BF)
    q = q.astype(BF).reshape(micro, length, kv, group, HEAD_DIMENSION)
    kvb = jnp.concatenate([k.astype(BF).reshape(rows, -1), v], axis=1).reshape(micro, length, -1)
    kv_all = [lax.all_gather(kvb[m], "seq", axis=0, tiled=True) for m in range(micro)]
    k_all = [a[:, : kv * HEAD_DIMENSION].reshape(-1, kv, HEAD_DIMENSION) for a in kv_all]
    v_all = [a[:, kv * HEAD_DIMENSION :].reshape(-1, kv, HEAD_DIMENSION) for a in kv_all]

    dz = dot_t(df, w_down)

    probs = []
    mixed = []
    attended = []
    for m in range(micro):
        raw = jnp.einsum("rkgd,lkd->kgrl", q[m], k_all[m], preferred_element_type=F32)
        scores = jnp.where(allowed[m][None, None], raw * HEAD_DIMENSION ** (-0.5), NEGATIVE)
        top = jnp.max(scores, axis=-1, keepdims=True)
        expd = jnp.exp(scores - top)
        prob = expd / jnp.sum(expd, axis=-1, keepdims=True)
        probs.append(prob)
        o = jnp.einsum("kgrl,lkd->rkgd", prob.astype(BF), v_all[m], preferred_element_type=F32)
        o = o.reshape(length, -1).astype(BF)
        attended.append(o)
        mixed.append(sum_tensor(dot(o, w_out)))
    mixed = jnp.concatenate(mixed, axis=0)
    ob = jnp.concatenate(attended, axis=0)

    hidden = in_f + active * mixed
    scale_two = lax.rsqrt(jnp.mean(hidden * hidden, axis=-1, keepdims=True) + EPSILON)
    hn2 = (hidden * scale_two * gain_two).astype(BF)
    g = dot(hn2, w_gate)
    u = dot(hn2, w_up)
    sig = jax.nn.sigmoid(g)
    silu = g * sig
    z = (silu * u).astype(BF)
    dg = (dz * u * sig * (1.0 + g * (1.0 - sig))).astype(BF)
    du = (dz * silu).astype(BF)
    ffn_half = z.shape[1] // 2
    core_half = width // 2

    middle = spread([hn2], [z])
    late = spread([], [dg, du])
    down_q = dot_rows(middle[:, core_half:], early[:, core_half:])
    down_all = finish(down_q, False)
    gate_up_q = dot_rows(middle[:, :core_half], late)
    gate_up_all = finish(gate_up_q, True)

    dn2 = sum_tensor(dot_t(dg, w_gate) + dot_t(du, w_up))
    branch = lax.psum_scatter(
        dot(z, w_down).astype(BF), "tensor", scatter_dimension=1, tiled=True
    ).astype(F32)
    output = (mine(hidden) + active * branch).astype(BF)

    d_scaled = dn2 * gain_two
    inner_two = jnp.mean(d_scaled * hidden, axis=-1, keepdims=True)
    dh = grad_f + scale_two * d_scaled - hidden * scale_two**3 * inner_two
    gain_terms = mine(jnp.sum(dn2 * hidden * scale_two, axis=0))
    da = (active * dh).astype(BF)
    do = dot_t(da, w_out).astype(BF).reshape(micro, length, kv, group, HEAD_DIMENSION)
    out_act = spread([da], [ob])
    out_q = dot_rows(out_act[:, core_half:], out_act[:, :core_half])
    out_all = finish(out_q, False)

    dqs = []
    dkvs = []
    for m in range(micro):
        prob = probs[m]
        dp = jnp.einsum("rkgd,lkd->kgrl", do[m], v_all[m], preferred_element_type=F32)
        inner = jnp.sum(prob * dp, axis=-1, keepdims=True)
        ds = (prob * (dp - inner) * HEAD_DIMENSION ** (-0.5)).astype(BF)
        dqs.append(jnp.einsum("kgrl,lkd->rkgd", ds, k_all[m], preferred_element_type=F32))
        dk = jnp.einsum("kgrl,rkgd->lkd", ds, q[m], preferred_element_type=F32)
        dv = jnp.einsum("kgrl,rkgd->lkd", prob.astype(BF), do[m], preferred_element_type=F32)
        dkv = jnp.concatenate([dk.reshape(dk.shape[0], -1), dv.reshape(dv.shape[0], -1)], axis=1)
        dkvs.append(lax.psum_scatter(dkv.astype(BF), "seq", scatter_dimension=0, tiled=True))
    dq = jnp.stack(dqs).reshape(rows, -1, HEAD_DIMENSION)
    dkv = jnp.stack(dkvs).reshape(rows, -1).astype(F32)
    dk = dkv[:, : kv * HEAD_DIMENSION].reshape(rows, -1, HEAD_DIMENSION)
    dqb = rotate(dq, cos_table, sine_table, -1.0).reshape(rows, -1).astype(BF)
    dkb = rotate(dk, cos_table, sine_table, -1.0).reshape(rows, -1).astype(BF)
    dvb = dkv[:, kv * HEAD_DIMENSION :].astype(BF)

    qkv_act = spread([], [dqb, dkb, dvb])
    qkv_q = dot_rows(early[:, :core_half], qkv_act)
    qkv_all = finish(qkv_q, True)

    dn1 = dot_t(dqb, query_weight) + dot_t(dkb, key_weight) + dot_t(dvb, value_weight)
    dn1 = lax.psum_scatter(dn1, "tensor", scatter_dimension=1, tiled=True)
    d_scaled_one = dn1 * gain_one_s
    in_slice = mine(in_f)
    inner_one = lax.psum(jnp.sum(d_scaled_one * in_slice, axis=-1, keepdims=True), "tensor")
    input_grad = (
        mine(dh) + scale_one * d_scaled_one - in_slice * scale_one**3 * (inner_one / width)
    )
    gains = jnp.stack([jnp.sum(dn1 * in_slice * scale_one, axis=0), gain_terms])
    gains = lax.psum(gains, ("dp", "seq"))

    q_half = dqb.shape[1] // 2
    k_half = dkb.shape[1] // 2
    return (
        output.reshape(micro, 1, length, slice_width),
        input_grad.reshape(micro, 1, length, slice_width),
        gains[0],
        assemble(*qkv_all, 0, q_half),
        assemble(*qkv_all, q_half, q_half + k_half),
        assemble(*qkv_all, q_half + k_half, q_half + 2 * k_half),
        assemble(*out_all, 0, core_half),
        gains[1],
        assemble(*gate_up_all, 0, ffn_half),
        assemble(*gate_up_all, ffn_half, 2 * ffn_half),
        assemble(*down_all, 0, core_half),
    )


def solution(mesh):
    return jax.shard_map(
        on_device,
        mesh=mesh,
        in_specs=(
            P(None, "dp", "seq", None),
            P(None, "dp"),
            P(None, "dp", None),
            P(),
            P(None, "tensor"),
            P(None, "tensor"),
            P(None, "tensor"),
            P("tensor", None),
            P(),
            P(None, "tensor"),
            P(None, "tensor"),
            P("tensor", None),
            P(None, "dp", "seq", None),
        ),
        out_specs=(
            P(None, "dp", "seq", "tensor"),
            P(None, "dp", "seq", "tensor"),
            P("tensor"),
            P(None, "tensor"),
            P(None, "tensor"),
            P(None, "tensor"),
            P("tensor", None),
            P("tensor"),
            P(None, "tensor"),
            P(None, "tensor"),
            P("tensor", None),
        ),
        check_vma=False,
    )
```

time: 2170 us -> 1130 us (0.52)
  waiting for transfers between devices: 1650 us -> 531 us
  local copies, waits for them, and re-layouts: 85.2 us -> 284 us
  matrix products: 272 us -> 140 us
  other arithmetic: 31.2 us -> 99.1 us
  blocking collectives: 101 us -> 38.9 us
    psum x3 -> x0, waiting for transfers between devices: 1650 us -> none  [the longest x1 1530 us: on_device(): lax.psum((acc_gain_one, acc_query, acc_key, acc_value, acc_out, acc_gain_...]
    all_gather x0 -> x6, waiting for transfers between devices: none -> 204 us  [the longest x4 178 us: finish(): every = lax.all_gather(part, ('dp', 'seq'), axis=0, tiled=False)]
    ppermute x0 -> x18, waiting for transfers between devices: none -> 186 us  [the longest x15 153 us: spread(): block = lax.ppermute(block, 'dp', [(i, i ^ mask) for i in range(count)])]
    convert_element_type x0 -> x11, local copies, waits for them, and re-layouts: none -> 147 us  [the longest x7 144 us: assemble(): return every.transpose(order).reshape(2 * seq * rows, 2 * cols).astype(F32)]
    dot_general x54 -> x29, matrix products: 272 us -> 133 us  [the longest x7 36.8 us: dot_t(): lax.dot_general(a, b, (((1,), (1,)), ((), ())), preferred_element_type=F32)]
    reduce_scatter x8, waiting for transfers between devices: 0.85 us -> 138 us  [the longest x4 84.1 us: finish(): lax.psum_scatter(quarter.astype(BF), 'seq', scatter_dimension=0, tiled=True)]
    all_gather x4 -> x0, blocking collectives: 60.2 us -> none  [the longest x2 31.5 us: on_device(): lax.all_gather(value_b, 'seq', axis=0, tiled=True)]
    convert_element_type x12 -> x15, other arithmetic: 5.42 us -> 55.3 us  [the longest x5 43.5 us: assemble(): return every.transpose(order).reshape(2 * seq * rows, 2 * cols).astype(F32)]
  transfers between devices with their start and end apart: 11 -> 32, of which waited for: 4 -> 22; matrix products, arithmetic and copies ran while one was open for 9% -> 26% of each run, Pallas kernels for 0% -> 0%
where the time goes in v1:
time: 1130 us; the launch traced here: 1120 us
  waiting for transfers between devices  531 us (47%)
  local copies, waits for them, and re-layouts  284 us (25%)
  matrix products  140 us (12%)
  other arithmetic  99.1 us (9%)
  blocking collectives  38.9 us (3%)
  starting transfers between devices  16.3 us (1%)
  between operations  15.3 us (1%)
    all_gather x4, waiting for transfers between devices, finish(): every = lax.all_gather(part, ('dp', 'seq'), axis=0, tiled=False)  178 us
    ppermute x15, waiting for transfers between devices, spread(): block = lax.ppermute(block, 'dp', [(i, i ^ mask) for i in range(count)])  153 us
    convert_element_type x7, local copies, waits for them, and re-layouts, assemble(): return every.transpose(order).reshape(2 * seq * rows, 2 * cols).astype(F32)  144 us
    unnamed x183, local copies, waits for them, and re-layouts  90.6 us
    reduce_scatter x4, waiting for transfers between devices, finish(): lax.psum_scatter(quarter.astype(BF), 'seq', scatter_dimension=0, tiled=True)  84.1 us
    convert_element_type x5, other arithmetic, assemble(): return every.transpose(order).reshape(2 * seq * rows, 2 * cols).astype(F32)  43.5 us
    dot_general x7, matrix products, dot_t(): lax.dot_general(a, b, (((1,), (1,)), ((), ())), preferred_element_type=F32)  36.8 us
    psum x1, blocking collectives, on_device(): gains = lax.psum(gains, ('dp', 'seq'))  33.9 us
  transfers between devices with their start and end apart: 32, of which 22 were waited for; matrix products, arithmetic and copies ran while one was open for 26% of the time, Pallas kernels for 0%

profile of v1, /device:TPU:0, one launch (start us, length us, event | category | flops | bytes accessed | tf_op | source)
XLA Modules:
  0.0 1124.9 jit_solution(18064101623691094941)
XLA Ops:
  37.5 13.5 %all-gather.11.cloned.1.call-done = bf16[512,1024]{1,0:T(8,128)(2,1)} async-done(((bf16[128,1024]{1,0:T(8,128)(2,1)}), bf16[512,1024]{1,0:T(8,128)(2,1)}) %all-gather.11.cloned.1.call-update) | async-done | bytes 1048592 | tf_op jit(solution)/shard_map/all_gather | solution.py:144
  124.1 14.4 %multiply_convert_fusion = (bf16[256,2816]{1,0:T(8,128)(2,1)S(1)}, bf16[256,2816]{1,0:T(8,128)(2,1)S(1)}, bf16[256,2816]{1,0:T(8,128)(2,1)}) fusion(f32[256,2816]{1,0:T(8,128)} %fusion.166, f32[256,2816]{1,0:T(8,128)} %fusion.167, bf16[256,2048]{1,0:T(8,128)(2,1)S(1)} %get-tuple-element.141, bf16[2816,2048]{1,0:T(8,128)(2,1)} %param.24), kind=kOutput, calls=%fused_computation.29 | convolution fusion | flops 2963603456 | bytes 22675456 | tf_op jit(solution)/shard_map/dot_general | solution.py:39
  154.6 22.5 %collective-permute-done.2 = bf16[256,2048]{1,0:T(8,128)(2,1)} collective-permute-done((bf16[256,2048]{1,0:T(8,128)(2,1)S(1)}, bf16[256,2048]{1,0:T(8,128)(2,1)}, u32[]{:S(2)}, u32[]{:S(2)}) %collective-permute-start.2) | collective-permute-done | bytes 1048608 | tf_op jit(solution)/shard_map/ppermute | solution.py:49
  258.0 15.7 %collective-permute-done.11 = bf16[256,1536]{1,0:T(8,128)(2,1)} collective-permute-done((bf16[256,1536]{1,0:T(8,128)(2,1)}, bf16[256,1536]{1,0:T(8,128)(2,1)}, u32[]{:S(2)}, u32[]{:S(2)}) %collective-permute-start.11) | collective-permute-done | bytes 786464 | tf_op jit(solution)/shard_map/ppermute | solution.py:69
  330.5 27.6 %collective-permute-done.13 = bf16[256,2432]{1,0:T(8,128)(2,1)S(1)} collective-permute-done((bf16[256,2432]{1,0:T(8,128)(2,1)S(1)}, bf16[256,2432]{1,0:T(8,128)(2,1)S(1)}, u32[]{:S(2)}, u32[]{:S(2)}) %collective-permute-start.13) | collective-permute-done | bytes 1245216 | tf_op jit(solution)/shard_map/ppermute | solution.py:69
  358.1 25.4 %collective-permute-done.14 = bf16[256,2432]{1,0:T(8,128)(2,1)S(1)} collective-permute-done((bf16[256,2432]{1,0:T(8,128)(2,1)S(1)}, bf16[256,2432]{1,0:T(8,128)(2,1)S(1)}, u32[]{:S(2)}, u32[]{:S(2)}) %collective-permute-start.14) | collective-permute-done | bytes 1245216 | tf_op jit(solution)/shard_map/ppermute | solution.py:69
  398.3 31.8 %collective-permute-done.16 = bf16[256,2816]{1,0:T(8,128)(2,1)S(1)} collective-permute-done((bf16[256,2816]{1,0:T(8,128)(2,1)S(1)}, bf16[256,2816]{1,0:T(8,128)(2,1)S(1)}, u32[]{:S(2)}, u32[]{:S(2)}) %collective-permute-start.16) | collective-permute-done | bytes 1441824 | tf_op jit(solution)/shard_map/ppermute | solution.py:69
  430.1 29.1 %collective-permute-done.17 = bf16[256,2816]{1,0:T(8,128)(2,1)S(1)} collective-permute-done((bf16[256,2816]{1,0:T(8,128)(2,1)S(1)}, bf16[256,2816]{1,0:T(8,128)(2,1)S(1)}, u32[]{:S(2)}, u32[]{:S(2)}) %collective-permute-start.17) | collective-permute-done | bytes 1441824 | tf_op jit(solution)/shard_map/ppermute | solution.py:69
  490.8 84.0 %reduce-scatter.21.cloned.1.call-done = bf16[256,2816]{1,0:T(8,128)(2,1)} async-done(((bf16[1024,2816]{1,0:T(8,128)(2,1)}), bf16[256,2816]{1,0:T(8,128)(2,1)}) %reduce-scatter.21.cloned.1.call-update) | async-done | bytes 1441808 | tf_op jit(solution)/shard_map/reduce_scatter | solution.py:75
  576.5 22.0 %reduce-scatter.13.cloned.1.call-done = bf16[256,1024]{1,0:T(8,128)(2,1)} async-done(((bf16[256,2048]{1,0:T(8,128)(2,1)}), bf16[256,1024]{1,0:T(8,128)(2,1)}) %reduce-scatter.13.cloned.1.call-update) | async-done | bytes 524304 | tf_op jit(solution)/shard_map/reduce_scatter | solution.py:188
  600.9 32.2 %reduce-scatter.15.cloned.1.call-done = f32[256,1024]{1,0:T(8,128)} async-done(((f32[256,2048]{1,0:T(8,128)}), f32[256,1024]{1,0:T(8,128)}) %reduce-scatter.15.cloned.1.call-update) | async-done | bytes 1048592 | tf_op jit(solution)/shard_map/reduce_scatter | solution.py:227
  639.7 33.9 %psum.15 = f32[2,1024]{1,0:T(2,128)S(1)} all-reduce(f32[2,1024]{1,0:T(2,128)S(1)} %pad_maximum_fusion.44), channel_id=1, replica_groups=mesh['dp'=4,'seq'=4,'tensor'=2] {'dp','seq'}, use_global_device_ids=true, to_apply=%region_17.18 | all-reduce | flops 2048 | bytes 16384 | tf_op jit(solution)/shard_map/psum | solution.py:235
  705.7 56.5 %all-gather.15.cloned.1.call-done = bf16[4096,1024]{1,0:T(8,128)(2,1)} async-done(((bf16[256,1024]{1,0:T(8,128)(2,1)}), bf16[4096,1024]{1,0:T(8,128)(2,1)}) %all-gather.15.cloned.1.call-update) | async-done | bytes 8388624 | tf_op jit(solution)/shard_map/all_gather | solution.py:76
  765.6 12.8 %copy.175 = f32[2,4,256,2,512]{4,3,2,1,0:T(2,128)S(1)} copy(f32[2,4,256,2,512]{4,2,1,0,3:T(8,128)S(1)} %convert_bitcast_fusion.4) | data formatting | bytes 16777216 | tf_op jit(solution)/shard_map/convert_element_type | solution.py:86
  796.4 60.8 %all-gather.21.cloned.1.call-done = bf16[5632,1024]{1,0:T(8,128)(2,1)} async-done(((bf16[352,1024]{1,0:T(8,128)(2,1)}), bf16[5632,1024]{1,0:T(8,128)(2,1)}) %all-gather.21.cloned.1.call-update) | async-done | bytes 11534352 | tf_op jit(solution)/shard_map/all_gather | solution.py:76
  857.2 13.4 %convert_bitcast_fusion = f32[2,4,352,2,1024]{4,2,1,3,0:T(8,128)} fusion(bf16[2,2,4,352,1024]{4,3,2,1,0:T(8,128)(2,1)} %bitcast.280), kind=kLoop, calls=%fused_computation.4 | loop fusion | flops 5767168 | bytes 34603008 | tf_op jit(solution)/shard_map/convert_element_type | solution.py:86
  870.5 38.8 %copy.182 = f32[2,4,352,2,1024]{4,3,2,1,0:T(2,128)} copy(f32[2,4,352,2,1024]{4,2,1,3,0:T(8,128)} %convert_bitcast_fusion) | data formatting | bytes 46137344 | tf_op jit(solution)/shard_map/convert_element_type | solution.py:86
  909.4 21.6 %copy.238 = f32[352,8,2,1024]{3,1,2,0:T(8,128)} copy(f32[352,8,2,1024]{3,2,1,0:T(2,128)} %bitcast.268) | data formatting | bytes 46137344
  931.0 51.0 %all-gather.19.cloned.1.call-done = bf16[4096,2816]{1,0:T(8,128)(2,1)} async-done(((bf16[256,2816]{1,0:T(8,128)(2,1)}), bf16[4096,2816]{1,0:T(8,128)(2,1)}) %all-gather.19.cloned.1.call-update) | async-done | bytes 23068688 | tf_op jit(solution)/shard_map/all_gather | solution.py:76
  982.0 22.5 %convert_bitcast_fusion.1 = (f32[2,4,256,2,1408]{4,2,1,0,3:T(8,128)}, f32[2,4,256,2,1408]{4,2,1,0,3:T(8,128)}) fusion(bf16[2,2,4,256,2816]{4,3,2,1,0:T(8,128)(2,1)} %bitcast.274), kind=kLoop, calls=%fused_computation.5 | loop fusion | flops 11534336 | bytes 69206016 | tf_op jit(solution)/shard_map/convert_element_type | solution.py:86
  1004.6 38.7 %copy.180 = f32[2,4,256,2,1408]{4,3,2,1,0:T(2,128)} copy(f32[2,4,256,2,1408]{4,2,1,0,3:T(8,128)} %get-tuple-element.64) | data formatting | bytes 46137344 | tf_op jit(solution)/shard_map/convert_element_type | solution.py:86
  1043.3 18.0 %copy.236 = f32[256,8,2,1408]{3,1,2,0:T(8,128)} copy(f32[256,8,2,1408]{3,2,1,0:T(2,128)} %bitcast.269) | data formatting | bytes 46137344
  1061.3 38.7 %copy.181 = f32[2,4,256,2,1408]{4,3,2,1,0:T(2,128)} copy(f32[2,4,256,2,1408]{4,2,1,0,3:T(8,128)} %get-tuple-element.63) | data formatting | bytes 46137344 | tf_op jit(solution)/shard_map/convert_element_type | solution.py:86
  1100.0 18.1 %copy.237 = f32[256,8,2,1408]{3,1,2,0:T(8,128)} copy(f32[256,8,2,1408]{3,2,1,0:T(2,128)} %bitcast.270) | data formatting | bytes 46137344
  (391 shorter events, 366.4 us)
Async XLA Ops:
  7.2 43.9 %all-gather.11.cloned.1.call-start = ((), (), s32[]{:S(2)}) async-start(), calls=%async_computation.8 | async-start | bytes 1310720 | tf_op jit(solution)/shard_map/all_gather | solution.py:144
  20.3 60.4 %all-gather.13.cloned.1.call-start = ((), (), s32[]{:S(2)}) async-start(), calls=%async_computation.9 | async-start | bytes 1310720 | tf_op jit(solution)/shard_map/all_gather | solution.py:144
  21.0 256.6 %reduce-scatter.25.cloned.1.call-start = ((), (), s32[]{:S(2)}) async-start(), calls=%async_computation.20 | async-start | bytes 1310720 | tf_op jit(solution)/shard_map/reduce_scatter | solution.py:214
  66.6 31.3 %collective-permute-start = (bf16[128,2048]{1,0:T(8,128)(2,1)}, bf16[128,2048]{1,0:T(8,128)(2,1)}, u32[]{:S(2)}, u32[]{:S(2)}) collective-permute-start(bf16[128,2048]{1,0:T(8,128)(2,1)} %convolution_convert_fusion.3), channel_id=1, source_target_pairs={{0,1},{1,0},{2,3},{3,2},{4,5},{5,4},{6,7},{7,6},{8,9},{9,8},{10,11... | collective-permute-start | bytes 1572872 | tf_op jit(solution)/shard_map/ppermute | solution.py:49
  203.4 74.2 %reduce-scatter.27.cloned.1.call-start = ((), (), s32[]{:S(2)}) async-start(), calls=%async_computation.21 | async-start | bytes 1310720 | tf_op jit(solution)/shard_map/reduce_scatter | solution.py:214
  213.3 80.8 %collective-permute-start.3 = (bf16[256,2048]{1,0:T(8,128)(2,1)}, bf16[256,2048]{1,0:T(8,128)(2,1)}, u32[]{:S(2)}, u32[]{:S(2)}) collective-permute-start(bf16[256,2048]{1,0:T(8,128)(2,1)} %pad_maximum_fusion.29), channel_id=1, source_target_pairs={{0,8},{8,0},{16,24},{24,16},{1,9},{9,1},{17,25},{25,17},{2,10},{10... | collective-permute-start | bytes 3145736 | tf_op jit(solution)/shard_map/ppermute | solution.py:69
  214.5 79.6 %collective-permute-start.4 = (bf16[256,2048]{1,0:T(8,128)(2,1)}, bf16[256,2048]{1,0:T(8,128)(2,1)}, u32[]{:S(2)}, u32[]{:S(2)}) collective-permute-start(bf16[256,2048]{1,0:T(8,128)(2,1)} %pad_maximum_fusion.30), channel_id=1, source_target_pairs={{0,16},{8,24},{16,0},{24,8},{1,17},{9,25},{17,1},{25,9},{2,18},{10... | collective-permute-start | bytes 3145736 | tf_op jit(solution)/shard_map/ppermute | solution.py:69
  216.9 40.7 %collective-permute-start.10 = (bf16[256,1536]{1,0:T(8,128)(2,1)}, bf16[256,1536]{1,0:T(8,128)(2,1)}, u32[]{:S(2)}, u32[]{:S(2)}) collective-permute-start(bf16[256,1536]{1,0:T(8,128)(2,1)} %pad_maximum_fusion.33), channel_id=1, source_target_pairs={{0,16},{8,24},{16,0},{24,8},{1,17},{9,25},{17,1},{25,9},{2,18},{10... | collective-permute-start | bytes 2359304 | tf_op jit(solution)/shard_map/ppermute | solution.py:69
  230.3 258.4 %reduce-scatter.19.cloned.1.call-start = ((), (), s32[]{:S(2)}) async-start(), calls=%async_computation.13 | async-start | bytes 1310720 | tf_op jit(solution)/shard_map/reduce_scatter | solution.py:75
  232.5 41.1 %collective-permute-start.11 = (bf16[256,1536]{1,0:T(8,128)(2,1)}, bf16[256,1536]{1,0:T(8,128)(2,1)}, u32[]{:S(2)}, u32[]{:S(2)}) collective-permute-start(bf16[256,1536]{1,0:T(8,128)(2,1)} %pad_maximum_fusion.34), channel_id=1, source_target_pairs={{0,24},{8,16},{16,8},{24,0},{1,25},{9,17},{17,9},{25,1},{2,26},{10... | collective-permute-start | bytes 2359304 | tf_op jit(solution)/shard_map/ppermute | solution.py:69
  234.4 39.2 %collective-permute-start.9 = (bf16[256,1536]{1,0:T(8,128)(2,1)}, bf16[256,1536]{1,0:T(8,128)(2,1)}, u32[]{:S(2)}, u32[]{:S(2)}) collective-permute-start(bf16[256,1536]{1,0:T(8,128)(2,1)} %pad_maximum_fusion.32), channel_id=1, source_target_pairs={{0,8},{8,0},{16,24},{24,16},{1,9},{9,1},{17,25},{25,17},{2,10},{10... | collective-permute-start | bytes 2359304 | tf_op jit(solution)/shard_map/ppermute | solution.py:69
  257.6 38.5 %collective-permute-start.5 = (bf16[256,2048]{1,0:T(8,128)(2,1)}, bf16[256,2048]{1,0:T(8,128)(2,1)}, u32[]{:S(2)}, u32[]{:S(2)}) collective-permute-start(bf16[256,2048]{1,0:T(8,128)(2,1)} %pad_maximum_fusion.31), channel_id=1, source_target_pairs={{0,24},{8,16},{16,8},{24,0},{1,25},{9,17},{17,9},{25,1},{2,26},{10... | collective-permute-start | bytes 3145736 | tf_op jit(solution)/shard_map/ppermute | solution.py:69
  277.5 211.9 %reduce-scatter.17.cloned.1.call-start = ((), (), s32[]{:S(2)}) async-start(), calls=%async_computation.12 | async-start | bytes 2621440 | tf_op jit(solution)/shard_map/reduce_scatter | solution.py:75
  324.3 165.7 %reduce-scatter.23.cloned.1.call-start = ((), (), s32[]{:S(2)}) async-start(), calls=%async_computation.15 | async-start | bytes 3604480 | tf_op jit(solution)/shard_map/reduce_scatter | solution.py:75
  329.5 54.1 %collective-permute-start.14 = (bf16[256,2432]{1,0:T(8,128)(2,1)S(1)}, bf16[256,2432]{1,0:T(8,128)(2,1)S(1)}, u32[]{:S(2)}, u32[]{:S(2)}) collective-permute-start(bf16[256,2432]{1,0:T(8,128)(2,1)S(1)} %pad_maximum_fusion.25), channel_id=1, source_target_pairs={{0,24},{8,16},{16,8},{24,0},{1,25},{9,17},{17,9},{25,1},{2,26},{10... | collective-permute-start | bytes 3735560 | tf_op jit(solution)/shard_map/ppermute | solution.py:69
  391.2 183.7 %reduce-scatter.21.cloned.1.call-start = ((), (), s32[]{:S(2)}) async-start(), calls=%async_computation.14 | async-start | bytes 7208960 | tf_op jit(solution)/shard_map/reduce_scatter | solution.py:75
  395.6 34.5 %collective-permute-start.16 = (bf16[256,2816]{1,0:T(8,128)(2,1)S(1)}, bf16[256,2816]{1,0:T(8,128)(2,1)S(1)}, u32[]{:S(2)}, u32[]{:S(2)}) collective-permute-start(bf16[256,2816]{1,0:T(8,128)(2,1)S(1)} %pad_maximum_fusion.21), channel_id=1, source_target_pairs={{0,16},{8,24},{16,0},{24,8},{1,17},{9,25},{17,1},{25,9},{2,18},{10... | collective-permute-start | bytes 4325384 | tf_op jit(solution)/shard_map/ppermute | solution.py:69
  397.2 62.0 %collective-permute-start.17 = (bf16[256,2816]{1,0:T(8,128)(2,1)S(1)}, bf16[256,2816]{1,0:T(8,128)(2,1)S(1)}, u32[]{:S(2)}, u32[]{:S(2)}) collective-permute-start(bf16[256,2816]{1,0:T(8,128)(2,1)S(1)} %pad_maximum_fusion.22), channel_id=1, source_target_pairs={{0,24},{8,16},{16,8},{24,0},{1,25},{9,17},{17,9},{25,1},{2,26},{10... | collective-permute-start | bytes 4325384 | tf_op jit(solution)/shard_map/ppermute | solution.py:69
  471.9 126.6 %reduce-scatter.13.cloned.1.call-start = ((), (), s32[]{:S(2)}) async-start(), calls=%async_computation.10 | async-start | bytes 1572864 | tf_op jit(solution)/shard_map/reduce_scatter | solution.py:188
  481.7 151.4 %reduce-scatter.15.cloned.1.call-start = ((), (), s32[]{:S(2)}) async-start(), calls=%async_computation.11 | async-start | bytes 3145728 | tf_op jit(solution)/shard_map/reduce_scatter | solution.py:227
  488.7 197.4 %all-gather.17.cloned.1.call-start = ((), (), s32[]{:S(2)}) async-start(), calls=%async_computation.17 | async-start | bytes 4456448 | tf_op jit(solution)/shard_map/all_gather | solution.py:76
  489.4 272.8 %all-gather.15.cloned.1.call-start = ((), (), s32[]{:S(2)}) async-start(), calls=%async_computation.16 | async-start | bytes 8912896 | tf_op jit(solution)/shard_map/all_gather | solution.py:76
  490.0 367.2 %all-gather.21.cloned.1.call-start = ((), (), s32[]{:S(2)}) async-start(), calls=%async_computation.19 | async-start | bytes 12255232 | tf_op jit(solution)/shard_map/all_gather | solution.py:76
  490.7 491.3 %all-gather.19.cloned.1.call-start = ((), (), s32[]{:S(2)}) async-start(), calls=%async_computation.18 | async-start | bytes 24510464 | tf_op jit(solution)/shard_map/all_gather | solution.py:76
  (95 other events, 1477.2 us)
Sparse Core Ops, SparseCore 0:
  20.4 30.6 all-gather.10
  53.2 27.4 all-gather.12
  203.6 27.2 reduce-scatter.24
  233.1 25.7 reduce-scatter.26
  277.7 27.8 reduce-scatter.18
  324.4 43.9 reduce-scatter.16
  391.3 56.4 reduce-scatter.22
  472.0 102.7 reduce-scatter.20
  577.6 20.8 reduce-scatter.12
  601.3 31.8 reduce-scatter.14
  635.3 50.7 all-gather.16
  688.2 74.0 all-gather.14
  764.6 92.5 all-gather.20
  858.6 123.4 all-gather.18

commit v2 on v1

v2 whole, which is shorter than its diff:
```python
import functools

import jax
import jax.numpy as jnp
from jax import lax
from jax.experimental import pallas as pl
from jax.experimental.pallas import tpu as pltpu
from jax.sharding import PartitionSpec as P

HEAD_DIMENSION = 128
EPSILON = 1e-05
NEGATIVE = -1e30
BF = jnp.bfloat16
F32 = jnp.float32
ACROSS = [(0, 2), (2, 0), (1, 3), (3, 1)]
CORES = [(0, 1), (1, 0), (2, 3), (3, 2)]
PAIRS = [(0, 1), (1, 0), (2, 3), (3, 2)]
MIDDLE = [(1, 2), (2, 1)]
QKV_CHUNKS = 2


def dot(a, b):
    return jnp.dot(a, b, preferred_element_type=F32)


def dot_t(a, b):
    return lax.dot_general(a, b, (((1,), (1,)), ((), ())), preferred_element_type=F32)


def dot_rows(a, b):
    out = lax.dot_general(a, b, (((0,), (0,)), ((), ())), preferred_element_type=F32)
    return out.astype(BF)


def swap_tensor(sent):
    if lax.axis_size("tensor") == 2:
        return lax.ppermute(sent, "tensor", [(0, 1), (1, 0)]).astype(F32)
    return lax.psum(sent.astype(F32), "tensor") - sent.astype(F32)


def half(values, index):
    width = values.shape[1] // 2
    return lax.dynamic_slice_in_dim(values, index * width, width, 1)


def to_core(sent):
    return lax.ppermute(sent, "dp", CORES)


def to_chip(sent):
    return lax.ppermute(sent, "dp", ACROSS)


def fits(rows, widths):
    return rows % 16 == 0 and all(w % 128 == 0 for w in widths)


def tables(positions):
    half_width = HEAD_DIMENSION // 2
    frequency = jnp.exp(
        jnp.arange(half_width, dtype=F32) * (-2.0 / HEAD_DIMENSION) * jnp.log(10000.0)
    )
    phases = positions.astype(F32)[:, None] * frequency[None, :]
    cos, sin = jnp.cos(phases), jnp.sin(phases)
    return jnp.concatenate([cos, cos], axis=1), jnp.concatenate([-sin, sin], axis=1)


def turn(values, cos, sin):
    return values * cos + pltpu.roll(values, HEAD_DIMENSION // 2, 1) * sin


def key_value_kernel(x_ref, key_ref, value_ref, cos_ref, sin_ref, out_ref):
    x = x_ref[...]
    keys = turn(dot(x, key_ref[...]), cos_ref[...], sin_ref[...])
    out_ref[:, :HEAD_DIMENSION] = keys.astype(BF)
    out_ref[:, HEAD_DIMENSION:] = dot(x, value_ref[...]).astype(BF)


def keys_and_values(x, key_weight, value_weight, cos, sin):
    rows, width = x.shape
    heads = key_weight.shape[1] // HEAD_DIMENSION
    whole = lambda step: (0, 0)
    column = lambda step: (0, step)
    return pl.pallas_call(
        key_value_kernel,
        grid=(heads,),
        in_specs=[
            pl.BlockSpec((rows, width), whole),
            pl.BlockSpec((width, HEAD_DIMENSION), column),
            pl.BlockSpec((width, HEAD_DIMENSION), column),
            pl.BlockSpec((rows, HEAD_DIMENSION), whole),
            pl.BlockSpec((rows, HEAD_DIMENSION), whole),
        ],
        out_specs=pl.BlockSpec((rows, 2 * HEAD_DIMENSION), column),
        out_shape=jax.ShapeDtypeStruct((rows, 2 * heads * HEAD_DIMENSION), BF),
        name="keys_and_values",
    )(x, key_weight, value_weight, cos, sin)


def query_kernel(x_ref, weight_ref, cos_ref, sin_ref, out_ref):
    raw = dot(x_ref[...], weight_ref[...])
    for start in range(0, raw.shape[1], HEAD_DIMENSION):
        head = raw[:, start : start + HEAD_DIMENSION]
        turned = turn(head, cos_ref[...], sin_ref[...])
        out_ref[:, start : start + HEAD_DIMENSION] = turned.astype(BF)


def queries(x, weight, cos, sin):
    rows, width = x.shape
    block = 2 * HEAD_DIMENSION
    whole = lambda step: (0, 0)
    column = lambda step: (0, step)
    return pl.pallas_call(
        query_kernel,
        grid=(weight.shape[1] // block,),
        in_specs=[
            pl.BlockSpec((rows, width), whole),
            pl.BlockSpec((width, block), column),
            pl.BlockSpec((rows, HEAD_DIMENSION), whole),
            pl.BlockSpec((rows, HEAD_DIMENSION), whole),
        ],
        out_specs=pl.BlockSpec((rows, block), column),
        out_shape=jax.ShapeDtypeStruct((rows, weight.shape[1]), BF),
        cost_estimate=pl.CostEstimate(
            flops=2 * rows * width * weight.shape[1],
            bytes_accessed=2 * width * weight.shape[1] + 2 * rows * width,
            transcendentals=0,
        ),
        name="queries",
    )(x, weight, cos, sin)


def probabilities(query, keys, query_pos, key_pos):
    scores = dot_t(query, keys) * HEAD_DIMENSION ** (-0.5)
    scores = jnp.where(key_pos <= query_pos, scores, NEGATIVE)
    expd = jnp.exp(scores - jnp.max(scores, axis=-1, keepdims=True))
    return expd / jnp.sum(expd, axis=-1, keepdims=True)


def attend_kernel(q_ref, kv_ref, query_pos_ref, key_pos_ref, out_ref):
    keys = kv_ref[:, :HEAD_DIMENSION]
    values = kv_ref[:, HEAD_DIMENSION:]
    for start in range(0, q_ref.shape[1], HEAD_DIMENSION):
        head = slice(start, start + HEAD_DIMENSION)
        prob = probabilities(q_ref[:, head], keys, query_pos_ref[...], key_pos_ref[...])
        out_ref[:, head] = dot(prob.astype(BF), values).astype(BF)


def attend_back_kernel(
    q_ref, kv_ref, query_pos_ref, key_pos_ref, do_ref, cos_ref, sin_ref, dq_ref, dkv_ref
):
    keys = kv_ref[:, :HEAD_DIMENSION]
    values = kv_ref[:, HEAD_DIMENSION:]
    dk = dv = None
    for start in range(0, q_ref.shape[1], HEAD_DIMENSION):
        head = slice(start, start + HEAD_DIMENSION)
        query = q_ref[:, head]
        do = do_ref[:, head]
        prob = probabilities(query, keys, query_pos_ref[...], key_pos_ref[...])
        dp = dot_t(do, values)
        inner = jnp.sum(prob * dp, axis=-1, keepdims=True)
        ds = (prob * (dp - inner) * HEAD_DIMENSION ** (-0.5)).astype(BF)
        dq = dot(ds, keys)
        dq_ref[:, head] = turn(dq, cos_ref[...], -sin_ref[...]).astype(BF)
        part_k = lax.dot_general(ds, query, (((0,), (0,)), ((), ())), preferred_element_type=F32)
        part_v = lax.dot_general(
            prob.astype(BF), do, (((0,), (0,)), ((), ())), preferred_element_type=F32
        )
        dk = part_k if dk is None else dk + part_k
        dv = part_v if dv is None else dv + part_v
    dkv_ref[:, :HEAD_DIMENSION] = dk.astype(BF)
    dkv_ref[:, HEAD_DIMENSION:] = dv.astype(BF)


def attention(m, length, q, kv_all, query_pos, key_pos, do=None, cos=None, sin=None):
    total = kv_all.shape[0]
    heads = kv_all.shape[1] // (2 * HEAD_DIMENSION)
    block = q.shape[1] // heads
    in_rows = lambda h: (m, h)
    column = lambda h: (0, h)
    in_specs = [
        pl.BlockSpec((length, block), in_rows),
        pl.BlockSpec((total, 2 * HEAD_DIMENSION), column),
        pl.BlockSpec((length, 1), lambda h: (m, 0)),
        pl.BlockSpec((None, 1, total), lambda h: (m, 0, 0)),
    ]
    operands = [q, kv_all, query_pos, key_pos]
    out_specs = pl.BlockSpec((length, block), column)
    out_shape = jax.ShapeDtypeStruct((length, q.shape[1]), BF)
    kernel = attend_kernel
    if do is not None:
        kernel = attend_back_kernel
        in_specs += [pl.BlockSpec((length, block), in_rows)]
        in_specs += [pl.BlockSpec((length, HEAD_DIMENSION), lambda h: (m, 0))] * 2
        operands += [do, cos, sin]
        out_specs = [out_specs, pl.BlockSpec((total, 2 * HEAD_DIMENSION), column)]
        out_shape = [out_shape, jax.ShapeDtypeStruct(kv_all.shape, BF)]
    return pl.pallas_call(
        kernel,
        grid=(heads,),
        in_specs=in_specs,
        out_specs=out_specs,
        out_shape=out_shape,
        cost_estimate=pl.CostEstimate(
            flops=(4 if do is None else 10) * length * total * q.shape[1],
            bytes_accessed=8 * kv_all.size,
            transcendentals=length * total * q.shape[1] // HEAD_DIMENSION,
        ),
        name="attend" if do is None else "attend_back",
    )(*operands)


def turn_back_kernel(dkv_ref, cos_ref, sin_ref, dk_ref, dv_ref):
    dk = dkv_ref[:, :HEAD_DIMENSION].astype(F32)
    dk_ref[...] = turn(dk, cos_ref[...], -sin_ref[...]).astype(BF)
    dv_ref[...] = dkv_ref[:, HEAD_DIMENSION:]


def turn_back(dkv, cos, sin):
    rows, both = dkv.shape
    column = lambda h: (0, h)
    return pl.pallas_call(
        turn_back_kernel,
        grid=(both // (2 * HEAD_DIMENSION),),
        in_specs=[pl.BlockSpec((rows, 2 * HEAD_DIMENSION), column)]
        + [pl.BlockSpec((rows, HEAD_DIMENSION), lambda h: (0, 0))] * 2,
        out_specs=[pl.BlockSpec((rows, HEAD_DIMENSION), column)] * 2,
        out_shape=[jax.ShapeDtypeStruct((rows, both // 2), BF)] * 2,
        name="turn_back",
    )(dkv, cos, sin)


def place_kernel(index_ref, *refs, widths, split):
    outs = refs[len(refs) - len(widths) :]
    step = pl.program_id(0)
    for number in range(4):

        @pl.when(step // split == number)
        def _(source=refs[number]):
            start = 0
            for width, out in zip(widths, outs):
                out[...] = source[:, start : start + width].astype(F32)
                start += width


def place(previous, pieces, row, quarter_rows, widths, row_by_core):
    rows, cols = pieces[0].shape
    me = lax.axis_index("dp")
    if not fits(rows, widths):
        outs = []
        start = 0
        for number, width in enumerate(widths):
            buffer = jnp.zeros((2 * quarter_rows, 2 * width), F32)
            if previous is not None:
                buffer = previous[number]
            for piece, mask in zip(pieces, (0, 2, 1, 3)):
                other = jnp.bitwise_xor(me, mask)
                chip, core = other // 2, other % 2
                first, second = (core, chip) if row_by_core else (chip, core)
                at = (first * quarter_rows + row, second * width)
                source = piece[:, start : start + width].astype(F32)
                buffer = lax.dynamic_update_slice(buffer, source, at)
            outs.append(buffer)
            start += width
        return outs
    split = 2 if rows % 32 == 0 else 1
    part = rows // split

    def out_index(step, index_ref):
        piece = step // split
        chip = jnp.where(piece % 2 == 0, index_ref[0], 1 - index_ref[0])
        core = jnp.where(piece < 2, index_ref[1], 1 - index_ref[1])
        first, second = (core, chip) if row_by_core else (chip, core)
        return first * (quarter_rows // part) + row // part + step % split, second

    def in_index(number):
        return lambda step, _: (jnp.clip(step - number * split, 0, split - 1), 0)

    in_specs = [pl.BlockSpec((part, cols), in_index(n)) for n in range(4)]
    operands = [jnp.stack([me // 2, me % 2]).astype(jnp.int32)] + list(pieces)
    aliases = {}
    if previous is not None:
        for number, buffer in enumerate(previous):
            in_specs.append(pl.BlockSpec(memory_space=pl.ANY))
            aliases[len(operands)] = number
            operands.append(buffer)
    return pl.pallas_call(
        functools.partial(place_kernel, widths=widths, split=split),
        grid_spec=pltpu.PrefetchScalarGridSpec(
            num_scalar_prefetch=1,
            grid=(4 * split,),
            in_specs=in_specs,
            out_specs=[pl.BlockSpec((part, width), out_index) for width in widths],
        ),
        out_shape=[jax.ShapeDtypeStruct((2 * quarter_rows, 2 * w), F32) for w in widths],
        input_output_aliases=aliases,
        cost_estimate=pl.CostEstimate(
            flops=0, bytes_accessed=24 * rows * cols, transcendentals=0
        ),
        name="place",
    )(*operands)


def share_kernel(every_ref, *out_refs, pieces):
    out_refs = list(out_refs)
    for start, stop, widths in pieces:
        at = 0
        for width in widths:
            out_refs.pop(0)[...] = every_ref[start:stop, at : at + width].astype(F32)
            at += width


def write_whole(every, pieces):
    count, rows, cols = every.shape
    seq = lax.axis_size("seq")
    aligned = all(size % 16 == 0 and all(w % 128 == 0 for w in ws) for size, ws, _ in pieces)
    if not aligned:
        results = []
        start = 0
        for size, widths, row_by_core in pieces:
            at = 0
            for width in widths:
                piece = every[:, start : start + size, at : at + width]
                piece = piece.reshape(2, 2, seq, size, width)
                piece = piece.transpose((1, 2, 3, 0, 4) if row_by_core else (0, 2, 3, 1, 4))
                results.append(piece.reshape(2 * seq * size, 2 * width).astype(F32))
                at += width
            start += size
        return results
    spans = []
    out_specs = []
    out_shape = []
    start = 0
    for size, widths, row_by_core in pieces:
        spans.append((start, start + size, widths))

        def index(device, row_by_core=row_by_core):
            chip, core, rank = device // (2 * seq), (device // seq) % 2, device % seq
            row, column = (core, chip) if row_by_core else (chip, core)
            return row * seq + rank, column

        for width in widths:
            out_specs.append(pl.BlockSpec((size, width), index))
            out_shape.append(jax.ShapeDtypeStruct((2 * seq * size, 2 * width), F32))
        start += size
    return pl.pallas_call(
        functools.partial(share_kernel, pieces=tuple(spans)),
        grid=(count,),
        in_specs=[pl.BlockSpec((None, rows, cols), lambda device: (device, 0, 0))],
        out_specs=out_specs,
        out_shape=out_shape,
        cost_estimate=pl.CostEstimate(
            flops=0, bytes_accessed=6 * every.size, transcendentals=0
        ),
        name="write_whole",
    )(every)


class Chain:
    def __init__(self):
        rank = lax.axis_index("seq")
        self.is_middle = (rank == 1) | (rank == 2)
        self.stages = {n: [] for n in ("in", "middle", "out", "across", "core")}
        self.outs = {}
        self.time = 0
        self.fresh = []
        self.writes = []
        self.arrived = []

    def add(self, name, quarter, count, widths, row_by_core):
        size = quarter.shape[0] // count
        for i in range(count):
            info = (name, i * size, quarter.shape[0], widths, row_by_core)
            self.stages["in"].append((0, quarter[i * size : (i + 1) * size], info))

    def busy(self):
        return bool(self.writes) or any(self.stages.values())

    def put(self, stage, value, info):
        self.stages[stage].append((self.time + 1, value, info))

    def tick(self, *values):
        self.time += 1
        taken = {}
        for name, queue in self.stages.items():
            if queue and queue[0][0] <= self.time:
                taken[name] = queue.pop(0)
        names = list(taken)
        done = self.arrived
        writes, self.writes = self.writes, []
        fresh, self.fresh = self.fresh, []
        flat = [taken[n][1] for n in names]
        flat += [a for pieces, _ in writes for a in pieces]
        flat += [b for n in fresh for b in self.outs[n]]
        tied = list(lax.optimization_barrier(tuple(flat) + tuple(done) + tuple(values)))
        values = tied[len(tied) - len(values) :] if values else []
        now = {n: tied.pop(0) for n in names}
        writes = [([tied.pop(0) for _ in pieces], info) for pieces, info in writes]
        for n in fresh:
            self.outs[n] = [tied.pop(0) for _ in self.outs[n]]
        meta = {n: taken[n][2] for n in names}
        arrived = []
        if "middle" in now:
            other = lax.ppermute(now["middle"], "seq", MIDDLE)
            arrived.append(other)
            self.put("out", now["middle"] + other, meta["middle"])
        if "in" in now:
            other = lax.ppermute(now["in"], "seq", [(0, 1), (3, 2)])
            arrived.append(other)
            self.put("middle", now["in"] + other, meta["in"])
        if "out" in now:
            other = lax.ppermute(now["out"], "seq", [(1, 0), (2, 3)])
            arrived.append(other)
            self.put("across", jnp.where(self.is_middle, now["out"], other), meta["out"])
        if "across" in now:
            other = to_chip(now["across"])
            beside = to_core(now["across"])
            arrived += [other, beside]
            self.put("core", other, (now["across"], beside, meta["across"]))
        if "core" in now:
            other = to_core(now["core"])
            arrived.append(other)
            own, beside, info = meta["core"]
            self.writes.append(([own, now["core"], beside, other], info))
        for pieces, (name, row, quarter_rows, widths, row_by_core) in writes:
            self.fresh.append(name)
            self.outs[name] = place(
                self.outs.get(name), pieces, row, quarter_rows, widths, row_by_core
            )
        self.arrived = arrived
        return values if len(values) != 1 else values[0]


def tie(*values):
    return lax.optimization_barrier(values)


def on_device(
    inputs,
    skip_mask,
    block_order,
    norm1_gain,
    query_weight,
    key_weight,
    value_weight,
    w_out,
    norm2_gain,
    w_gate,
    w_up,
    w_down,
    out_grad,
):
    tensor_count = lax.axis_size("tensor")
    tensor_rank = lax.axis_index("tensor")
    seq_rank = lax.axis_index("seq")
    me = lax.axis_index("dp")
    chip, core = me // 2, me % 2
    micro, _, length, width = inputs.shape
    rows = micro * length
    slice_width = width // tensor_count
    core_half = width // 2
    block_rows = length // 2
    col_start = tensor_rank * slice_width

    def mine(values):
        return lax.dynamic_slice_in_dim(values, col_start, slice_width, values.ndim - 1)

    def scatter_tensor(part):
        if tensor_count != 2:
            sent = part.astype(BF)
            got = lax.psum_scatter(sent, "tensor", scatter_dimension=1, tiled=True)
            return got.astype(F32)
        sent = lax.dynamic_slice_in_dim(
            part, (1 - tensor_rank) * slice_width, slice_width, 1
        ).astype(BF)
        return mine(part) + swap_tensor(sent)

    gain_one = norm1_gain.astype(F32)
    gain_two = norm2_gain.astype(F32)
    gain_one_s = mine(gain_one)

    x_in = inputs.reshape(rows, width)
    g_in = out_grad.reshape(rows, width)
    in_f = x_in.astype(F32)
    active = jnp.repeat((1 - skip_mask[:, 0]).astype(F32), length)[:, None]
    offsets = jnp.arange(block_rows, dtype=jnp.int32)
    order = block_order[:, 0]
    key_pos = (order[:, :, None] * block_rows + offsets).reshape(micro, 1, -1)
    my_blocks = lax.dynamic_slice_in_dim(order, 2 * seq_rank, 2, 1)
    query_pos = (my_blocks[:, :, None] * block_rows + offsets).reshape(rows, 1)
    cos, sin = tables(query_pos[:, 0])

    scale_one = lax.rsqrt(jnp.mean(in_f * in_f, axis=-1, keepdims=True) + EPSILON)
    hn1 = (in_f * scale_one * gain_one).astype(BF)
    df = (active * g_in.astype(F32)).astype(BF)
    kvb = keys_and_values(hn1, key_weight, value_weight, cos, sin)
    kvb, hn1, df = tie(kvb, hn1, df)

    kv_all = lax.all_gather(kvb.reshape(micro, length, -1), "seq", axis=1, tiled=True)
    hn1_other = to_chip(hn1)
    df_other = to_chip(df)
    q = queries(hn1, query_weight, cos, sin)
    dz = dot_t(df, w_down)
    kv_all, hn1_other, df_other, q, dz, hn1, df = tie(kv_all, hn1_other, df_other, q, dz, hn1, df)

    def by_core(own, other):
        both = jnp.concatenate([own, other], axis=0)
        return jnp.concatenate([half(both, core), to_core(half(both, 1 - core))], axis=0)

    def by_chip(own, other):
        both = jnp.concatenate([own, other], axis=0)
        return jnp.concatenate([both, to_core(both)], axis=0)

    attended = []
    parts = []
    others = []
    for m in range(micro):
        o = attention(m, length, q, kv_all[m], query_pos, key_pos)
        attended.append(o)
        part = dot(o, w_out).astype(BF)
        parts.append(part)
        others.append(swap_tensor(part))
    hn1_core = by_core(hn1, hn1_other)
    df_core = by_core(df, df_other)
    mixed = jnp.concatenate([a.astype(F32) + b for a, b in zip(parts, others)], axis=0)
    ob = jnp.concatenate(attended, axis=0)
    hidden = in_f + active * mixed
    scale_two = lax.rsqrt(jnp.mean(hidden * hidden, axis=-1, keepdims=True) + EPSILON)
    hn2 = (hidden * scale_two * gain_two).astype(BF)
    hn2, hidden, scale_two, hn1_core, df_core = tie(hn2, hidden, scale_two, hn1_core, df_core)

    hn2_other = to_chip(hn2)
    g = dot(hn2, w_gate)
    u = dot(hn2, w_up)
    sig = jax.nn.sigmoid(g)
    silu = g * sig
    z = (silu * u).astype(BF)
    dg = (dz * u * sig * (1.0 + g * (1.0 - sig))).astype(BF)
    du = (dz * silu).astype(BF)
    z, dg, du = tie(z, dg, du)

    z_other = to_chip(half(z, 1 - chip))
    dn2_part = (dot_t(dg, w_gate) + dot_t(du, w_up)).astype(BF)
    z_other, dn2_part, hn2_other, dg, du = tie(z_other, dn2_part, hn2_other, dg, du)

    dn2_other = swap_tensor(dn2_part)
    z_chip = by_chip(half(z, chip), z_other)
    hn2_core = by_core(hn2, hn2_other)
    dgu_other = to_chip(jnp.concatenate([half(dg, 1 - chip), half(du, 1 - chip)], axis=1))
    down_quarter = dot_rows(z_chip, df_core)
    down_quarter, hn2_core = tie(down_quarter, hn2_core)
    down_part = lax.psum_scatter(down_quarter, "seq", scatter_dimension=0, tiled=True)
    dn2_other, dgu_other = tie(dn2_other, dgu_other)

    dgu = jnp.concatenate([half(dg, chip), half(du, chip)], axis=1)
    dgu_chip = by_chip(dgu, dgu_other)
    gate_up_quarter = dot_rows(hn2_core, dgu_chip)
    gate_up_part = lax.psum_scatter(gate_up_quarter, "seq", scatter_dimension=0, tiled=True)

    dn2 = dn2_part.astype(F32) + dn2_other
    grad_f = g_in.astype(F32)
    d_scaled = dn2 * gain_two
    inner_two = jnp.mean(d_scaled * hidden, axis=-1, keepdims=True)
    dh = grad_f + scale_two * d_scaled - hidden * scale_two**3 * inner_two
    gain_terms = mine(jnp.sum(dn2 * hidden * scale_two, axis=0))
    da = (active * dh).astype(BF)
    do = dot_t(da, w_out).astype(BF)
    da_other = to_chip(da)
    o_other = to_chip(half(ob, 1 - chip))
    dqs = []
    dkvs = []
    for m in range(micro):
        dq, dkv = attention(m, length, q, kv_all[m], query_pos, key_pos, do, cos, sin)
        dqs.append(dq)
        dkvs.append(dkv)
    dqb = jnp.concatenate(dqs, axis=0)
    dkvs, dqb, da_other, o_other, down_part = tie(
        jnp.stack(dkvs), dqb, da_other, o_other, down_part
    )

    dkv = lax.psum_scatter(dkvs, "seq", scatter_dimension=1, tiled=True)
    dq_part = dot_t(dqb, query_weight)
    branch = scatter_tensor(dot(z, w_down))
    da_core = by_core(da, da_other)
    o_chip = by_chip(half(ob, chip), o_other)
    out_quarter = dot_rows(o_chip, da_core)
    output = (mine(hidden) + active * branch).astype(BF)
    dkv, dq_part, out_quarter, output = tie(dkv, dq_part, out_quarter, output)

    chain = Chain()
    chain.add("out", out_quarter, 1, (core_half,), False)
    dkb, dvb = turn_back(dkv.reshape(rows, -1), cos, sin)
    grads = (dqb, dkb, dvb)
    widths = tuple(a.shape[1] // 2 for a in grads)
    qkv_other = to_chip(jnp.concatenate([half(a, 1 - chip) for a in grads], axis=1))
    qkv_own = jnp.concatenate([half(a, chip) for a in grads], axis=1)
    dn1 = dq_part + dot_t(dkb, key_weight) + dot_t(dvb, value_weight)
    qkv_other, qkv_own, dn1 = chain.tick(qkv_other, qkv_own, dn1)
    qkv_chip = by_chip(qkv_own, qkv_other)
    qkv_quarter = dot_rows(hn1_core, qkv_chip)
    dn1 = scatter_tensor(dn1)
    qkv_quarter, dn1 = chain.tick(qkv_quarter, dn1)
    chain.add("qkv", qkv_quarter, QKV_CHUNKS, widths, True)

    d_scaled_one = dn1 * gain_one_s
    in_slice = mine(in_f)
    inner_own = jnp.sum(d_scaled_one * in_slice, axis=-1)
    gains = jnp.stack([jnp.sum(dn1 * in_slice * scale_one, axis=0), gain_terms])
    inner_own, gains, d_scaled_one = chain.tick(inner_own, gains, d_scaled_one)
    inner_one = (inner_own + swap_tensor(inner_own))[:, None]
    input_grad = (
        mine(dh) + scale_one * d_scaled_one - in_slice * scale_one**3 * (inner_one / width)
    )
    gains = gains + to_chip(gains)
    gains, input_grad = chain.tick(gains, input_grad)
    gains = gains + to_core(gains)
    gains = chain.tick(gains)
    gains = gains + lax.ppermute(gains, "seq", PAIRS)
    gains = chain.tick(gains)
    gains = gains + lax.ppermute(gains, "seq", [(0, 2), (2, 0), (1, 3), (3, 1)])
    gains = chain.tick(gains)
    while chain.busy():
        chain.tick()

    gate_up = lax.all_gather(gate_up_part, ("dp", "seq"), axis=0, tiled=False)
    half_ff = z.shape[1] // 2
    gate, up = write_whole(gate_up, [(gate_up_part.shape[0], (half_ff, half_ff), True)])
    down_part, _ = tie(down_part, gate_up_part)
    every = lax.all_gather(down_part, ("dp", "seq"), axis=0, tiled=False)
    (down,) = write_whole(every, [(down_part.shape[0], (core_half,), False)])

    return (
        output.reshape(micro, 1, length, slice_width),
        input_grad.reshape(micro, 1, length, slice_width),
        gains[0],
        *chain.outs["qkv"],
        chain.outs["out"][0],
        gains[1],
        gate,
        up,
        down,
    )


def solution(mesh):
    return jax.shard_map(
        on_device,
        mesh=mesh,
        in_specs=(
            P(None, "dp", "seq", None),
            P(None, "dp"),
            P(None, "dp", None),
            P(),
            P(None, "tensor"),
            P(None, "tensor"),
            P(None, "tensor"),
            P("tensor", None),
            P(),
            P(None, "tensor"),
            P(None, "tensor"),
            P("tensor", None),
            P(None, "dp", "seq", None),
        ),
        out_specs=(
            P(None, "dp", "seq", "tensor"),
            P(None, "dp", "seq", "tensor"),
            P("tensor"),
            P(None, "tensor"),
            P(None, "tensor"),
            P(None, "tensor"),
            P("tensor", None),
            P("tensor"),
            P(None, "tensor"),
            P(None, "tensor"),
            P("tensor", None),
        ),
        check_vma=False,
    )
```

time: 1130 us -> 767 us (0.68)
  local copies, waits for them, and re-layouts: 284 us -> 22.8 us
  waiting for transfers between devices: 531 us -> 376 us
  Pallas kernels: 0 us -> 105 us
  starting transfers between devices: 16.3 us -> 103 us
  matrix products: 140 us -> 84.8 us
  other arithmetic: 99.1 us -> 51.3 us
  blocking collectives: 38.9 us -> 0 us
    all_gather x6 -> x3, waiting for transfers between devices: 204 us -> 0.01 us  [the longest x1 0.01 us: on_device(): lax.all_gather(kvb.reshape(micro, length, -1), 'seq', axis=1, tiled=True)]
    convert_element_type x11 -> x3, local copies, waits for them, and re-layouts: 147 us -> 1.18 us  [the longest x2 1.1 us: scatter_tensor(): sent = lax.dynamic_slice_in_dim(part, (1 - tensor_rank) * slice_width, sl...]
    pallas_call x0 -> x12, Pallas kernels: none -> 105 us  [the longest x2 39.8 us: write_whole(): pl.pallas_call(functools.partial(share_kernel, pieces=tuple(spans)), grid...]
    ppermute x18 -> x44, waiting for transfers between devices: 186 us -> 286 us  [the longest x12 89.7 us: to_chip(): return lax.ppermute(sent, 'dp', ACROSS)]
    ppermute x18 -> x44, starting transfers between devices: 15.1 us -> 102 us  [the longest x3 59.5 us: tick(): other = lax.ppermute(now['in'], 'seq', [(0, 1), (3, 2)])]
    unnamed x183 -> x97, local copies, waits for them, and re-layouts: 90.6 us -> 4.93 us
    reduce_scatter x8 -> x3, waiting for transfers between devices: 138 us -> 89.2 us  [the longest x1 75.6 us: on_device(): lax.psum_scatter(gate_up_quarter, 'seq', scatter_dimension=0, tiled=True)]
    convert_element_type x9 -> x4, other arithmetic: 45.8 us -> 4.78 us  [the longest x1 1.63 us: on_device(): du = (dz * silu).astype(BF)]
  transfers between devices with their start and end apart: 32 -> 50, of which waited for: 22 -> 23; matrix products, arithmetic and copies ran while one was open for 26% -> 18% of each run, Pallas kernels for 0% -> 9%
where the time goes in v2:
time: 767 us; the launch traced here: 758 us
  waiting for transfers between devices  376 us (49%)
  Pallas kernels  105 us (14%)
  starting transfers between devices  103 us (13%)
  matrix products  84.8 us (11%)
  other arithmetic  51.3 us (7%)
  local copies, waits for them, and re-layouts  22.8 us (3%)
  between operations  15.6 us (2%)
    ppermute x12, waiting for transfers between devices, to_chip(): return lax.ppermute(sent, 'dp', ACROSS)  89.7 us
    ppermute x3, waiting for transfers between devices, tick(): other = lax.ppermute(now['in'], 'seq', [(0, 1), (3, 2)])  76.5 us
    reduce_scatter x1, waiting for transfers between devices, on_device(): lax.psum_scatter(gate_up_quarter, 'seq', scatter_dimension=0, tiled=True)  75.6 us
    ppermute x3, starting transfers between devices, tick(): other = lax.ppermute(now['in'], 'seq', [(0, 1), (3, 2)])  59.5 us
    ppermute x6, waiting for transfers between devices, swap_tensor(): return lax.ppermute(sent, 'tensor', [(0, 1), (1, 0)]).astype(F32)  55.7 us
    dot_general x7, matrix products, dot_t(): lax.dot_general(a, b, (((1,), (1,)), ((), ())), preferred_element_type=F32)  41.8 us
    pallas_call x2, Pallas kernels, write_whole(): pl.pallas_call(functools.partial(share_kernel, pieces=tuple(spans)), grid...  39.8 us
    ppermute x1, waiting for transfers between devices, on_device(): gains = gains + lax.ppermute(gains, 'seq', PAIRS)  33.6 us
  transfers between devices with their start and end apart: 50, of which 23 were waited for; matrix products, arithmetic and copies ran while one was open for 18% of the time, Pallas kernels for 9%

profile of v2, /device:TPU:0, one launch (start us, length us, event | category | flops | bytes accessed | tf_op | source)
XLA Modules:
  0.0 758.1 jit_solution(12064326125767532496)
XLA Ops:
  29.9 9.3 %fusion.56 = f32[256,2816]{1,0:T(8,128)} fusion(bf16[256,2048]{1,0:T(8,128)(2,1)S(1)} %get-tuple-element.113, bf16[2816,2048]{1,0:T(8,128)(2,1)} %param.24), kind=kOutput, calls=%fused_computation.150 | convolution fusion | flops 2952790016 | bytes 15466496 | tf_op jit(solution)/shard_map/dot_general | solution.py:27
  47.1 21.6 %collective-permute-done.1 = bf16[256,2048]{1,0:T(8,128)(2,1)} collective-permute-done((bf16[256,2048]{1,0:T(8,128)(2,1)S(1)}, bf16[256,2048]{1,0:T(8,128)(2,1)}, u32[]{:S(2)}, u32[]{:S(2)}) %collective-permute-start.1) | collective-permute-done | bytes 1048608 | tf_op jit(solution)/shard_map/ppermute | solution.py:51
  96.0 8.8 %collective-permute-done.2 = bf16[128,2048]{1,0:T(8,128)(2,1)S(1)} collective-permute-done((bf16[128,2048]{1,0:T(8,128)(2,1)S(1)}, bf16[128,2048]{1,0:T(8,128)(2,1)S(1)}, u32[]{:S(2)}, u32[]{:S(2)}) %collective-permute-start.2) | collective-permute-done | bytes 524320 | tf_op jit(solution)/shard_map/ppermute | solution.py:37
  122.1 8.8 %fusion.59 = f32[256,2048]{1,0:T(8,128)} fusion(bf16[256,2816]{1,0:T(8,128)(2,1)S(1)} %get-tuple-element.122, bf16[2048,2816]{1,0:T(8,128)(2,1)} %param.22), kind=kOutput, calls=%fused_computation.153 | convolution fusion | flops 2952790016 | bytes 15073280 | tf_op jit(solution)/shard_map/dot_general | solution.py:27
  130.8 13.2 %fusion.17 = bf16[256,2048]{1,0:T(8,128)(2,1)} fusion(f32[256,2048]{1,0:T(8,128)} %fusion.59, bf16[256,2816]{1,0:T(8,128)(2,1)S(1)} %get-tuple-element.123, bf16[2048,2816]{1,0:T(8,128)(2,1)} %param.23), kind=kOutput, calls=%fused_computation.26 | convolution fusion | flops 2953838592 | bytes 16121856 | tf_op jit(solution)/shard_map/dot_general | solution.py:27
  163.8 24.0 %collective-permute-done.8 = bf16[256,2048]{1,0:T(8,128)(2,1)S(1)} collective-permute-done((bf16[256,2048]{1,0:T(8,128)(2,1)}, bf16[256,2048]{1,0:T(8,128)(2,1)S(1)}, u32[]{:S(2)}, u32[]{:S(2)}) %collective-permute-start.8) | collective-permute-done | bytes 1048608 | tf_op jit(solution)/shard_map/ppermute | solution.py:37
  196.4 13.7 %fusion.8 = bf16[1024,2816]{1,0:T(8,128)(2,1)} fusion(bf16[1024,1024]{1,0:T(8,128)(2,1)S(1)} %copy-done.22, bf16[512,2816]{1,0:T(8,128)(2,1)S(1)} %collective-permute-done.43, bf16[256,2816]{1,0:T(8,128)(2,1)} %collective-permute-done.9, bf16[256,1408]{1,0:T(8,128)(2,1)S(1)} %copy-done.16, bf16[256,1408]{1,0:T(8,128)(2,1)S(1)} %copy-done.17), kind=kOutput, calls=%fused_computation.8 | convolution fusion | flops 5931532288 | bytes 13631488 | tf_op jit(solution)/shard_map/dot_general | solution.py:31
  247.2 75.6 %reduce-scatter.8.cloned.1.call-done = bf16[256,2816]{1,0:T(8,128)(2,1)} async-done(((bf16[1024,2816]{1,0:T(8,128)(2,1)}), bf16[256,2816]{1,0:T(8,128)(2,1)}) %reduce-scatter.8.cloned.1.call-update) | async-done | bytes 1441808 | tf_op jit(solution)/shard_map/reduce_scatter | solution.py:558
  335.5 9.5 %collective-permute-done.16 = bf16[256,1024]{1,0:T(8,128)(2,1)} collective-permute-done((bf16[256,1024]{1,0:T(8,128)(2,1)}, bf16[256,1024]{1,0:T(8,128)(2,1)}, u32[]{:S(2)}, u32[]{:S(2)}) %collective-permute-start.16) | collective-permute-done | bytes 524320 | tf_op jit(solution)/shard_map/ppermute | solution.py:37
  356.4 13.5 %reduce-scatter.6.cloned.1.call-done = bf16[2,128,1024]{2,1,0:T(8,128)(2,1)} async-done(((bf16[2,512,1024]{2,1,0:T(8,128)(2,1)}), bf16[2,128,1024]{2,1,0:T(8,128)(2,1)}) %reduce-scatter.6.cloned.1.call-update) | async-done | bytes 524304 | tf_op jit(solution)/shard_map/reduce_scatter | solution.py:581
  381.6 16.2 %collective-permute-done.17 = bf16[256,1024]{1,0:T(8,128)(2,1)S(1)} collective-permute-done((bf16[256,1024]{1,0:T(8,128)(2,1)S(1)}, bf16[256,1024]{1,0:T(8,128)(2,1)S(1)}, u32[]{:S(2)}, u32[]{:S(2)}) %collective-permute-start.17) | collective-permute-done | bytes 524320 | tf_op jit(solution)/shard_map/ppermute | solution.py:51
  401.1 12.8 %collective-permute-done.20 = bf16[256,1024]{1,0:T(8,128)(2,1)S(1)} collective-permute-done((bf16[256,1024]{1,0:T(8,128)(2,1)S(1)}, bf16[256,1024]{1,0:T(8,128)(2,1)S(1)}, u32[]{:S(2)}, u32[]{:S(2)}) %collective-permute-start.20) | collective-permute-done | bytes 524320 | tf_op jit(solution)/shard_map/ppermute | solution.py:37
  414.1 23.1 %collective-permute-done.18 = bf16[512,1024]{1,0:T(8,128)(2,1)S(1)} collective-permute-done((bf16[512,1024]{1,0:T(8,128)(2,1)S(1)}, bf16[512,1024]{1,0:T(8,128)(2,1)S(1)}, u32[]{:S(2)}, u32[]{:S(2)}) %collective-permute-start.18) | collective-permute-done | bytes 1048608 | tf_op jit(solution)/shard_map/ppermute | solution.py:408
  444.4 56.3 %collective-permute-start.22 = (bf16[512,1024]{1,0:T(8,128)(2,1)}, bf16[512,1024]{1,0:T(8,128)(2,1)}, u32[]{:S(2)}, u32[]{:S(2)}) collective-permute-start(bf16[512,1024]{1,0:T(8,128)(2,1)} %get-tuple-element.152), channel_id=1, source_target_pairs={{0,2},{6,4},{1,3},{7,5},{8,10},{14,12},{9,11},{15,13},{16,18},{22,... | collective-permute-start | bytes 3145736 | tf_op jit(solution)/shard_map/ppermute | solution.py:408
  508.1 25.7 %collective-permute-done.22 = bf16[512,1024]{1,0:T(8,128)(2,1)} collective-permute-done((bf16[512,1024]{1,0:T(8,128)(2,1)}, bf16[512,1024]{1,0:T(8,128)(2,1)}, u32[]{:S(2)}, u32[]{:S(2)}) %collective-permute-start.22) | collective-permute-done | bytes 1048608 | tf_op jit(solution)/shard_map/ppermute | solution.py:408
  547.6 27.7 %collective-permute-done.26 = bf16[512,1024]{1,0:T(8,128)(2,1)S(1)} collective-permute-done((bf16[512,1024]{1,0:T(8,128)(2,1)S(1)}, bf16[512,1024]{1,0:T(8,128)(2,1)S(1)}, u32[]{:S(2)}, u32[]{:S(2)}) %collective-permute-start.26) | collective-permute-done | bytes 1048608 | tf_op jit(solution)/shard_map/ppermute | solution.py:408
  583.8 33.6 %collective-permute-done.34 = f32[2,1024]{1,0:T(2,128)S(1)} collective-permute-done((f32[2,1024]{1,0:T(2,128)S(1)}, f32[2,1024]{1,0:T(2,128)S(1)}, u32[]{:S(2)}, u32[]{:S(2)}) %collective-permute-start.34) | collective-permute-done | bytes 8224 | tf_op jit(solution)/shard_map/ppermute | solution.py:618
  626.5 8.7 %place.3 = f32[1024,2048]{1,0:T(8,128)} custom-call(s32[2]{0:T(128)} %pad_add_fusion.index_ref, bf16[512,1024]{1,0:T(8,128)(2,1)} %copy-done.8, bf16[512,1024]{1,0:T(8,128)(2,1)} %copy-done.24, bf16[512,1024]{1,0:T(8,128)(2,1)} %copy-done.25, bf16[512,1024]{1,0:T(8,128)(2,1)} %copy-done.28), custom_call_target="tpu_custom_call" | custom-call | bytes 12582912 | tf_op jit(solution)/shard_map/place/pallas_call | solution.py:287
  635.2 20.2 %collective-permute-done.35 = bf16[512,1024]{1,0:T(8,128)(2,1)} collective-permute-done((bf16[512,1024]{1,0:T(8,128)(2,1)S(1)}, bf16[512,1024]{1,0:T(8,128)(2,1)}, u32[]{:S(2)}, u32[]{:S(2)}) %collective-permute-start.35) | collective-permute-done | bytes 1048608 | tf_op jit(solution)/shard_map/ppermute | solution.py:412
  659.4 32.4 %collective-permute-done.39.refs_1_ = bf16[512,1024]{1,0:T(8,128)(2,1)S(1)} collective-permute-done((bf16[512,1024]{1,0:T(8,128)(2,1)S(1)}, bf16[512,1024]{1,0:T(8,128)(2,1)S(1)}, u32[]{:S(2)}, u32[]{:S(2)}) %collective-permute-start.39) | collective-permute-done | bytes 1048608 | tf_op jit(solution)/shard_map/ppermute | solution.py:51
  693.5 8.7 %place.4 = (f32[2048,1024]{1,0:T(8,128)}, f32[2048,512]{1,0:T(8,128)}, f32[2048,512]{1,0:T(8,128)}) custom-call(s32[2]{0:T(128)} %pad_add_fusion.index_ref, bf16[512,1024]{1,0:T(8,128)(2,1)} %copy-done.9, bf16[512,1024]{1,0:T(8,128)(2,1)} %collective-permute-done.36.refs_1_, bf16[512,1024]{1,0:T(8,128)(2,1)} %collective-permute-done.37.refs_2_, ...), custom_call_target="tpu_custom_call" | custom-call | bytes 12582912 | tf_op jit(solution)/shard_map/place/pallas_call | solution.py:287
  702.3 8.7 %place.5 = (f32[2048,1024]{1,0:T(8,128)}, f32[2048,512]{1,0:T(8,128)}, f32[2048,512]{1,0:T(8,128)}) custom-call(s32[2]{0:T(128)} %pad_add_fusion.index_ref, bf16[512,1024]{1,0:T(8,128)(2,1)} %copy-done.10, bf16[512,1024]{1,0:T(8,128)(2,1)} %copy-done.29, bf16[512,1024]{1,0:T(8,128)(2,1)} %copy-done.30, ...), custom_call_target="tpu_custom_call", output_to_operand_aliasing={{0}: (5, {}), {1}: (6, {}), {2}: (7, {})} | custom-call | bytes 12582912 | tf_op jit(solution)/shard_map/place/pallas_call | solution.py:287
  711.0 15.8 %write_whole.3 = f32[2816,2048]{1,0:T(8,128)} custom-call(bf16[16,352,1024]{2,1,0:T(8,128)(2,1)} %bitcast.79), custom_call_target="tpu_custom_call" | custom-call | bytes 34603008 | tf_op jit(solution)/shard_map/write_whole/pallas_call | solution.py:346
  726.7 24.1 %write_whole.2 = (f32[2048,2816]{1,0:T(8,128)}, f32[2048,2816]{1,0:T(8,128)}) custom-call(bf16[16,256,2816]{2,1,0:T(8,128)(2,1)} %bitcast.78), custom_call_target="tpu_custom_call" | custom-call | bytes 69206016 | tf_op jit(solution)/shard_map/write_whole/pallas_call | solution.py:346
  (296 shorter events, 230.6 us)
Async XLA Ops:
  7.2 61.5 %all-gather.6.cloned.1.call-start = ((), (), s32[]{:S(2)}) async-start(), calls=%async_computation.3 | async-start | bytes 2621440 | tf_op jit(solution)/shard_map/all_gather | solution.py:499
  19.9 227.3 %reduce-scatter.4.cloned.1.call-start = ((), (), s32[]{:S(2)}) async-start(), calls=%async_computation.4 | async-start | bytes 3604480 | tf_op jit(solution)/shard_map/reduce_scatter | solution.py:552
  23.0 45.7 %collective-permute-start.1 = (bf16[256,2048]{1,0:T(8,128)(2,1)S(1)}, bf16[256,2048]{1,0:T(8,128)(2,1)}, u32[]{:S(2)}, u32[]{:S(2)}) collective-permute-start(bf16[256,2048]{1,0:T(8,128)(2,1)S(1)} %get-tuple-element.113), channel_id=1, source_target_pairs={{0,16},{16,0},{8,24},{24,8},{1,17},{17,1},{9,25},{25,9},{2,18},{18... | collective-permute-start | bytes 3145736 | tf_op jit(solution)/shard_map/ppermute | solution.py:51
  109.2 39.5 %collective-permute-start.7 = (bf16[256,2048]{1,0:T(8,128)(2,1)S(1)}, bf16[256,2048]{1,0:T(8,128)(2,1)}, u32[]{:S(2)}, u32[]{:S(2)}) collective-permute-start(bf16[256,2048]{1,0:T(8,128)(2,1)S(1)} %get-tuple-element.116), channel_id=1, source_target_pairs={{0,16},{16,0},{8,24},{24,8},{1,17},{17,1},{9,25},{25,9},{2,18},{18... | collective-permute-start | bytes 3145736 | tf_op jit(solution)/shard_map/ppermute | solution.py:51
  154.1 35.2 %collective-permute-start.9 = (bf16[256,2816]{1,0:T(8,128)(2,1)}, bf16[256,2816]{1,0:T(8,128)(2,1)}, u32[]{:S(2)}, u32[]{:S(2)}) collective-permute-start(bf16[256,2816]{1,0:T(8,128)(2,1)} %pad_maximum_fusion.6), channel_id=1, source_target_pairs={{0,16},{16,0},{8,24},{24,8},{1,17},{17,1},{9,25},{25,9},{2,18},{18... | collective-permute-start | bytes 4325384 | tf_op jit(solution)/shard_map/ppermute | solution.py:51
  162.6 160.2 %reduce-scatter.8.cloned.1.call-start = ((), (), s32[]{:S(2)}) async-start(), calls=%async_computation.6 | async-start | bytes 7208960 | tf_op jit(solution)/shard_map/reduce_scatter | solution.py:558
  210.2 159.8 %reduce-scatter.6.cloned.1.call-start = ((), (), s32[]{:S(2)}) async-start(), calls=%async_computation.5 | async-start | bytes 2621440 | tf_op jit(solution)/shard_map/reduce_scatter | solution.py:581
  247.2 463.8 %all-gather.10.cloned.1.call-start = ((), (), s32[]{:S(2)}) async-start(), calls=%async_computation.8 | async-start | bytes 12255232 | tf_op jit(solution)/shard_map/all_gather | solution.py:629
  322.9 403.9 %all-gather.8.cloned.1.call-start = ((), (), s32[]{:S(2)}) async-start(), calls=%async_computation.7 | async-start | bytes 24510464 | tf_op jit(solution)/shard_map/all_gather | solution.py:625
  397.7 39.4 %collective-permute-start.18 = (bf16[512,1024]{1,0:T(8,128)(2,1)S(1)}, bf16[512,1024]{1,0:T(8,128)(2,1)S(1)}, u32[]{:S(2)}, u32[]{:S(2)}) collective-permute-start(bf16[512,1024]{1,0:T(8,128)(2,1)S(1)} %copy-done.26), channel_id=1, source_target_pairs={{0,2},{6,4},{1,3},{7,5},{8,10},{14,12},{9,11},{15,13},{16,18},{22,... | collective-permute-start | bytes 3145736 | tf_op jit(solution)/shard_map/ppermute | solution.py:408
  399.4 38.2 %collective-permute-start.19 = (bf16[512,1024]{1,0:T(8,128)(2,1)S(1)}, bf16[512,1024]{1,0:T(8,128)(2,1)S(1)}, u32[]{:S(2)}, u32[]{:S(2)}) collective-permute-start(bf16[512,1024]{1,0:T(8,128)(2,1)S(1)} %pad_maximum_fusion.8), channel_id=1, source_target_pairs={{0,8},{8,0},{16,24},{24,16},{1,9},{9,1},{17,25},{25,17},{2,10},{10... | collective-permute-start | bytes 3145736 | tf_op jit(solution)/shard_map/ppermute | solution.py:47
  444.4 89.5 %collective-permute-start.22 = (bf16[512,1024]{1,0:T(8,128)(2,1)}, bf16[512,1024]{1,0:T(8,128)(2,1)}, u32[]{:S(2)}, u32[]{:S(2)}) collective-permute-start(bf16[512,1024]{1,0:T(8,128)(2,1)} %get-tuple-element.152), channel_id=1, source_target_pairs={{0,2},{6,4},{1,3},{7,5},{8,10},{14,12},{9,11},{15,13},{16,18},{22,... | collective-permute-start | bytes 3145736 | tf_op jit(solution)/shard_map/ppermute | solution.py:408
  500.7 38.4 %collective-permute-start.23 = (bf16[512,1024]{1,0:T(8,128)(2,1)}, bf16[512,1024]{1,0:T(8,128)(2,1)}, u32[]{:S(2)}, u32[]{:S(2)}) collective-permute-start(bf16[512,1024]{1,0:T(8,128)(2,1)} %add.265), channel_id=1, source_target_pairs={{2,0},{4,6},{3,1},{5,7},{10,8},{12,14},{11,9},{13,15},{18,16},{20,... | collective-permute-start | bytes 3145736 | tf_op jit(solution)/shard_map/ppermute | solution.py:412
  540.4 34.8 %collective-permute-start.26 = (bf16[512,1024]{1,0:T(8,128)(2,1)S(1)}, bf16[512,1024]{1,0:T(8,128)(2,1)S(1)}, u32[]{:S(2)}, u32[]{:S(2)}) collective-permute-start(bf16[512,1024]{1,0:T(8,128)(2,1)S(1)} %copy-done.14), channel_id=1, source_target_pairs={{0,2},{6,4},{1,3},{7,5},{8,10},{14,12},{9,11},{15,13},{16,18},{22,... | collective-permute-start | bytes 3145736 | tf_op jit(solution)/shard_map/ppermute | solution.py:408
  542.8 36.1 %collective-permute-start.28 = (bf16[512,1024]{1,0:T(8,128)(2,1)S(1)}, bf16[512,1024]{1,0:T(8,128)(2,1)S(1)}, u32[]{:S(2)}, u32[]{:S(2)}) collective-permute-start(bf16[512,1024]{1,0:T(8,128)(2,1)S(1)} %broadcast_select_fusion.2.refs_0_), channel_id=1, source_target_pairs={{0,16},{16,0},{8,24},{24,8},{1,17},{17,1},{9,25},{25,9},{2,18},{18... | collective-permute-start | bytes 3145736 | tf_op jit(solution)/shard_map/ppermute | solution.py:51
  544.9 34.0 %collective-permute-start.29 = (bf16[512,1024]{1,0:T(8,128)(2,1)S(1)}, bf16[512,1024]{1,0:T(8,128)(2,1)S(1)}, u32[]{:S(2)}, u32[]{:S(2)}) collective-permute-start(bf16[512,1024]{1,0:T(8,128)(2,1)S(1)} %broadcast_select_fusion.2.refs_0_), channel_id=1, source_target_pairs={{0,8},{8,0},{16,24},{24,16},{1,9},{9,1},{17,25},{25,17},{2,10},{10... | collective-permute-start | bytes 3145736 | tf_op jit(solution)/shard_map/ppermute | solution.py:47
  578.9 38.5 %collective-permute-start.31 = (bf16[512,1024]{1,0:T(8,128)(2,1)S(1)}, bf16[512,1024]{1,0:T(8,128)(2,1)S(1)}, u32[]{:S(2)}, u32[]{:S(2)}) collective-permute-start(bf16[512,1024]{1,0:T(8,128)(2,1)S(1)} %add.270), channel_id=1, source_target_pairs={{2,4},{4,2},{3,5},{5,3},{10,12},{12,10},{11,13},{13,11},{18,20},{2... | collective-permute-start | bytes 3145736 | tf_op jit(solution)/shard_map/ppermute | solution.py:404
  579.6 38.2 %collective-permute-start.32 = (bf16[512,1024]{1,0:T(8,128)(2,1)S(1)}, bf16[512,1024]{1,0:T(8,128)(2,1)S(1)}, u32[]{:S(2)}, u32[]{:S(2)}) collective-permute-start(bf16[512,1024]{1,0:T(8,128)(2,1)S(1)} %add.271), channel_id=1, source_target_pairs={{2,0},{4,6},{3,1},{5,7},{10,8},{12,14},{11,9},{13,15},{18,16},{20,... | collective-permute-start | bytes 3145736 | tf_op jit(solution)/shard_map/ppermute | solution.py:412
  580.9 37.0 %collective-permute-start.33 = (bf16[512,1024]{1,0:T(8,128)(2,1)S(1)}, bf16[512,1024]{1,0:T(8,128)(2,1)S(1)}, u32[]{:S(2)}, u32[]{:S(2)}) collective-permute-start(bf16[512,1024]{1,0:T(8,128)(2,1)S(1)} %collective-permute-done.28.refs_1_), channel_id=1, source_target_pairs={{0,8},{8,0},{16,24},{24,16},{1,9},{9,1},{17,25},{25,17},{2,10},{10... | collective-permute-start | bytes 3145736 | tf_op jit(solution)/shard_map/ppermute | solution.py:47
  581.0 36.4 %collective-permute-start.34 = (f32[2,1024]{1,0:T(2,128)S(1)}, f32[2,1024]{1,0:T(2,128)S(1)}, u32[]{:S(2)}, u32[]{:S(2)}) collective-permute-start(f32[2,1024]{1,0:T(2,128)S(1)} %add.272), channel_id=1, source_target_pairs={{0,2},{2,0},{4,6},{6,4},{1,3},{3,1},{5,7},{7,5},{8,10},{10,8},{12,... | collective-permute-start | bytes 24584 | tf_op jit(solution)/shard_map/ppermute | solution.py:618
  618.0 37.4 %collective-permute-start.35 = (bf16[512,1024]{1,0:T(8,128)(2,1)S(1)}, bf16[512,1024]{1,0:T(8,128)(2,1)}, u32[]{:S(2)}, u32[]{:S(2)}) collective-permute-start(bf16[512,1024]{1,0:T(8,128)(2,1)S(1)} %add.273), channel_id=1, source_target_pairs={{2,0},{4,6},{3,1},{5,7},{10,8},{12,14},{11,9},{13,15},{18,16},{20,... | collective-permute-start | bytes 3145736 | tf_op jit(solution)/shard_map/ppermute | solution.py:412
  619.3 37.5 %collective-permute-start.36 = (bf16[512,1024]{1,0:T(8,128)(2,1)S(1)}, bf16[512,1024]{1,0:T(8,128)(2,1)}, u32[]{:S(2)}, u32[]{:S(2)}) collective-permute-start(bf16[512,1024]{1,0:T(8,128)(2,1)S(1)} %broadcast_select_fusion.1.refs_0_), channel_id=1, source_target_pairs={{0,16},{16,0},{8,24},{24,8},{1,17},{17,1},{9,25},{25,9},{2,18},{18... | collective-permute-start | bytes 3145736 | tf_op jit(solution)/shard_map/ppermute | solution.py:51
  621.3 35.5 %collective-permute-start.37 = (bf16[512,1024]{1,0:T(8,128)(2,1)S(1)}, bf16[512,1024]{1,0:T(8,128)(2,1)}, u32[]{:S(2)}, u32[]{:S(2)}) collective-permute-start(bf16[512,1024]{1,0:T(8,128)(2,1)S(1)} %broadcast_select_fusion.1.refs_0_), channel_id=1, source_target_pairs={{0,8},{8,0},{16,24},{24,16},{1,9},{9,1},{17,25},{25,17},{2,10},{10... | collective-permute-start | bytes 3145736 | tf_op jit(solution)/shard_map/ppermute | solution.py:47
  656.8 35.1 %collective-permute-start.39 = (bf16[512,1024]{1,0:T(8,128)(2,1)S(1)}, bf16[512,1024]{1,0:T(8,128)(2,1)S(1)}, u32[]{:S(2)}, u32[]{:S(2)}) collective-permute-start(bf16[512,1024]{1,0:T(8,128)(2,1)S(1)} %broadcast_select_fusion.refs_0_), channel_id=1, source_target_pairs={{0,16},{16,0},{8,24},{24,8},{1,17},{17,1},{9,25},{25,9},{2,18},{18... | collective-permute-start | bytes 3145736 | tf_op jit(solution)/shard_map/ppermute | solution.py:51
  (73 other events, 989.2 us)
Sparse Core Ops, SparseCore 0:
  20.0 48.6 all-gather.5
  162.8 55.0 reduce-scatter.3
  220.7 102.1 reduce-scatter.7
  325.6 44.3 reduce-scatter.5
  372.4 115.8 all-gather.9
  489.7 215.0 all-gather.7

commit v3 on v2

--- a/solution.py
+++ b/solution.py
@@ -15,8 +15,6 @@
 ACROSS = [(0, 2), (2, 0), (1, 3), (3, 1)]
 CORES = [(0, 1), (1, 0), (2, 3), (3, 2)]
 PAIRS = [(0, 1), (1, 0), (2, 3), (3, 2)]
-MIDDLE = [(1, 2), (2, 1)]
-QKV_CHUNKS = 2
 
 
 def dot(a, b):
@@ -49,10 +47,6 @@
 
 def to_chip(sent):
     return lax.ppermute(sent, "dp", ACROSS)
-
-
-def fits(rows, widths):
-    return rows % 16 == 0 and all(w % 128 == 0 for w in widths)
 
 
 def tables(positions):
@@ -230,77 +224,6 @@
     )(dkv, cos, sin)
 
 
-def place_kernel(index_ref, *refs, widths, split):
-    outs = refs[len(refs) - len(widths) :]
-    step = pl.program_id(0)
-    for number in range(4):
-
-        @pl.when(step // split == number)
-        def _(source=refs[number]):
-            start = 0
-            for width, out in zip(widths, outs):
-                out[...] = source[:, start : start + width].astype(F32)
-                start += width
-
-
-def place(previous, pieces, row, quarter_rows, widths, row_by_core):
-    rows, cols = pieces[0].shape
-    me = lax.axis_index("dp")
-    if not fits(rows, widths):
-        outs = []
-        start = 0
-        for number, width in enumerate(widths):
-            buffer = jnp.zeros((2 * quarter_rows, 2 * width), F32)
-            if previous is not None:
-                buffer = previous[number]
-            for piece, mask in zip(pieces, (0, 2, 1, 3)):
-                other = jnp.bitwise_xor(me, mask)
-                chip, core = other // 2, other % 2
-                first, second = (core, chip) if row_by_core else (chip, core)
-                at = (first * quarter_rows + row, second * width)
-                source = piece[:, start : start + width].astype(F32)
-                buffer = lax.dynamic_update_slice(buffer, source, at)
-            outs.append(buffer)
-            start += width
-        return outs
-    split = 2 if rows % 32 == 0 else 1
-    part = rows // split
-
-    def out_index(step, index_ref):
-        piece = step // split
-        chip = jnp.where(piece % 2 == 0, index_ref[0], 1 - index_ref[0])
-        core = jnp.where(piece < 2, index_ref[1], 1 - index_ref[1])
-        first, second = (core, chip) if row_by_core else (chip, core)
-        return first * (quarter_rows // part) + row // part + step % split, second
-
-    def in_index(number):
-        return lambda step, _: (jnp.clip(step - number * split, 0, split - 1), 0)
-
-    in_specs = [pl.BlockSpec((part, cols), in_index(n)) for n in range(4)]
-    operands = [jnp.stack([me // 2, me % 2]).astype(jnp.int32)] + list(pieces)
-    aliases = {}
-    if previous is not None:
-        for number, buffer in enumerate(previous):
-            in_specs.append(pl.BlockSpec(memory_space=pl.ANY))
-            aliases[len(operands)] = number
-            operands.append(buffer)
-    return pl.pallas_call(
-        functools.partial(place_kernel, widths=widths, split=split),
-        grid_spec=pltpu.PrefetchScalarGridSpec(
-            num_scalar_prefetch=1,
-            grid=(4 * split,),
-            in_specs=in_specs,
-            out_specs=[pl.BlockSpec((part, width), out_index) for width in widths],
-        ),
-        out_shape=[jax.ShapeDtypeStruct((2 * quarter_rows, 2 * w), F32) for w in widths],
-        input_output_aliases=aliases,
-        cost_estimate=pl.CostEstimate(
-            flops=0, bytes_accessed=24 * rows * cols, transcendentals=0
-        ),
-        name="place",
-    )(*operands)
-
-
 def share_kernel(every_ref, *out_refs, pieces):
     out_refs = list(out_refs)
     for start, stop, widths in pieces:
@@ -356,79 +279,37 @@
     )(every)
 
 
-class Chain:
-    def __init__(self):
-        rank = lax.axis_index("seq")
-        self.is_middle = (rank == 1) | (rank == 2)
-        self.stages = {n: [] for n in ("in", "middle", "out", "across", "core")}
-        self.outs = {}
-        self.time = 0
-        self.fresh = []
-        self.writes = []
-        self.arrived = []
-
-    def add(self, name, quarter, count, widths, row_by_core):
-        size = quarter.shape[0] // count
-        for i in range(count):
-            info = (name, i * size, quarter.shape[0], widths, row_by_core)
-            self.stages["in"].append((0, quarter[i * size : (i + 1) * size], info))
-
-    def busy(self):
-        return bool(self.writes) or any(self.stages.values())
-
-    def put(self, stage, value, info):
-        self.stages[stage].append((self.time + 1, value, info))
-
-    def tick(self, *values):
-        self.time += 1
-        taken = {}
-        for name, queue in self.stages.items():
-            if queue and queue[0][0] <= self.time:
-                taken[name] = queue.pop(0)
-        names = list(taken)
-        done = self.arrived
-        writes, self.writes = self.writes, []
-        fresh, self.fresh = self.fresh, []
-        flat = [taken[n][1] for n in names]
-        flat += [a for pieces, _ in writes for a in pieces]
-        flat += [b for n in fresh for b in self.outs[n]]
-        tied = list(lax.optimization_barrier(tuple(flat) + tuple(done) + tuple(values)))
-        values = tied[len(tied) - len(values) :] if values else []
-        now = {n: tied.pop(0) for n in names}
-        writes = [([tied.pop(0) for _ in pieces], info) for pieces, info in writes]
-        for n in fresh:
-            self.outs[n] = [tied.pop(0) for _ in self.outs[n]]
-        meta = {n: taken[n][2] for n in names}
-        arrived = []
-        if "middle" in now:
-            other = lax.ppermute(now["middle"], "seq", MIDDLE)
-            arrived.append(other)
-            self.put("out", now["middle"] + other, meta["middle"])
-        if "in" in now:
-            other = lax.ppermute(now["in"], "seq", [(0, 1), (3, 2)])
-            arrived.append(other)
-            self.put("middle", now["in"] + other, meta["in"])
-        if "out" in now:
-            other = lax.ppermute(now["out"], "seq", [(1, 0), (2, 3)])
-            arrived.append(other)
-            self.put("across", jnp.where(self.is_middle, now["out"], other), meta["out"])
-        if "across" in now:
-            other = to_chip(now["across"])
-            beside = to_core(now["across"])
-            arrived += [other, beside]
-            self.put("core", other, (now["across"], beside, meta["across"]))
-        if "core" in now:
-            other = to_core(now["core"])
-            arrived.append(other)
-            own, beside, info = meta["core"]
-            self.writes.append(([own, now["core"], beside, other], info))
-        for pieces, (name, row, quarter_rows, widths, row_by_core) in writes:
-            self.fresh.append(name)
-            self.outs[name] = place(
-                self.outs.get(name), pieces, row, quarter_rows, widths, row_by_core
-            )
-        self.arrived = arrived
-        return values if len(values) != 1 else values[0]
+def share(down_part, gate_up_part, out_quarter, qkv_quarter, widths):
+    half_ff = gate_up_part.shape[1] // 2
+    gate_up = lax.all_gather(gate_up_part, ("dp", "seq"), axis=0, tiled=False)
+    gate, up = write_whole(gate_up, [(gate_up_part.shape[0], (half_ff, half_ff), True)])
+    seq = lax.axis_size("seq")
+    cols = out_quarter.shape[1]
+    out_rows, qkv_rows = out_quarter.shape[0] // seq, qkv_quarter.shape[0] // seq
+    down_rows = down_part.shape[0]
+    if qkv_quarter.shape[1] == cols:
+        joined = jnp.concatenate(
+            [out_quarter.reshape(seq, out_rows, cols), qkv_quarter.reshape(seq, qkv_rows, cols)],
+            axis=1,
+        )
+        part = lax.psum_scatter(joined, "seq", scatter_dimension=0, tiled=False)
+        part = jnp.concatenate([down_part, part.reshape(out_rows + qkv_rows, cols)], axis=0)
+        every = lax.all_gather(part, ("dp", "seq"), axis=0, tiled=False)
+        down, out, query, key, value = write_whole(
+            every,
+            [(down_rows, (cols,), False), (out_rows, (cols,), False), (qkv_rows, widths, True)],
+        )
+    else:
+        out_part = lax.psum_scatter(out_quarter, "seq", scatter_dimension=0, tiled=True)
+        qkv_part = lax.psum_scatter(qkv_quarter, "seq", scatter_dimension=0, tiled=True)
+        part = jnp.concatenate([down_part, out_part], axis=0)
+        every = lax.all_gather(part, ("dp", "seq"), axis=0, tiled=False)
+        down, out = write_whole(
+            every, [(down_rows, (cols,), False), (out_rows, (cols,), False)]
+        )
+        every = lax.all_gather(qkv_part, ("dp", "seq"), axis=0, tiled=False)
+        query, key, value = write_whole(every, [(qkv_rows, widths, True)])
+    return dict(gate=gate, up=up, down=down, out=out, query=query, key=key, value=value)
 
 
 def tie(*values):
@@ -529,7 +410,6 @@
     hn2 = (hidden * scale_two * gain_two).astype(BF)
     hn2, hidden, scale_two, hn1_core, df_core = tie(hn2, hidden, scale_two, hn1_core, df_core)
 
-    hn2_other = to_chip(hn2)
     g = dot(hn2, w_gate)
     u = dot(hn2, w_up)
     sig = jax.nn.sigmoid(g)
@@ -541,22 +421,14 @@
 
     z_other = to_chip(half(z, 1 - chip))
     dn2_part = (dot_t(dg, w_gate) + dot_t(du, w_up)).astype(BF)
-    z_other, dn2_part, hn2_other, dg, du = tie(z_other, dn2_part, hn2_other, dg, du)
+    z_other, dn2_part, dg, du, hn2 = tie(z_other, dn2_part, dg, du, hn2)
+    hn2_other = to_chip(hn2)
 
     dn2_other = swap_tensor(dn2_part)
     z_chip = by_chip(half(z, chip), z_other)
-    hn2_core = by_core(hn2, hn2_other)
     dgu_other = to_chip(jnp.concatenate([half(dg, 1 - chip), half(du, 1 - chip)], axis=1))
-    down_quarter = dot_rows(z_chip, df_core)
-    down_quarter, hn2_core = tie(down_quarter, hn2_core)
+    down_quarter, hidden = tie(dot_rows(z_chip, df_core), hidden)
     down_part = lax.psum_scatter(down_quarter, "seq", scatter_dimension=0, tiled=True)
-    dn2_other, dgu_other = tie(dn2_other, dgu_other)
-
-    dgu = jnp.concatenate([half(dg, chip), half(du, chip)], axis=1)
-    dgu_chip = by_chip(dgu, dgu_other)
-    gate_up_quarter = dot_rows(hn2_core, dgu_chip)
-    gate_up_part = lax.psum_scatter(gate_up_quarter, "seq", scatter_dimension=0, tiled=True)
-
     dn2 = dn2_part.astype(F32) + dn2_other
     grad_f = g_in.astype(F32)
     d_scaled = dn2 * gain_two
@@ -574,71 +446,61 @@
         dqs.append(dq)
         dkvs.append(dkv)
     dqb = jnp.concatenate(dqs, axis=0)
-    dkvs, dqb, da_other, o_other, down_part = tie(
-        jnp.stack(dkvs), dqb, da_other, o_other, down_part
+    dkvs, dqb, hn2_other, dgu_other, down_part = tie(
+        jnp.stack(dkvs), dqb, hn2_other, dgu_other, down_part
     )
-
     dkv = lax.psum_scatter(dkvs, "seq", scatter_dimension=1, tiled=True)
+
+    hn2_core = by_core(hn2, hn2_other)
+    dgu = jnp.concatenate([half(dg, chip), half(du, chip)], axis=1)
+    dgu_chip = by_chip(dgu, dgu_other)
+    gate_up_quarter = dot_rows(hn2_core, dgu_chip)
+    dkv, da_other, o_other, gate_up_quarter = tie(dkv, da_other, o_other, gate_up_quarter)
+    gate_up_part = lax.psum_scatter(gate_up_quarter, "seq", scatter_dimension=0, tiled=True)
     dq_part = dot_t(dqb, query_weight)
     branch = scatter_tensor(dot(z, w_down))
     da_core = by_core(da, da_other)
     o_chip = by_chip(half(ob, chip), o_other)
     out_quarter = dot_rows(o_chip, da_core)
     output = (mine(hidden) + active * branch).astype(BF)
-    dkv, dq_part, out_quarter, output = tie(dkv, dq_part, out_quarter, output)
-
-    chain = Chain()
-    chain.add("out", out_quarter, 1, (core_half,), False)
+
     dkb, dvb = turn_back(dkv.reshape(rows, -1), cos, sin)
     grads = (dqb, dkb, dvb)
     widths = tuple(a.shape[1] // 2 for a in grads)
     qkv_other = to_chip(jnp.concatenate([half(a, 1 - chip) for a in grads], axis=1))
     qkv_own = jnp.concatenate([half(a, chip) for a in grads], axis=1)
-    dn1 = dq_part + dot_t(dkb, key_weight) + dot_t(dvb, value_weight)
-    qkv_other, qkv_own, dn1 = chain.tick(qkv_other, qkv_own, dn1)
+    qkv_other, qkv_own = tie(qkv_other, qkv_own)
     qkv_chip = by_chip(qkv_own, qkv_other)
     qkv_quarter = dot_rows(hn1_core, qkv_chip)
-    dn1 = scatter_tensor(dn1)
-    qkv_quarter, dn1 = chain.tick(qkv_quarter, dn1)
-    chain.add("qkv", qkv_quarter, QKV_CHUNKS, widths, True)
-
+    out_quarter, qkv_quarter, gate_up_part = tie(out_quarter, qkv_quarter, gate_up_part)
+    results = share(down_part, gate_up_part, out_quarter, qkv_quarter, widths)
+
+    dn1 = scatter_tensor(dq_part + dot_t(dkb, key_weight) + dot_t(dvb, value_weight))
     d_scaled_one = dn1 * gain_one_s
     in_slice = mine(in_f)
     inner_own = jnp.sum(d_scaled_one * in_slice, axis=-1)
     gains = jnp.stack([jnp.sum(dn1 * in_slice * scale_one, axis=0), gain_terms])
-    inner_own, gains, d_scaled_one = chain.tick(inner_own, gains, d_scaled_one)
     inner_one = (inner_own + swap_tensor(inner_own))[:, None]
     input_grad = (
         mine(dh) + scale_one * d_scaled_one - in_slice * scale_one**3 * (inner_one / width)
     )
     gains = gains + to_chip(gains)
-    gains, input_grad = chain.tick(gains, input_grad)
     gains = gains + to_core(gains)
-    gains = chain.tick(gains)
     gains = gains + lax.ppermute(gains, "seq", PAIRS)
-    gains = chain.tick(gains)
     gains = gains + lax.ppermute(gains, "seq", [(0, 2), (2, 0), (1, 3), (3, 1)])
-    gains = chain.tick(gains)
-    while chain.busy():
-        chain.tick()
-
-    gate_up = lax.all_gather(gate_up_part, ("dp", "seq"), axis=0, tiled=False)
-    half_ff = z.shape[1] // 2
-    gate, up = write_whole(gate_up, [(gate_up_part.shape[0], (half_ff, half_ff), True)])
-    down_part, _ = tie(down_part, gate_up_part)
-    every = lax.all_gather(down_part, ("dp", "seq"), axis=0, tiled=False)
-    (down,) = write_whole(every, [(down_part.shape[0], (core_half,), False)])
 
     return (
         output.reshape(micro, 1, length, slice_width),
         input_grad.reshape(micro, 1, length, slice_width),
         gains[0],
-        *chain.outs["qkv"],
-        chain.outs["out"][0],
+        results["query"],
+        results["key"],
+        results["value"],
+        results["out"],
         gains[1],
-        gate,
-        up,
-        down,
+        results["gate"],
+        results["up"],
+        results["down"],
     )
 
 

time: 767 us -> 719 us (0.937)
  starting transfers between devices: 103 us -> 25.2 us
  waiting for transfers between devices: 376 us -> 443 us
  Pallas kernels: 105 us -> 88.8 us
  other arithmetic: 51.3 us -> 41.1 us
  matrix products: 84.8 us -> 75 us
    all_gather x2, waiting for transfers between devices: 0.01 us -> 189 us  [the longest x1 108 us: share(): every = lax.all_gather(part, ('dp', 'seq'), axis=0, tiled=False)]
    ppermute x9 -> x0, waiting for transfers between devices: 99.9 us -> none  [the longest x3 76.5 us: tick(): other = lax.ppermute(now['in'], 'seq', [(0, 1), (3, 2)])]
    ppermute x9 -> x0, starting transfers between devices: 65.6 us -> none  [the longest x3 59.5 us: tick(): other = lax.ppermute(now['in'], 'seq', [(0, 1), (3, 2)])]
    reduce_scatter x0 -> x1, waiting for transfers between devices: none -> 60 us  [share(): part = lax.psum_scatter(joined, 'seq', scatter_dimension=0, tiled=False)]
    ppermute x1, waiting for transfers between devices: 33.6 us -> 1.56 us  [on_device(): gains = gains + lax.ppermute(gains, 'seq', PAIRS)]
    pallas_call x3 -> x0, Pallas kernels: 26.2 us -> none  [place(): pl.pallas_call(functools.partial(place_kernel, widths=widths, split=split...]
    ppermute x12 -> x9, waiting for transfers between devices: 89.7 us -> 67.2 us  [to_chip(): return lax.ppermute(sent, 'dp', ACROSS)]
    ppermute x6, waiting for transfers between devices: 55.7 us -> 38.8 us  [swap_tensor(): return lax.ppermute(sent, 'tensor', [(0, 1), (1, 0)]).astype(F32)]
  transfers between devices with their start and end apart: 50 -> 33, of which waited for: 23 -> 22; matrix products, arithmetic and copies ran while one was open for 18% -> 14% of each run, Pallas kernels for 9% -> 7%
where the time goes in v3:
time: 719 us; the launch traced here: 715 us
  waiting for transfers between devices  443 us (62%)
  Pallas kernels  88.8 us (12%)
  matrix products  75 us (10%)
  other arithmetic  41.1 us (6%)
  local copies, waits for them, and re-layouts  26.3 us (4%)
  starting transfers between devices  25.2 us (4%)
  between operations  15.1 us (2%)
    all_gather x1, waiting for transfers between devices, share(): every = lax.all_gather(part, ('dp', 'seq'), axis=0, tiled=False)  108 us
    all_gather x1, waiting for transfers between devices, share(): gate_up = lax.all_gather(gate_up_part, ('dp', 'seq'), axis=0, tiled=False)  80.4 us
    reduce_scatter x1, waiting for transfers between devices, on_device(): lax.psum_scatter(gate_up_quarter, 'seq', scatter_dimension=0, tiled=True)  72.9 us
    ppermute x9, waiting for transfers between devices, to_chip(): return lax.ppermute(sent, 'dp', ACROSS)  67.2 us
    reduce_scatter x1, waiting for transfers between devices, share(): part = lax.psum_scatter(joined, 'seq', scatter_dimension=0, tiled=False)  60 us
    pallas_call x2, Pallas kernels, write_whole(): pl.pallas_call(functools.partial(share_kernel, pieces=tuple(spans)), grid...  49.8 us
    ppermute x6, waiting for transfers between devices, swap_tensor(): return lax.ppermute(sent, 'tensor', [(0, 1), (1, 0)]).astype(F32)  38.8 us
    dot_general x7, matrix products, dot_t(): lax.dot_general(a, b, (((1,), (1,)), ((), ())), preferred_element_type=F32)  30.3 us
  transfers between devices with their start and end apart: 33, of which 22 were waited for; matrix products, arithmetic and copies ran while one was open for 14% of the time, Pallas kernels for 7%

profile of v3, /device:TPU:0, one launch (start us, length us, event | category | flops | bytes accessed | tf_op | source)
XLA Modules:
  0.0 714.6 jit_solution(483578748688960867)
XLA Ops:
  14.0 6.2 keys_and_values.1
  30.8 9.2 %fusion.61 = f32[256,2816]{1,0:T(8,128)} fusion(bf16[256,2048]{1,0:T(8,128)(2,1)S(1)} %get-tuple-element.70, bf16[2816,2048]{1,0:T(8,128)(2,1)} %param.24), kind=kOutput, calls=%fused_computation.150 | convolution fusion | flops 2952790016 | bytes 15466496 | tf_op jit(solution)/shard_map/dot_general | solution.py:25
  40.0 7.9 %collective-permute-done = bf16[256,2048]{1,0:T(8,128)(2,1)} collective-permute-done((bf16[256,2048]{1,0:T(8,128)(2,1)S(1)}, bf16[256,2048]{1,0:T(8,128)(2,1)}, u32[]{:S(2)}, u32[]{:S(2)}) %collective-permute-start) | collective-permute-done | bytes 1048608 | tf_op jit(solution)/shard_map/ppermute | solution.py:49
  47.9 21.6 %collective-permute-done.1 = bf16[256,2048]{1,0:T(8,128)(2,1)} collective-permute-done((bf16[256,2048]{1,0:T(8,128)(2,1)S(1)}, bf16[256,2048]{1,0:T(8,128)(2,1)}, u32[]{:S(2)}, u32[]{:S(2)}) %collective-permute-start.1) | collective-permute-done | bytes 1048608 | tf_op jit(solution)/shard_map/ppermute | solution.py:49
  98.1 8.0 %collective-permute-done.2 = bf16[128,2048]{1,0:T(8,128)(2,1)S(1)} collective-permute-done((bf16[128,2048]{1,0:T(8,128)(2,1)S(1)}, bf16[128,2048]{1,0:T(8,128)(2,1)S(1)}, u32[]{:S(2)}, u32[]{:S(2)}) %collective-permute-start.2) | collective-permute-done | bytes 524320 | tf_op jit(solution)/shard_map/ppermute | solution.py:35
  115.0 6.6 fusion.63
  126.1 6.0 fusion.64
  132.2 8.4 %fusion.18 = bf16[256,2048]{1,0:T(8,128)(2,1)} fusion(f32[256,2048]{1,0:T(8,128)S(1)} %fusion.64, bf16[256,2816]{1,0:T(8,128)(2,1)S(1)} %get-tuple-element.89, bf16[2048,2816]{1,0:T(8,128)(2,1)} %param.23), kind=kOutput, calls=%fused_computation.27 | convolution fusion | flops 2953838592 | bytes 16121856 | tf_op jit(solution)/shard_map/dot_general | solution.py:25
  156.8 17.6 %collective-permute-done.9 = bf16[256,2048]{1,0:T(8,128)(2,1)S(1)} collective-permute-done((bf16[256,2048]{1,0:T(8,128)(2,1)}, bf16[256,2048]{1,0:T(8,128)(2,1)S(1)}, u32[]{:S(2)}, u32[]{:S(2)}) %collective-permute-start.9) | collective-permute-done | bytes 1048608 | tf_op jit(solution)/shard_map/ppermute | solution.py:35
  181.0 6.9 attend_back.3
  187.9 6.8 attend_back.2
  199.5 6.8 collective-permute-done.11
  217.3 11.2 %fusion.8 = bf16[1024,2816]{1,0:T(8,128)(2,1)} fusion(bf16[512,2816]{1,0:T(8,128)(2,1)} %collective-permute-done.15, bf16[256,2816]{1,0:T(8,128)(2,1)} %collective-permute-done.11, bf16[256,1408]{1,0:T(8,128)(2,1)} %get-tuple-element.160, bf16[256,1408]{1,0:T(8,128)(2,1)} %get-tuple-element.158, bf16[512,1024]{1,0:T(8,128)(2,1)} %collective-permute-done.14, ...), kind=kOutput, calls=%fused_computation.8 | convolution fusion | flops 5935726592 | bytes 13631488 | tf_op jit(solution)/shard_map/dot_general | solution.py:29
  228.5 17.7 %collective-permute-done.12 = bf16[256,2048]{1,0:T(8,128)(2,1)} collective-permute-done((bf16[256,2048]{1,0:T(8,128)(2,1)}, bf16[256,2048]{1,0:T(8,128)(2,1)}, u32[]{:S(2)}, u32[]{:S(2)}) %collective-permute-start.12) | collective-permute-done | bytes 1048608 | tf_op jit(solution)/shard_map/ppermute | solution.py:49
  246.3 6.6 reduce-scatter.7.cloned.1.call-done
  264.3 10.4 %collective-permute-done.24 = bf16[256,1024]{1,0:T(8,128)(2,1)S(1)} collective-permute-done((bf16[256,1024]{1,0:T(8,128)(2,1)S(1)}, bf16[256,1024]{1,0:T(8,128)(2,1)S(1)}, u32[]{:S(2)}, u32[]{:S(2)}) %collective-permute-start.24) | collective-permute-done | bytes 524320 | tf_op jit(solution)/shard_map/ppermute | solution.py:49
  284.4 72.9 %reduce-scatter.9.cloned.1.call-done = bf16[256,2816]{1,0:T(8,128)(2,1)} async-done(((bf16[1024,2816]{1,0:T(8,128)(2,1)}), bf16[256,2816]{1,0:T(8,128)(2,1)}) %reduce-scatter.9.cloned.1.call-update) | async-done | bytes 1441808 | tf_op jit(solution)/shard_map/reduce_scatter | solution.py:459
  362.0 60.0 %reduce-scatter.11.cloned.1.call-done = bf16[1,384,1024]{2,1,0:T(8,128)(2,1)} async-done(((bf16[4,384,1024]{2,1,0:T(8,128)(2,1)}), bf16[1,384,1024]{2,1,0:T(8,128)(2,1)}) %reduce-scatter.11.cloned.1.call-update) | async-done | bytes 786448 | tf_op jit(solution)/shard_map/reduce_scatter | solution.py:295
  434.3 6.3 fusion.65
  441.3 6.4 collective-permute-done.16
  468.8 80.4 %all-gather.10.cloned.1.call-done = bf16[4096,2816]{1,0:T(8,128)(2,1)} async-done(((bf16[256,2816]{1,0:T(8,128)(2,1)}), bf16[4096,2816]{1,0:T(8,128)(2,1)}) %all-gather.10.cloned.1.call-update) | async-done | bytes 23068688 | tf_op jit(solution)/shard_map/all_gather | solution.py:284
  549.2 24.2 %write_whole.3 = (f32[2048,2816]{1,0:T(8,128)}, f32[2048,2816]{1,0:T(8,128)}) custom-call(bf16[16,256,2816]{2,1,0:T(8,128)(2,1)} %bitcast.79), custom_call_target="tpu_custom_call" | custom-call | bytes 69206016 | tf_op jit(solution)/shard_map/write_whole/pallas_call | solution.py:269
  573.4 108.5 %all-gather.8.cloned.1.call-done = bf16[11776,1024]{1,0:T(8,128)(2,1)} async-done(((bf16[736,1024]{1,0:T(8,128)(2,1)}), bf16[11776,1024]{1,0:T(8,128)(2,1)}) %all-gather.8.cloned.1.call-update) | async-done | bytes 24117264 | tf_op jit(solution)/shard_map/all_gather | solution.py:297
  681.9 25.6 %write_whole.2 = (f32[2816,2048]{1,0:T(8,128)}, f32[1024,2048]{1,0:T(8,128)}, f32[2048,1024]{1,0:T(8,128)}, f32[2048,512]{1,0:T(8,128)}, f32[2048,512]{1,0:T(8,128)}) custom-call(bf16[16,736,1024]{2,1,0:T(8,128)(2,1)} %bitcast.78), custom_call_target="tpu_custom_call" | custom-call | bytes 72351744 | tf_op jit(solution)/shard_map/write_whole/pallas_call | solution.py:269
  (229 shorter events, 157.0 us)
Async XLA Ops:
  7.2 62.3 %all-gather.6.cloned.1.call-start = ((), (), s32[]{:S(2)}) async-start(), calls=%async_computation.4 | async-start | bytes 2621440 | tf_op jit(solution)/shard_map/all_gather | solution.py:380
  20.2 186.1 %reduce-scatter.5.cloned.1.call-start = ((), (), s32[]{:S(2)}) async-start(), calls=%async_computation.5 | async-start | bytes 3604480 | tf_op jit(solution)/shard_map/reduce_scatter | solution.py:431
  20.8 27.1 %collective-permute-start = (bf16[256,2048]{1,0:T(8,128)(2,1)S(1)}, bf16[256,2048]{1,0:T(8,128)(2,1)}, u32[]{:S(2)}, u32[]{:S(2)}) collective-permute-start(bf16[256,2048]{1,0:T(8,128)(2,1)S(1)} %copy-done.3), channel_id=1, source_target_pairs={{0,16},{16,0},{8,24},{24,8},{1,17},{17,1},{9,25},{25,9},{2,18},{18... | collective-permute-start | bytes 3145736 | tf_op jit(solution)/shard_map/ppermute | solution.py:49
  23.8 45.7 %collective-permute-start.1 = (bf16[256,2048]{1,0:T(8,128)(2,1)S(1)}, bf16[256,2048]{1,0:T(8,128)(2,1)}, u32[]{:S(2)}, u32[]{:S(2)}) collective-permute-start(bf16[256,2048]{1,0:T(8,128)(2,1)S(1)} %get-tuple-element.70), channel_id=1, source_target_pairs={{0,16},{16,0},{8,24},{24,8},{1,17},{17,1},{9,25},{25,9},{2,18},{18... | collective-permute-start | bytes 3145736 | tf_op jit(solution)/shard_map/ppermute | solution.py:49
  81.6 15.2 %collective-permute-start.3 = (bf16[128,2048]{1,0:T(8,128)(2,1)}, bf16[128,2048]{1,0:T(8,128)(2,1)}, u32[]{:S(2)}, u32[]{:S(2)}) collective-permute-start(bf16[128,2048]{1,0:T(8,128)(2,1)} %convolution_convert_fusion.1), channel_id=1, source_target_pairs={{0,1},{1,0},{2,3},{3,2},{4,5},{5,4},{6,7},{7,6},{8,9},{9,8},{10,11... | collective-permute-start | bytes 1572872 | tf_op jit(solution)/shard_map/ppermute | solution.py:35
  91.7 14.5 %collective-permute-start.2 = (bf16[128,2048]{1,0:T(8,128)(2,1)S(1)}, bf16[128,2048]{1,0:T(8,128)(2,1)S(1)}, u32[]{:S(2)}, u32[]{:S(2)}) collective-permute-start(bf16[128,2048]{1,0:T(8,128)(2,1)S(1)} %convolution_convert_fusion.2), channel_id=1, source_target_pairs={{0,1},{1,0},{2,3},{3,2},{4,5},{5,4},{6,7},{7,6},{8,9},{9,8},{10,11... | collective-permute-start | bytes 1572872 | tf_op jit(solution)/shard_map/ppermute | solution.py:35
  93.6 13.9 %collective-permute-start.4 = (bf16[512,1024]{1,0:T(8,128)(2,1)S(1)}, bf16[512,1024]{1,0:T(8,128)(2,1)S(1)}, u32[]{:S(2)}, u32[]{:S(2)}) collective-permute-start(bf16[512,1024]{1,0:T(8,128)(2,1)S(1)} %get-tuple-element.155), channel_id=1, source_target_pairs={{0,8},{8,0},{16,24},{24,16},{1,9},{9,1},{17,25},{25,17},{2,10},{10... | collective-permute-start | bytes 3145736 | tf_op jit(solution)/shard_map/ppermute | solution.py:45
  96.3 12.8 %collective-permute-start.5 = (bf16[512,1024]{1,0:T(8,128)(2,1)S(1)}, bf16[512,1024]{1,0:T(8,128)(2,1)S(1)}, u32[]{:S(2)}, u32[]{:S(2)}) collective-permute-start(bf16[512,1024]{1,0:T(8,128)(2,1)S(1)} %get-tuple-element.153), channel_id=1, source_target_pairs={{0,8},{8,0},{16,24},{24,16},{1,9},{9,1},{17,25},{25,17},{2,10},{10... | collective-permute-start | bytes 3145736 | tf_op jit(solution)/shard_map/ppermute | solution.py:45
  124.5 16.5 %collective-permute-start.6 = (bf16[256,1408]{1,0:T(8,128)(2,1)S(1)}, bf16[256,1408]{1,0:T(8,128)(2,1)S(1)}, u32[]{:S(2)}, u32[]{:S(2)}) collective-permute-start(bf16[256,1408]{1,0:T(8,128)(2,1)S(1)} %get-tuple-element.163), channel_id=1, source_target_pairs={{0,16},{16,0},{8,24},{24,8},{1,17},{17,1},{9,25},{25,9},{2,18},{18... | collective-permute-start | bytes 2162696 | tf_op jit(solution)/shard_map/ppermute | solution.py:49
  148.9 103.9 %reduce-scatter.7.cloned.1.call-start = ((), (), s32[]{:S(2)}) async-start(), calls=%async_computation.6 | async-start | bytes 2621440 | tf_op jit(solution)/shard_map/reduce_scatter | solution.py:452
  149.0 25.5 %collective-permute-start.9 = (bf16[256,2048]{1,0:T(8,128)(2,1)}, bf16[256,2048]{1,0:T(8,128)(2,1)S(1)}, u32[]{:S(2)}, u32[]{:S(2)}) collective-permute-start(bf16[256,2048]{1,0:T(8,128)(2,1)} %fusion.18), channel_id=1, source_target_pairs={{0,1},{1,0},{2,3},{3,2},{4,5},{5,4},{6,7},{7,6},{8,9},{9,8},{10,11... | collective-permute-start | bytes 3145736 | tf_op jit(solution)/shard_map/ppermute | solution.py:35
  150.2 49.3 %collective-permute-start.10 = (bf16[256,2048]{1,0:T(8,128)(2,1)}, bf16[256,2048]{1,0:T(8,128)(2,1)}, u32[]{:S(2)}, u32[]{:S(2)}) collective-permute-start(bf16[256,2048]{1,0:T(8,128)(2,1)} %copy-done.19), channel_id=1, source_target_pairs={{0,16},{16,0},{8,24},{24,8},{1,17},{17,1},{9,25},{25,9},{2,18},{18... | collective-permute-start | bytes 3145736 | tf_op jit(solution)/shard_map/ppermute | solution.py:49
  156.3 50.1 %collective-permute-start.11 = (bf16[256,2816]{1,0:T(8,128)(2,1)}, bf16[256,2816]{1,0:T(8,128)(2,1)}, u32[]{:S(2)}, u32[]{:S(2)}) collective-permute-start(bf16[256,2816]{1,0:T(8,128)(2,1)} %pad_maximum_fusion.8), channel_id=1, source_target_pairs={{0,16},{16,0},{8,24},{24,8},{1,17},{17,1},{9,25},{25,9},{2,18},{18... | collective-permute-start | bytes 4325384 | tf_op jit(solution)/shard_map/ppermute | solution.py:49
  206.4 150.9 %reduce-scatter.9.cloned.1.call-start = ((), (), s32[]{:S(2)}) async-start(), calls=%async_computation.7 | async-start | bytes 7208960 | tf_op jit(solution)/shard_map/reduce_scatter | solution.py:459
  215.3 13.3 %collective-permute-start.13 = (bf16[256,512]{1,0:T(8,128)(2,1)}, bf16[256,512]{1,0:T(8,128)(2,1)S(1)}, u32[]{:S(2)}, u32[]{:S(2)}) collective-permute-start(bf16[256,512]{1,0:T(8,128)(2,1)} %get-tuple-element.167), channel_id=1, source_target_pairs={{0,16},{16,0},{8,24},{24,8},{1,17},{17,1},{9,25},{25,9},{2,18},{18... | collective-permute-start | bytes 786440 | tf_op jit(solution)/shard_map/ppermute | solution.py:49
  216.8 29.4 %collective-permute-start.12 = (bf16[256,2048]{1,0:T(8,128)(2,1)}, bf16[256,2048]{1,0:T(8,128)(2,1)}, u32[]{:S(2)}, u32[]{:S(2)}) collective-permute-start(bf16[256,2048]{1,0:T(8,128)(2,1)} %copy-done.14), channel_id=1, source_target_pairs={{0,16},{16,0},{8,24},{24,8},{1,17},{17,1},{9,25},{25,9},{2,18},{18... | collective-permute-start | bytes 3145736 | tf_op jit(solution)/shard_map/ppermute | solution.py:49
  252.9 169.2 %reduce-scatter.11.cloned.1.call-start = ((), (), s32[]{:S(2)}) async-start(), calls=%async_computation.8 | async-start | bytes 3932160 | tf_op jit(solution)/shard_map/reduce_scatter | solution.py:295
  261.3 13.5 %collective-permute-start.24 = (bf16[256,1024]{1,0:T(8,128)(2,1)S(1)}, bf16[256,1024]{1,0:T(8,128)(2,1)S(1)}, u32[]{:S(2)}, u32[]{:S(2)}) collective-permute-start(bf16[256,1024]{1,0:T(8,128)(2,1)S(1)} %pad_maximum_fusion.12), channel_id=1, source_target_pairs={{0,16},{16,0},{8,24},{24,8},{1,17},{17,1},{9,25},{25,9},{2,18},{18... | collective-permute-start | bytes 1572872 | tf_op jit(solution)/shard_map/ppermute | solution.py:49
  264.2 14.1 %collective-permute-start.23 = (bf16[512,1024]{1,0:T(8,128)(2,1)S(1)}, bf16[512,1024]{1,0:T(8,128)(2,1)S(1)}, u32[]{:S(2)}, u32[]{:S(2)}) collective-permute-start(bf16[512,1024]{1,0:T(8,128)(2,1)S(1)} %get-tuple-element.149), channel_id=1, source_target_pairs={{0,8},{8,0},{16,24},{24,16},{1,9},{9,1},{17,25},{25,17},{2,10},{10... | collective-permute-start | bytes 3145736 | tf_op jit(solution)/shard_map/ppermute | solution.py:45
  361.1 188.1 %all-gather.10.cloned.1.call-start = ((), (), s32[]{:S(2)}) async-start(), calls=%async_computation.10 | async-start | bytes 24510464 | tf_op jit(solution)/shard_map/all_gather | solution.py:284
  361.7 320.2 %all-gather.8.cloned.1.call-start = ((), (), s32[]{:S(2)}) async-start(), calls=%async_computation.9 | async-start | bytes 25624576 | tf_op jit(solution)/shard_map/all_gather | solution.py:297
  432.8 14.9 %collective-permute-start.16 = (bf16[256,1024]{1,0:T(8,128)(2,1)S(1)}, bf16[256,1024]{1,0:T(8,128)(2,1)S(1)}, u32[]{:S(2)}, u32[]{:S(2)}) collective-permute-start(bf16[256,1024]{1,0:T(8,128)(2,1)S(1)} %dynamic-slice_convert_fusion), channel_id=1, source_target_pairs={{0,1},{1,0},{2,3},{3,2},{4,5},{5,4},{6,7},{7,6},{8,9},{9,8},{10,11... | collective-permute-start | bytes 1572872 | tf_op jit(solution)/shard_map/ppermute | solution.py:35
  440.7 16.7 %collective-permute-start.8 = (bf16[256,1024]{1,0:T(8,128)(2,1)S(1)}, bf16[256,1024]{1,0:T(8,128)(2,1)S(1)}, u32[]{:S(2)}, u32[]{:S(2)}) collective-permute-start(bf16[256,1024]{1,0:T(8,128)(2,1)S(1)} %dynamic-slice_convert_fusion.1), channel_id=1, source_target_pairs={{0,1},{1,0},{2,3},{3,2},{4,5},{5,4},{6,7},{7,6},{8,9},{9,8},{10,11... | collective-permute-start | bytes 1572872 | tf_op jit(solution)/shard_map/ppermute | solution.py:35
  452.0 7.7 %collective-permute-start.19 = (f32[2,1024]{1,0:T(2,128)S(1)}, f32[2,1024]{1,0:T(2,128)S(1)}, u32[]{:S(2)}, u32[]{:S(2)}) collective-permute-start(f32[2,1024]{1,0:T(2,128)S(1)} %fusion.58), channel_id=1, source_target_pairs={{0,8},{8,0},{16,24},{24,16},{1,9},{9,1},{17,25},{25,17},{2,10},{10... | collective-permute-start | bytes 24584 | tf_op jit(solution)/shard_map/ppermute | solution.py:45
  (47 other events, 283.4 us)
Sparse Core Ops, SparseCore 0:
  20.3 48.4 all-gather.5
  149.0 57.1 reduce-scatter.4
  209.1 43.6 reduce-scatter.6
  255.7 101.5 reduce-scatter.8
  361.3 60.7 reduce-scatter.10
  423.5 125.6 all-gather.9
  551.4 130.4 all-gather.7

commit v4 on v3

--- a/solution.py
+++ b/solution.py
@@ -65,28 +65,33 @@
 
 def key_value_kernel(x_ref, key_ref, value_ref, cos_ref, sin_ref, out_ref):
     x = x_ref[...]
-    keys = turn(dot(x, key_ref[...]), cos_ref[...], sin_ref[...])
-    out_ref[:, :HEAD_DIMENSION] = keys.astype(BF)
-    out_ref[:, HEAD_DIMENSION:] = dot(x, value_ref[...]).astype(BF)
+    keys = dot(x, key_ref[...])
+    values = dot(x, value_ref[...]).astype(BF)
+    for start in range(0, keys.shape[1], HEAD_DIMENSION):
+        head = slice(start, start + HEAD_DIMENSION)
+        turned = turn(keys[:, head], cos_ref[...], sin_ref[...])
+        out_ref[:, 2 * start : 2 * start + HEAD_DIMENSION] = turned.astype(BF)
+        out_ref[:, 2 * start + HEAD_DIMENSION : 2 * (start + HEAD_DIMENSION)] = values[:, head]
 
 
 def keys_and_values(x, key_weight, value_weight, cos, sin):
     rows, width = x.shape
-    heads = key_weight.shape[1] // HEAD_DIMENSION
+    columns = key_weight.shape[1]
+    block = 2 * HEAD_DIMENSION if columns % (2 * HEAD_DIMENSION) == 0 else HEAD_DIMENSION
     whole = lambda step: (0, 0)
     column = lambda step: (0, step)
     return pl.pallas_call(
         key_value_kernel,
-        grid=(heads,),
+        grid=(columns // block,),
         in_specs=[
             pl.BlockSpec((rows, width), whole),
-            pl.BlockSpec((width, HEAD_DIMENSION), column),
-            pl.BlockSpec((width, HEAD_DIMENSION), column),
+            pl.BlockSpec((width, block), column),
+            pl.BlockSpec((width, block), column),
             pl.BlockSpec((rows, HEAD_DIMENSION), whole),
             pl.BlockSpec((rows, HEAD_DIMENSION), whole),
         ],
-        out_specs=pl.BlockSpec((rows, 2 * HEAD_DIMENSION), column),
-        out_shape=jax.ShapeDtypeStruct((rows, 2 * heads * HEAD_DIMENSION), BF),
+        out_specs=pl.BlockSpec((rows, 2 * block), column),
+        out_shape=jax.ShapeDtypeStruct((rows, 2 * columns), BF),
         name="keys_and_values",
     )(x, key_weight, value_weight, cos, sin)
 
@@ -167,14 +172,14 @@
 
 
 def attention(m, length, q, kv_all, query_pos, key_pos, do=None, cos=None, sin=None):
-    total = kv_all.shape[0]
-    heads = kv_all.shape[1] // (2 * HEAD_DIMENSION)
+    _, total, both = kv_all.shape
+    heads = both // (2 * HEAD_DIMENSION)
     block = q.shape[1] // heads
     in_rows = lambda h: (m, h)
     column = lambda h: (0, h)
     in_specs = [
         pl.BlockSpec((length, block), in_rows),
-        pl.BlockSpec((total, 2 * HEAD_DIMENSION), column),
+        pl.BlockSpec((None, total, 2 * HEAD_DIMENSION), lambda h: (m, 0, h)),
         pl.BlockSpec((length, 1), lambda h: (m, 0)),
         pl.BlockSpec((None, 1, total), lambda h: (m, 0, 0)),
     ]
@@ -188,7 +193,7 @@
         in_specs += [pl.BlockSpec((length, HEAD_DIMENSION), lambda h: (m, 0))] * 2
         operands += [do, cos, sin]
         out_specs = [out_specs, pl.BlockSpec((total, 2 * HEAD_DIMENSION), column)]
-        out_shape = [out_shape, jax.ShapeDtypeStruct(kv_all.shape, BF)]
+        out_shape = [out_shape, jax.ShapeDtypeStruct((total, both), BF)]
     return pl.pallas_call(
         kernel,
         grid=(heads,),
@@ -197,7 +202,7 @@
         out_shape=out_shape,
         cost_estimate=pl.CostEstimate(
             flops=(4 if do is None else 10) * length * total * q.shape[1],
-            bytes_accessed=8 * kv_all.size,
+            bytes_accessed=8 * total * both,
             transcendentals=length * total * q.shape[1] // HEAD_DIMENSION,
         ),
         name="attend" if do is None else "attend_back",
@@ -227,9 +232,13 @@
 def share_kernel(every_ref, *out_refs, pieces):
     out_refs = list(out_refs)
     for start, stop, widths in pieces:
+        size = stop - start
         at = 0
         for width in widths:
-            out_refs.pop(0)[...] = every_ref[start:stop, at : at + width].astype(F32)
+            out_ref = out_refs.pop(0)
+            for i in range(every_ref.shape[0]):
+                source = every_ref[i, start:stop, at : at + width]
+                out_ref[i * size : (i + 1) * size, :] = source.astype(F32)
             at += width
 
 
@@ -258,23 +267,23 @@
         spans.append((start, start + size, widths))
 
         def index(device, row_by_core=row_by_core):
-            chip, core, rank = device // (2 * seq), (device // seq) % 2, device % seq
-            row, column = (core, chip) if row_by_core else (chip, core)
-            return row * seq + rank, column
+            chip, core = device // 2, device % 2
+            return (core, chip) if row_by_core else (chip, core)
 
         for width in widths:
-            out_specs.append(pl.BlockSpec((size, width), index))
+            out_specs.append(pl.BlockSpec((seq * size, width), index))
             out_shape.append(jax.ShapeDtypeStruct((2 * seq * size, 2 * width), F32))
         start += size
     return pl.pallas_call(
         functools.partial(share_kernel, pieces=tuple(spans)),
-        grid=(count,),
-        in_specs=[pl.BlockSpec((None, rows, cols), lambda device: (device, 0, 0))],
+        grid=(count // seq,),
+        in_specs=[pl.BlockSpec((seq, rows, cols), lambda device: (device, 0, 0))],
         out_specs=out_specs,
         out_shape=out_shape,
         cost_estimate=pl.CostEstimate(
             flops=0, bytes_accessed=6 * every.size, transcendentals=0
         ),
+        compiler_params=pltpu.CompilerParams(vmem_limit_bytes=48 * 2**20),
         name="write_whole",
     )(every)
 
@@ -382,7 +391,7 @@
     df_other = to_chip(df)
     q = queries(hn1, query_weight, cos, sin)
     dz = dot_t(df, w_down)
-    kv_all, hn1_other, df_other, q, dz, hn1, df = tie(kv_all, hn1_other, df_other, q, dz, hn1, df)
+    kv_all, q, dz = tie(kv_all, q, dz)
 
     def by_core(own, other):
         both = jnp.concatenate([own, other], axis=0)
@@ -396,11 +405,12 @@
     parts = []
     others = []
     for m in range(micro):
-        o = attention(m, length, q, kv_all[m], query_pos, key_pos)
+        o = attention(m, length, q, kv_all, query_pos, key_pos)
         attended.append(o)
         part = dot(o, w_out).astype(BF)
         parts.append(part)
         others.append(swap_tensor(part))
+    hn1_other, df_other, attended[-1] = tie(hn1_other, df_other, attended[-1])
     hn1_core = by_core(hn1, hn1_other)
     df_core = by_core(df, df_other)
     mixed = jnp.concatenate([a.astype(F32) + b for a, b in zip(parts, others)], axis=0)
@@ -442,7 +452,7 @@
     dqs = []
     dkvs = []
     for m in range(micro):
-        dq, dkv = attention(m, length, q, kv_all[m], query_pos, key_pos, do, cos, sin)
+        dq, dkv = attention(m, length, q, kv_all, query_pos, key_pos, do, cos, sin)
         dqs.append(dq)
         dkvs.append(dkv)
     dqb = jnp.concatenate(dqs, axis=0)

time: 719 us -> 711 us (0.989)
  Pallas kernels: 88.8 us -> 81.5 us
    ppermute x9, waiting for transfers between devices: 67.2 us -> 38.1 us  [to_chip(): return lax.ppermute(sent, 'dp', ACROSS)]
    all_gather x1, waiting for transfers between devices: 0.01 us -> 27.4 us  [on_device(): lax.all_gather(kvb.reshape(micro, length, -1), 'seq', axis=1, tiled=True)]
  transfers between devices with their start and end apart: 33 -> 33, of which waited for: 22 -> 21; matrix products, arithmetic and copies ran while one was open for 14% -> 15% of each run, Pallas kernels for 7% -> 8%
where the time goes in v4:
time: 711 us; the launch traced here: 705 us
  waiting for transfers between devices  442 us (62%)
  Pallas kernels  81.5 us (11%)
  matrix products  77.3 us (11%)
  other arithmetic  39.5 us (6%)
  local copies, waits for them, and re-layouts  25.5 us (4%)
  starting transfers between devices  24.9 us (4%)
  between operations  15 us (2%)
    all_gather x1, waiting for transfers between devices, share(): every = lax.all_gather(part, ('dp', 'seq'), axis=0, tiled=False)  111 us
    all_gather x1, waiting for transfers between devices, share(): gate_up = lax.all_gather(gate_up_part, ('dp', 'seq'), axis=0, tiled=False)  80.4 us
    reduce_scatter x1, waiting for transfers between devices, on_device(): lax.psum_scatter(gate_up_quarter, 'seq', scatter_dimension=0, tiled=True)  72.9 us
    reduce_scatter x1, waiting for transfers between devices, share(): part = lax.psum_scatter(joined, 'seq', scatter_dimension=0, tiled=False)  60.3 us
    pallas_call x2, Pallas kernels, write_whole(): pl.pallas_call(functools.partial(share_kernel, pieces=tuple(spans)), grid...  44.4 us
    ppermute x6, waiting for transfers between devices, swap_tensor(): return lax.ppermute(sent, 'tensor', [(0, 1), (1, 0)]).astype(F32)  38.5 us
    ppermute x9, waiting for transfers between devices, to_chip(): return lax.ppermute(sent, 'dp', ACROSS)  38.1 us
    dot_general x7, matrix products, dot_t(): lax.dot_general(a, b, (((1,), (1,)), ((), ())), preferred_element_type=F32)  30.4 us
  transfers between devices with their start and end apart: 33, of which 21 were waited for; matrix products, arithmetic and copies ran while one was open for 15% of the time, Pallas kernels for 8%

profile of v4, /device:TPU:0, one launch (start us, length us, event | category | flops | bytes accessed | tf_op | source)
XLA Modules:
  0.0 705.4 jit_solution(16145700672340822811)
XLA Ops:
  23.4 9.1 %fusion.61 = f32[256,2816]{1,0:T(8,128)} fusion(bf16[256,2048]{1,0:T(8,128)(2,1)S(1)} %get-tuple-element.64, bf16[2816,2048]{1,0:T(8,128)(2,1)} %param.24), kind=kOutput, calls=%fused_computation.148 | convolution fusion | flops 2952790016 | bytes 15466496 | tf_op jit(solution)/shard_map/dot_general | solution.py:25
  32.5 5.4 queries.1.q_ref
  39.8 27.4 %all-gather.6.cloned.1.call-done.kv_ref = bf16[2,512,1024]{2,1,0:T(8,128)(2,1)} async-done(((bf16[2,128,1024]{2,1,0:T(8,128)(2,1)}), bf16[2,512,1024]{2,1,0:T(8,128)(2,1)}) %all-gather.6.cloned.1.call-update) | async-done | bytes 2097168 | tf_op jit(solution)/shard_map/all_gather | solution.py:389
  77.6 5.2 attend.2
  92.6 8.6 %collective-permute-done = bf16[128,2048]{1,0:T(8,128)(2,1)S(1)} collective-permute-done((bf16[128,2048]{1,0:T(8,128)(2,1)S(1)}, bf16[128,2048]{1,0:T(8,128)(2,1)S(1)}, u32[]{:S(2)}, u32[]{:S(2)}) %collective-permute-start) | collective-permute-done | bytes 524320 | tf_op jit(solution)/shard_map/ppermute | solution.py:35
  110.1 8.3 %multiply_convert_fusion = (bf16[256,2816]{1,0:T(8,128)(2,1)S(1)}, bf16[256,2816]{1,0:T(8,128)(2,1)S(1)}, bf16[256,2816]{1,0:T(8,128)(2,1)S(1)}) fusion(f32[256,2816]{1,0:T(8,128)S(1)} %copy-done.33, f32[256,2816]{1,0:T(8,128)S(1)} %fusion.62, bf16[256,2048]{1,0:T(8,128)(2,1)S(1)} %get-tuple-element.84, bf16[2048,2816]{1,0:T(8,128)(2,1)} %param.22), kind=kOutput, calls=%fused_computation.17 | convolution fusion | flops 2963603456 | bytes 22675456 | tf_op jit(solution)/shard_map/dot_general | solution.py:21
  121.2 6.2 fusion.63
  127.5 8.4 %fusion.18 = bf16[256,2048]{1,0:T(8,128)(2,1)} fusion(f32[256,2048]{1,0:T(8,128)S(1)} %fusion.63, bf16[256,2816]{1,0:T(8,128)(2,1)S(1)} %get-tuple-element.86, bf16[2048,2816]{1,0:T(8,128)(2,1)} %param.23), kind=kOutput, calls=%fused_computation.27 | convolution fusion | flops 2953838592 | bytes 16121856 | tf_op jit(solution)/shard_map/dot_general | solution.py:25
  152.8 17.3 %collective-permute-done.9 = bf16[256,2048]{1,0:T(8,128)(2,1)S(1)} collective-permute-done((bf16[256,2048]{1,0:T(8,128)(2,1)}, bf16[256,2048]{1,0:T(8,128)(2,1)S(1)}, u32[]{:S(2)}, u32[]{:S(2)}) %collective-permute-start.9) | collective-permute-done | bytes 1048608 | tf_op jit(solution)/shard_map/ppermute | solution.py:35
  176.6 6.7 attend_back.3
  183.3 6.8 attend_back.2
  195.0 7.3 %collective-permute-done.11 = bf16[256,2816]{1,0:T(8,128)(2,1)} collective-permute-done((bf16[256,2816]{1,0:T(8,128)(2,1)}, bf16[256,2816]{1,0:T(8,128)(2,1)}, u32[]{:S(2)}, u32[]{:S(2)}) %collective-permute-start.11) | collective-permute-done | bytes 1441824 | tf_op jit(solution)/shard_map/ppermute | solution.py:49
  213.3 11.7 %fusion.8 = bf16[1024,2816]{1,0:T(8,128)(2,1)} fusion(bf16[512,2816]{1,0:T(8,128)(2,1)} %collective-permute-done.15, bf16[256,2816]{1,0:T(8,128)(2,1)} %collective-permute-done.11, bf16[256,1408]{1,0:T(8,128)(2,1)} %get-tuple-element.156, bf16[256,1408]{1,0:T(8,128)(2,1)} %get-tuple-element.154, bf16[512,1024]{1,0:T(8,128)(2,1)} %collective-permute-done.14, ...), kind=kOutput, calls=%fused_computation.8 | convolution fusion | flops 5935726592 | bytes 13631488 | tf_op jit(solution)/shard_map/dot_general | solution.py:29
  224.9 17.3 %collective-permute-done.12 = bf16[256,2048]{1,0:T(8,128)(2,1)} collective-permute-done((bf16[256,2048]{1,0:T(8,128)(2,1)}, bf16[256,2048]{1,0:T(8,128)(2,1)}, u32[]{:S(2)}, u32[]{:S(2)}) %collective-permute-start.12) | collective-permute-done | bytes 1048608 | tf_op jit(solution)/shard_map/ppermute | solution.py:49
  258.3 10.4 %collective-permute-done.24 = bf16[256,1024]{1,0:T(8,128)(2,1)S(1)} collective-permute-done((bf16[256,1024]{1,0:T(8,128)(2,1)S(1)}, bf16[256,1024]{1,0:T(8,128)(2,1)S(1)}, u32[]{:S(2)}, u32[]{:S(2)}) %collective-permute-start.24) | collective-permute-done | bytes 524320 | tf_op jit(solution)/shard_map/ppermute | solution.py:49
  278.4 72.9 %reduce-scatter.9.cloned.1.call-done = bf16[256,2816]{1,0:T(8,128)(2,1)} async-done(((bf16[1024,2816]{1,0:T(8,128)(2,1)}), bf16[256,2816]{1,0:T(8,128)(2,1)}) %reduce-scatter.9.cloned.1.call-update) | async-done | bytes 1441808 | tf_op jit(solution)/shard_map/reduce_scatter | solution.py:469
  355.8 60.3 %reduce-scatter.11.cloned.1.call-done = bf16[1,384,1024]{2,1,0:T(8,128)(2,1)} async-done(((bf16[4,384,1024]{2,1,0:T(8,128)(2,1)}), bf16[1,384,1024]{2,1,0:T(8,128)(2,1)}) %reduce-scatter.11.cloned.1.call-update) | async-done | bytes 786448 | tf_op jit(solution)/shard_map/reduce_scatter | solution.py:304
  428.3 6.4 fusion.64
  435.5 6.2 collective-permute-done.16
  446.1 5.3 collective-permute-done.8
  462.8 80.4 %all-gather.10.cloned.1.call-done = bf16[4096,2816]{1,0:T(8,128)(2,1)} async-done(((bf16[256,2816]{1,0:T(8,128)(2,1)}), bf16[4096,2816]{1,0:T(8,128)(2,1)}) %all-gather.10.cloned.1.call-update) | async-done | bytes 23068688 | tf_op jit(solution)/shard_map/all_gather | solution.py:293
  543.2 22.0 %write_whole.3 = (f32[2048,2816]{1,0:T(8,128)}, f32[2048,2816]{1,0:T(8,128)}) custom-call(bf16[16,256,2816]{2,1,0:T(8,128)(2,1)} %bitcast.75), custom_call_target="tpu_custom_call" | custom-call | bytes 69206016 | tf_op jit(solution)/shard_map/write_whole/pallas_call | solution.py:277
  565.2 110.8 %all-gather.8.cloned.1.call-done = bf16[11776,1024]{1,0:T(8,128)(2,1)} async-done(((bf16[736,1024]{1,0:T(8,128)(2,1)}), bf16[11776,1024]{1,0:T(8,128)(2,1)}) %all-gather.8.cloned.1.call-update) | async-done | bytes 24117264 | tf_op jit(solution)/shard_map/all_gather | solution.py:306
  675.9 22.4 %write_whole.2 = (f32[2816,2048]{1,0:T(8,128)}, f32[1024,2048]{1,0:T(8,128)}, f32[2048,1024]{1,0:T(8,128)}, f32[2048,512]{1,0:T(8,128)}, f32[2048,512]{1,0:T(8,128)}) custom-call(bf16[16,736,1024]{2,1,0:T(8,128)(2,1)} %bitcast.74), custom_call_target="tpu_custom_call" | custom-call | bytes 72351744 | tf_op jit(solution)/shard_map/write_whole/pallas_call | solution.py:277
  (225 shorter events, 147.5 us)
Async XLA Ops:
  7.2 60.0 %all-gather.6.cloned.1.call-start = ((), (), s32[]{:S(2)}) async-start(), calls=%async_computation.4 | async-start | bytes 2621440 | tf_op jit(solution)/shard_map/all_gather | solution.py:389
  18.4 183.9 %reduce-scatter.5.cloned.1.call-start = ((), (), s32[]{:S(2)}) async-start(), calls=%async_computation.5 | async-start | bytes 3604480 | tf_op jit(solution)/shard_map/reduce_scatter | solution.py:441
  18.4 68.2 %collective-permute-start.2 = (bf16[256,2048]{1,0:T(8,128)(2,1)S(1)}, bf16[256,2048]{1,0:T(8,128)(2,1)}, u32[]{:S(2)}, u32[]{:S(2)}) collective-permute-start(bf16[256,2048]{1,0:T(8,128)(2,1)S(1)} %copy-done.3), channel_id=1, source_target_pairs={{0,16},{16,0},{8,24},{24,8},{1,17},{17,1},{9,25},{25,9},{2,18},{18... | collective-permute-start | bytes 3145736 | tf_op jit(solution)/shard_map/ppermute | solution.py:49
  21.4 65.2 %collective-permute-start.3 = (bf16[256,2048]{1,0:T(8,128)(2,1)S(1)}, bf16[256,2048]{1,0:T(8,128)(2,1)}, u32[]{:S(2)}, u32[]{:S(2)}) collective-permute-start(bf16[256,2048]{1,0:T(8,128)(2,1)S(1)} %get-tuple-element.64), channel_id=1, source_target_pairs={{0,16},{16,0},{8,24},{24,8},{1,17},{17,1},{9,25},{25,9},{2,18},{18... | collective-permute-start | bytes 3145736 | tf_op jit(solution)/shard_map/ppermute | solution.py:49
  76.2 15.1 %collective-permute-start.1 = (bf16[128,2048]{1,0:T(8,128)(2,1)}, bf16[128,2048]{1,0:T(8,128)(2,1)}, u32[]{:S(2)}, u32[]{:S(2)}) collective-permute-start(bf16[128,2048]{1,0:T(8,128)(2,1)} %convolution_convert_fusion.1), channel_id=1, source_target_pairs={{0,1},{1,0},{2,3},{3,2},{4,5},{5,4},{6,7},{7,6},{8,9},{9,8},{10,11... | collective-permute-start | bytes 1572872 | tf_op jit(solution)/shard_map/ppermute | solution.py:35
  86.0 15.2 %collective-permute-start = (bf16[128,2048]{1,0:T(8,128)(2,1)S(1)}, bf16[128,2048]{1,0:T(8,128)(2,1)S(1)}, u32[]{:S(2)}, u32[]{:S(2)}) collective-permute-start(bf16[128,2048]{1,0:T(8,128)(2,1)S(1)} %convolution_convert_fusion.2), channel_id=1, source_target_pairs={{0,1},{1,0},{2,3},{3,2},{4,5},{5,4},{6,7},{7,6},{8,9},{9,8},{10,11... | collective-permute-start | bytes 1572872 | tf_op jit(solution)/shard_map/ppermute | solution.py:35
  88.2 14.4 %collective-permute-start.4 = (bf16[512,1024]{1,0:T(8,128)(2,1)S(1)}, bf16[512,1024]{1,0:T(8,128)(2,1)S(1)}, u32[]{:S(2)}, u32[]{:S(2)}) collective-permute-start(bf16[512,1024]{1,0:T(8,128)(2,1)S(1)} %get-tuple-element.153), channel_id=1, source_target_pairs={{0,8},{8,0},{16,24},{24,16},{1,9},{9,1},{17,25},{25,17},{2,10},{10... | collective-permute-start | bytes 3145736 | tf_op jit(solution)/shard_map/ppermute | solution.py:45
  91.1 13.1 %collective-permute-start.5 = (bf16[512,1024]{1,0:T(8,128)(2,1)S(1)}, bf16[512,1024]{1,0:T(8,128)(2,1)S(1)}, u32[]{:S(2)}, u32[]{:S(2)}) collective-permute-start(bf16[512,1024]{1,0:T(8,128)(2,1)S(1)} %get-tuple-element.151), channel_id=1, source_target_pairs={{0,8},{8,0},{16,24},{24,16},{1,9},{9,1},{17,25},{25,17},{2,10},{10... | collective-permute-start | bytes 3145736 | tf_op jit(solution)/shard_map/ppermute | solution.py:45
  119.6 17.0 %collective-permute-start.6 = (bf16[256,1408]{1,0:T(8,128)(2,1)S(1)}, bf16[256,1408]{1,0:T(8,128)(2,1)S(1)}, u32[]{:S(2)}, u32[]{:S(2)}) collective-permute-start(bf16[256,1408]{1,0:T(8,128)(2,1)S(1)} %get-tuple-element.159), channel_id=1, source_target_pairs={{0,16},{16,0},{8,24},{24,8},{1,17},{17,1},{9,25},{25,9},{2,18},{18... | collective-permute-start | bytes 2162696 | tf_op jit(solution)/shard_map/ppermute | solution.py:49
  144.5 102.3 %reduce-scatter.7.cloned.1.call-start = ((), (), s32[]{:S(2)}) async-start(), calls=%async_computation.6 | async-start | bytes 2621440 | tf_op jit(solution)/shard_map/reduce_scatter | solution.py:462
  144.6 25.5 %collective-permute-start.9 = (bf16[256,2048]{1,0:T(8,128)(2,1)}, bf16[256,2048]{1,0:T(8,128)(2,1)S(1)}, u32[]{:S(2)}, u32[]{:S(2)}) collective-permute-start(bf16[256,2048]{1,0:T(8,128)(2,1)} %fusion.18), channel_id=1, source_target_pairs={{0,1},{1,0},{2,3},{3,2},{4,5},{5,4},{6,7},{7,6},{8,9},{9,8},{10,11... | collective-permute-start | bytes 3145736 | tf_op jit(solution)/shard_map/ppermute | solution.py:35
  146.1 48.8 %collective-permute-start.10 = (bf16[256,2048]{1,0:T(8,128)(2,1)}, bf16[256,2048]{1,0:T(8,128)(2,1)}, u32[]{:S(2)}, u32[]{:S(2)}) collective-permute-start(bf16[256,2048]{1,0:T(8,128)(2,1)} %copy-done.15), channel_id=1, source_target_pairs={{0,16},{16,0},{8,24},{24,8},{1,17},{17,1},{9,25},{25,9},{2,18},{18... | collective-permute-start | bytes 3145736 | tf_op jit(solution)/shard_map/ppermute | solution.py:49
  152.2 50.1 %collective-permute-start.11 = (bf16[256,2816]{1,0:T(8,128)(2,1)}, bf16[256,2816]{1,0:T(8,128)(2,1)}, u32[]{:S(2)}, u32[]{:S(2)}) collective-permute-start(bf16[256,2816]{1,0:T(8,128)(2,1)} %pad_maximum_fusion.8), channel_id=1, source_target_pairs={{0,16},{16,0},{8,24},{24,8},{1,17},{17,1},{9,25},{25,9},{2,18},{18... | collective-permute-start | bytes 4325384 | tf_op jit(solution)/shard_map/ppermute | solution.py:49
  202.3 149.0 %reduce-scatter.9.cloned.1.call-start = ((), (), s32[]{:S(2)}) async-start(), calls=%async_computation.7 | async-start | bytes 7208960 | tf_op jit(solution)/shard_map/reduce_scatter | solution.py:469
  211.2 13.7 %collective-permute-start.13 = (bf16[256,512]{1,0:T(8,128)(2,1)}, bf16[256,512]{1,0:T(8,128)(2,1)S(1)}, u32[]{:S(2)}, u32[]{:S(2)}) collective-permute-start(bf16[256,512]{1,0:T(8,128)(2,1)} %get-tuple-element.163), channel_id=1, source_target_pairs={{0,16},{16,0},{8,24},{24,8},{1,17},{17,1},{9,25},{25,9},{2,18},{18... | collective-permute-start | bytes 786440 | tf_op jit(solution)/shard_map/ppermute | solution.py:49
  212.7 29.5 %collective-permute-start.12 = (bf16[256,2048]{1,0:T(8,128)(2,1)}, bf16[256,2048]{1,0:T(8,128)(2,1)}, u32[]{:S(2)}, u32[]{:S(2)}) collective-permute-start(bf16[256,2048]{1,0:T(8,128)(2,1)} %copy-done.10), channel_id=1, source_target_pairs={{0,16},{16,0},{8,24},{24,8},{1,17},{17,1},{9,25},{25,9},{2,18},{18... | collective-permute-start | bytes 3145736 | tf_op jit(solution)/shard_map/ppermute | solution.py:49
  246.9 169.2 %reduce-scatter.11.cloned.1.call-start = ((), (), s32[]{:S(2)}) async-start(), calls=%async_computation.8 | async-start | bytes 3932160 | tf_op jit(solution)/shard_map/reduce_scatter | solution.py:304
  255.3 13.5 %collective-permute-start.24 = (bf16[256,1024]{1,0:T(8,128)(2,1)S(1)}, bf16[256,1024]{1,0:T(8,128)(2,1)S(1)}, u32[]{:S(2)}, u32[]{:S(2)}) collective-permute-start(bf16[256,1024]{1,0:T(8,128)(2,1)S(1)} %pad_maximum_fusion.12), channel_id=1, source_target_pairs={{0,16},{16,0},{8,24},{24,8},{1,17},{17,1},{9,25},{25,9},{2,18},{18... | collective-permute-start | bytes 1572872 | tf_op jit(solution)/shard_map/ppermute | solution.py:49
  258.2 14.1 %collective-permute-start.23 = (bf16[512,1024]{1,0:T(8,128)(2,1)S(1)}, bf16[512,1024]{1,0:T(8,128)(2,1)S(1)}, u32[]{:S(2)}, u32[]{:S(2)}) collective-permute-start(bf16[512,1024]{1,0:T(8,128)(2,1)S(1)} %get-tuple-element.147), channel_id=1, source_target_pairs={{0,8},{8,0},{16,24},{24,16},{1,9},{9,1},{17,25},{25,17},{2,10},{10... | collective-permute-start | bytes 3145736 | tf_op jit(solution)/shard_map/ppermute | solution.py:45
  355.1 188.1 %all-gather.10.cloned.1.call-start = ((), (), s32[]{:S(2)}) async-start(), calls=%async_computation.10 | async-start | bytes 24510464 | tf_op jit(solution)/shard_map/all_gather | solution.py:293
  355.7 320.2 %all-gather.8.cloned.1.call-start = ((), (), s32[]{:S(2)}) async-start(), calls=%async_computation.9 | async-start | bytes 25624576 | tf_op jit(solution)/shard_map/all_gather | solution.py:306
  426.8 14.9 %collective-permute-start.16 = (bf16[256,1024]{1,0:T(8,128)(2,1)S(1)}, bf16[256,1024]{1,0:T(8,128)(2,1)S(1)}, u32[]{:S(2)}, u32[]{:S(2)}) collective-permute-start(bf16[256,1024]{1,0:T(8,128)(2,1)S(1)} %dynamic-slice_convert_fusion), channel_id=1, source_target_pairs={{0,1},{1,0},{2,3},{3,2},{4,5},{5,4},{6,7},{7,6},{8,9},{9,8},{10,11... | collective-permute-start | bytes 1572872 | tf_op jit(solution)/shard_map/ppermute | solution.py:35
  434.8 16.5 %collective-permute-start.8 = (bf16[256,1024]{1,0:T(8,128)(2,1)S(1)}, bf16[256,1024]{1,0:T(8,128)(2,1)S(1)}, u32[]{:S(2)}, u32[]{:S(2)}) collective-permute-start(bf16[256,1024]{1,0:T(8,128)(2,1)S(1)} %dynamic-slice_convert_fusion.1), channel_id=1, source_target_pairs={{0,1},{1,0},{2,3},{3,2},{4,5},{5,4},{6,7},{7,6},{8,9},{9,8},{10,11... | collective-permute-start | bytes 1572872 | tf_op jit(solution)/shard_map/ppermute | solution.py:35
  446.0 7.7 %collective-permute-start.19 = (f32[2,1024]{1,0:T(2,128)S(1)}, f32[2,1024]{1,0:T(2,128)S(1)}, u32[]{:S(2)}, u32[]{:S(2)}) collective-permute-start(f32[2,1024]{1,0:T(2,128)S(1)} %fusion.58), channel_id=1, source_target_pairs={{0,8},{8,0},{16,24},{24,16},{1,9},{9,1},{17,25},{25,17},{2,10},{10... | collective-permute-start | bytes 24584 | tf_op jit(solution)/shard_map/ppermute | solution.py:45
  (46 other events, 251.6 us)
Sparse Core Ops, SparseCore 0:
  18.5 48.6 all-gather.5
  144.7 55.5 reduce-scatter.4
  203.1 43.7 reduce-scatter.6
  249.7 101.5 reduce-scatter.8
  355.3 60.7 reduce-scatter.10
  417.6 125.6 all-gather.9
  545.4 130.4 all-gather.7

commit v5 on v4

--- a/solution.py
+++ b/solution.py
@@ -253,8 +253,8 @@
             at = 0
             for width in widths:
                 piece = every[:, start : start + size, at : at + width]
-                piece = piece.reshape(2, 2, seq, size, width)
-                piece = piece.transpose((1, 2, 3, 0, 4) if row_by_core else (0, 2, 3, 1, 4))
+                piece = piece.reshape(seq, 2, 2, size, width)
+                piece = piece.transpose((2, 0, 3, 1, 4) if row_by_core else (1, 0, 3, 2, 4))
                 results.append(piece.reshape(2 * seq * size, 2 * width).astype(F32))
                 at += width
             start += size
@@ -277,7 +277,7 @@
     return pl.pallas_call(
         functools.partial(share_kernel, pieces=tuple(spans)),
         grid=(count // seq,),
-        in_specs=[pl.BlockSpec((seq, rows, cols), lambda device: (device, 0, 0))],
+        in_specs=[pl.BlockSpec((seq, None, rows, cols), lambda device: (0, device, 0, 0))],
         out_specs=out_specs,
         out_shape=out_shape,
         cost_estimate=pl.CostEstimate(
@@ -285,12 +285,12 @@
         ),
         compiler_params=pltpu.CompilerParams(vmem_limit_bytes=48 * 2**20),
         name="write_whole",
-    )(every)
+    )(every.reshape(seq, count // seq, rows, cols))
 
 
 def share(down_part, gate_up_part, out_quarter, qkv_quarter, widths):
     half_ff = gate_up_part.shape[1] // 2
-    gate_up = lax.all_gather(gate_up_part, ("dp", "seq"), axis=0, tiled=False)
+    gate_up = lax.all_gather(gate_up_part, ("seq", "dp"), axis=0, tiled=False)
     gate, up = write_whole(gate_up, [(gate_up_part.shape[0], (half_ff, half_ff), True)])
     seq = lax.axis_size("seq")
     cols = out_quarter.shape[1]
@@ -303,7 +303,7 @@
         )
         part = lax.psum_scatter(joined, "seq", scatter_dimension=0, tiled=False)
         part = jnp.concatenate([down_part, part.reshape(out_rows + qkv_rows, cols)], axis=0)
-        every = lax.all_gather(part, ("dp", "seq"), axis=0, tiled=False)
+        every = lax.all_gather(part, ("seq", "dp"), axis=0, tiled=False)
         down, out, query, key, value = write_whole(
             every,
             [(down_rows, (cols,), False), (out_rows, (cols,), False), (qkv_rows, widths, True)],
@@ -312,11 +312,11 @@
         out_part = lax.psum_scatter(out_quarter, "seq", scatter_dimension=0, tiled=True)
         qkv_part = lax.psum_scatter(qkv_quarter, "seq", scatter_dimension=0, tiled=True)
         part = jnp.concatenate([down_part, out_part], axis=0)
-        every = lax.all_gather(part, ("dp", "seq"), axis=0, tiled=False)
+        every = lax.all_gather(part, ("seq", "dp"), axis=0, tiled=False)
         down, out = write_whole(
             every, [(down_rows, (cols,), False), (out_rows, (cols,), False)]
         )
-        every = lax.all_gather(qkv_part, ("dp", "seq"), axis=0, tiled=False)
+        every = lax.all_gather(qkv_part, ("seq", "dp"), axis=0, tiled=False)
         query, key, value = write_whole(every, [(qkv_rows, widths, True)])
     return dict(gate=gate, up=up, down=down, out=out, query=query, key=key, value=value)
 

time: 711 us -> 698 us (0.982)
  waiting for transfers between devices: 442 us -> 428 us
    all_gather x2, waiting for transfers between devices: 191 us -> 178 us  [the longest x1 104 us: share(): every = lax.all_gather(part, ('seq', 'dp'), axis=0, tiled=False)]
where the time goes in v5:
time: 698 us; the launch traced here: 692 us
  waiting for transfers between devices  428 us (61%)
  Pallas kernels  81.6 us (12%)
  matrix products  77.3 us (11%)
  other arithmetic  39.5 us (6%)
  local copies, waits for them, and re-layouts  25.9 us (4%)
  starting transfers between devices  24.5 us (4%)
  between operations  15 us (2%)
    all_gather x1, waiting for transfers between devices, share(): every = lax.all_gather(part, ('seq', 'dp'), axis=0, tiled=False)  104 us
    all_gather x1, waiting for transfers between devices, share(): gate_up = lax.all_gather(gate_up_part, ('seq', 'dp'), axis=0, tiled=False)  73.8 us
    reduce_scatter x1, waiting for transfers between devices, on_device(): lax.psum_scatter(gate_up_quarter, 'seq', scatter_dimension=0, tiled=True)  72.9 us
    reduce_scatter x1, waiting for transfers between devices, share(): part = lax.psum_scatter(joined, 'seq', scatter_dimension=0, tiled=False)  60.3 us
    pallas_call x2, Pallas kernels, write_whole(): pl.pallas_call(functools.partial(share_kernel, pieces=tuple(spans)), grid...  44.5 us
    ppermute x9, waiting for transfers between devices, to_chip(): return lax.ppermute(sent, 'dp', ACROSS)  38.5 us
    ppermute x6, waiting for transfers between devices, swap_tensor(): return lax.ppermute(sent, 'tensor', [(0, 1), (1, 0)]).astype(F32)  38 us
    dot_general x7, matrix products, dot_t(): lax.dot_general(a, b, (((1,), (1,)), ((), ())), preferred_element_type=F32)  30.4 us
  transfers between devices with their start and end apart: 33, of which 21 were waited for; matrix products, arithmetic and copies ran while one was open for 15% of the time, Pallas kernels for 8%

profile of v5, /device:TPU:0, one launch (start us, length us, event | category | flops | bytes accessed | tf_op | source)
XLA Modules:
  0.0 692.1 jit_solution(6356614686162630595)
XLA Ops:
  23.4 9.1 %fusion.61 = f32[256,2816]{1,0:T(8,128)} fusion(bf16[256,2048]{1,0:T(8,128)(2,1)S(1)} %get-tuple-element.64, bf16[2816,2048]{1,0:T(8,128)(2,1)} %param.24), kind=kOutput, calls=%fused_computation.148 | convolution fusion | flops 2952790016 | bytes 15466496 | tf_op jit(solution)/shard_map/dot_general | solution.py:25
  32.5 5.4 queries.1.q_ref
  39.8 27.4 %all-gather.6.cloned.1.call-done.kv_ref = bf16[2,512,1024]{2,1,0:T(8,128)(2,1)} async-done(((bf16[2,128,1024]{2,1,0:T(8,128)(2,1)}), bf16[2,512,1024]{2,1,0:T(8,128)(2,1)}) %all-gather.6.cloned.1.call-update) | async-done | bytes 2097168 | tf_op jit(solution)/shard_map/all_gather | solution.py:389
  67.2 5.2 attend.3
  77.6 5.2 attend.2
  92.6 8.6 %collective-permute-done = bf16[128,2048]{1,0:T(8,128)(2,1)S(1)} collective-permute-done((bf16[128,2048]{1,0:T(8,128)(2,1)S(1)}, bf16[128,2048]{1,0:T(8,128)(2,1)S(1)}, u32[]{:S(2)}, u32[]{:S(2)}) %collective-permute-start) | collective-permute-done | bytes 524320 | tf_op jit(solution)/shard_map/ppermute | solution.py:35
  110.1 8.3 %multiply_convert_fusion = (bf16[256,2816]{1,0:T(8,128)(2,1)S(1)}, bf16[256,2816]{1,0:T(8,128)(2,1)S(1)}, bf16[256,2816]{1,0:T(8,128)(2,1)S(1)}) fusion(f32[256,2816]{1,0:T(8,128)S(1)} %copy-done.33, f32[256,2816]{1,0:T(8,128)S(1)} %fusion.62, bf16[256,2048]{1,0:T(8,128)(2,1)S(1)} %get-tuple-element.84, bf16[2048,2816]{1,0:T(8,128)(2,1)} %param.22), kind=kOutput, calls=%fused_computation.17 | convolution fusion | flops 2963603456 | bytes 22675456 | tf_op jit(solution)/shard_map/dot_general | solution.py:21
  121.2 6.2 fusion.63
  127.5 8.4 %fusion.18 = bf16[256,2048]{1,0:T(8,128)(2,1)} fusion(f32[256,2048]{1,0:T(8,128)S(1)} %fusion.63, bf16[256,2816]{1,0:T(8,128)(2,1)S(1)} %get-tuple-element.86, bf16[2048,2816]{1,0:T(8,128)(2,1)} %param.23), kind=kOutput, calls=%fused_computation.27 | convolution fusion | flops 2953838592 | bytes 16121856 | tf_op jit(solution)/shard_map/dot_general | solution.py:25
  152.8 17.3 %collective-permute-done.9 = bf16[256,2048]{1,0:T(8,128)(2,1)S(1)} collective-permute-done((bf16[256,2048]{1,0:T(8,128)(2,1)}, bf16[256,2048]{1,0:T(8,128)(2,1)S(1)}, u32[]{:S(2)}, u32[]{:S(2)}) %collective-permute-start.9) | collective-permute-done | bytes 1048608 | tf_op jit(solution)/shard_map/ppermute | solution.py:35
  176.6 6.7 attend_back.3
  183.3 6.8 attend_back.2
  195.0 7.3 %collective-permute-done.11 = bf16[256,2816]{1,0:T(8,128)(2,1)} collective-permute-done((bf16[256,2816]{1,0:T(8,128)(2,1)}, bf16[256,2816]{1,0:T(8,128)(2,1)}, u32[]{:S(2)}, u32[]{:S(2)}) %collective-permute-start.11) | collective-permute-done | bytes 1441824 | tf_op jit(solution)/shard_map/ppermute | solution.py:49
  213.3 11.7 %fusion.8 = bf16[1024,2816]{1,0:T(8,128)(2,1)} fusion(bf16[512,2816]{1,0:T(8,128)(2,1)} %collective-permute-done.15, bf16[256,2816]{1,0:T(8,128)(2,1)} %collective-permute-done.11, bf16[256,1408]{1,0:T(8,128)(2,1)} %get-tuple-element.156, bf16[256,1408]{1,0:T(8,128)(2,1)} %get-tuple-element.154, bf16[512,1024]{1,0:T(8,128)(2,1)} %collective-permute-done.14, ...), kind=kOutput, calls=%fused_computation.8 | convolution fusion | flops 5935726592 | bytes 13631488 | tf_op jit(solution)/shard_map/dot_general | solution.py:29
  224.9 17.3 %collective-permute-done.12 = bf16[256,2048]{1,0:T(8,128)(2,1)} collective-permute-done((bf16[256,2048]{1,0:T(8,128)(2,1)}, bf16[256,2048]{1,0:T(8,128)(2,1)}, u32[]{:S(2)}, u32[]{:S(2)}) %collective-permute-start.12) | collective-permute-done | bytes 1048608 | tf_op jit(solution)/shard_map/ppermute | solution.py:49
  258.3 10.4 %collective-permute-done.24 = bf16[256,1024]{1,0:T(8,128)(2,1)S(1)} collective-permute-done((bf16[256,1024]{1,0:T(8,128)(2,1)S(1)}, bf16[256,1024]{1,0:T(8,128)(2,1)S(1)}, u32[]{:S(2)}, u32[]{:S(2)}) %collective-permute-start.24) | collective-permute-done | bytes 524320 | tf_op jit(solution)/shard_map/ppermute | solution.py:49
  278.4 72.9 %reduce-scatter.9.cloned.1.call-done = bf16[256,2816]{1,0:T(8,128)(2,1)} async-done(((bf16[1024,2816]{1,0:T(8,128)(2,1)}), bf16[256,2816]{1,0:T(8,128)(2,1)}) %reduce-scatter.9.cloned.1.call-update) | async-done | bytes 1441808 | tf_op jit(solution)/shard_map/reduce_scatter | solution.py:469
  355.8 60.3 %reduce-scatter.11.cloned.1.call-done = bf16[1,384,1024]{2,1,0:T(8,128)(2,1)} async-done(((bf16[4,384,1024]{2,1,0:T(8,128)(2,1)}), bf16[1,384,1024]{2,1,0:T(8,128)(2,1)}) %reduce-scatter.11.cloned.1.call-update) | async-done | bytes 786448 | tf_op jit(solution)/shard_map/reduce_scatter | solution.py:304
  428.4 6.4 fusion.64
  435.9 6.3 collective-permute-done.16
  462.9 73.8 %all-gather.10.cloned.1.call-done = bf16[4096,2816]{1,0:T(8,128)(2,1)} async-done(((bf16[256,2816]{1,0:T(8,128)(2,1)}), bf16[4096,2816]{1,0:T(8,128)(2,1)}) %all-gather.10.cloned.1.call-update) | async-done | bytes 23068688 | tf_op jit(solution)/shard_map/all_gather | solution.py:293
  536.7 22.0 %write_whole.3 = (f32[2048,2816]{1,0:T(8,128)}, f32[2048,2816]{1,0:T(8,128)}) custom-call(bf16[4,4,256,2816]{3,2,1,0:T(8,128)(2,1)} %bitcast.75), custom_call_target="tpu_custom_call" | custom-call | bytes 69206016 | tf_op jit(solution)/shard_map/write_whole/pallas_call | solution.py:277
  558.7 103.9 %all-gather.8.cloned.1.call-done = bf16[11776,1024]{1,0:T(8,128)(2,1)} async-done(((bf16[736,1024]{1,0:T(8,128)(2,1)}), bf16[11776,1024]{1,0:T(8,128)(2,1)}) %all-gather.8.cloned.1.call-update) | async-done | bytes 24117264 | tf_op jit(solution)/shard_map/all_gather | solution.py:306
  662.6 22.4 %write_whole.2 = (f32[2816,2048]{1,0:T(8,128)}, f32[1024,2048]{1,0:T(8,128)}, f32[2048,1024]{1,0:T(8,128)}, f32[2048,512]{1,0:T(8,128)}, f32[2048,512]{1,0:T(8,128)}) custom-call(bf16[4,4,736,1024]{3,2,1,0:T(8,128)(2,1)} %bitcast.74), custom_call_target="tpu_custom_call" | custom-call | bytes 72351744 | tf_op jit(solution)/shard_map/write_whole/pallas_call | solution.py:277
  (225 shorter events, 147.6 us)
Async XLA Ops:
  7.2 60.0 %all-gather.6.cloned.1.call-start = ((), (), s32[]{:S(2)}) async-start(), calls=%async_computation.4 | async-start | bytes 2621440 | tf_op jit(solution)/shard_map/all_gather | solution.py:389
  18.4 183.9 %reduce-scatter.5.cloned.1.call-start = ((), (), s32[]{:S(2)}) async-start(), calls=%async_computation.5 | async-start | bytes 3604480 | tf_op jit(solution)/shard_map/reduce_scatter | solution.py:441
  18.4 68.2 %collective-permute-start.2 = (bf16[256,2048]{1,0:T(8,128)(2,1)S(1)}, bf16[256,2048]{1,0:T(8,128)(2,1)}, u32[]{:S(2)}, u32[]{:S(2)}) collective-permute-start(bf16[256,2048]{1,0:T(8,128)(2,1)S(1)} %copy-done.3), channel_id=1, source_target_pairs={{0,16},{16,0},{8,24},{24,8},{1,17},{17,1},{9,25},{25,9},{2,18},{18... | collective-permute-start | bytes 3145736 | tf_op jit(solution)/shard_map/ppermute | solution.py:49
  21.4 65.2 %collective-permute-start.3 = (bf16[256,2048]{1,0:T(8,128)(2,1)S(1)}, bf16[256,2048]{1,0:T(8,128)(2,1)}, u32[]{:S(2)}, u32[]{:S(2)}) collective-permute-start(bf16[256,2048]{1,0:T(8,128)(2,1)S(1)} %get-tuple-element.64), channel_id=1, source_target_pairs={{0,16},{16,0},{8,24},{24,8},{1,17},{17,1},{9,25},{25,9},{2,18},{18... | collective-permute-start | bytes 3145736 | tf_op jit(solution)/shard_map/ppermute | solution.py:49
  76.2 15.1 %collective-permute-start.1 = (bf16[128,2048]{1,0:T(8,128)(2,1)}, bf16[128,2048]{1,0:T(8,128)(2,1)}, u32[]{:S(2)}, u32[]{:S(2)}) collective-permute-start(bf16[128,2048]{1,0:T(8,128)(2,1)} %convolution_convert_fusion.1), channel_id=1, source_target_pairs={{0,1},{1,0},{2,3},{3,2},{4,5},{5,4},{6,7},{7,6},{8,9},{9,8},{10,11... | collective-permute-start | bytes 1572872 | tf_op jit(solution)/shard_map/ppermute | solution.py:35
  86.0 15.2 %collective-permute-start = (bf16[128,2048]{1,0:T(8,128)(2,1)S(1)}, bf16[128,2048]{1,0:T(8,128)(2,1)S(1)}, u32[]{:S(2)}, u32[]{:S(2)}) collective-permute-start(bf16[128,2048]{1,0:T(8,128)(2,1)S(1)} %convolution_convert_fusion.2), channel_id=1, source_target_pairs={{0,1},{1,0},{2,3},{3,2},{4,5},{5,4},{6,7},{7,6},{8,9},{9,8},{10,11... | collective-permute-start | bytes 1572872 | tf_op jit(solution)/shard_map/ppermute | solution.py:35
  88.2 14.4 %collective-permute-start.4 = (bf16[512,1024]{1,0:T(8,128)(2,1)S(1)}, bf16[512,1024]{1,0:T(8,128)(2,1)S(1)}, u32[]{:S(2)}, u32[]{:S(2)}) collective-permute-start(bf16[512,1024]{1,0:T(8,128)(2,1)S(1)} %get-tuple-element.153), channel_id=1, source_target_pairs={{0,8},{8,0},{16,24},{24,16},{1,9},{9,1},{17,25},{25,17},{2,10},{10... | collective-permute-start | bytes 3145736 | tf_op jit(solution)/shard_map/ppermute | solution.py:45
  91.1 13.1 %collective-permute-start.5 = (bf16[512,1024]{1,0:T(8,128)(2,1)S(1)}, bf16[512,1024]{1,0:T(8,128)(2,1)S(1)}, u32[]{:S(2)}, u32[]{:S(2)}) collective-permute-start(bf16[512,1024]{1,0:T(8,128)(2,1)S(1)} %get-tuple-element.151), channel_id=1, source_target_pairs={{0,8},{8,0},{16,24},{24,16},{1,9},{9,1},{17,25},{25,17},{2,10},{10... | collective-permute-start | bytes 3145736 | tf_op jit(solution)/shard_map/ppermute | solution.py:45
  119.6 17.0 %collective-permute-start.6 = (bf16[256,1408]{1,0:T(8,128)(2,1)S(1)}, bf16[256,1408]{1,0:T(8,128)(2,1)S(1)}, u32[]{:S(2)}, u32[]{:S(2)}) collective-permute-start(bf16[256,1408]{1,0:T(8,128)(2,1)S(1)} %get-tuple-element.159), channel_id=1, source_target_pairs={{0,16},{16,0},{8,24},{24,8},{1,17},{17,1},{9,25},{25,9},{2,18},{18... | collective-permute-start | bytes 2162696 | tf_op jit(solution)/shard_map/ppermute | solution.py:49
  144.5 102.3 %reduce-scatter.7.cloned.1.call-start = ((), (), s32[]{:S(2)}) async-start(), calls=%async_computation.6 | async-start | bytes 2621440 | tf_op jit(solution)/shard_map/reduce_scatter | solution.py:462
  144.6 25.5 %collective-permute-start.9 = (bf16[256,2048]{1,0:T(8,128)(2,1)}, bf16[256,2048]{1,0:T(8,128)(2,1)S(1)}, u32[]{:S(2)}, u32[]{:S(2)}) collective-permute-start(bf16[256,2048]{1,0:T(8,128)(2,1)} %fusion.18), channel_id=1, source_target_pairs={{0,1},{1,0},{2,3},{3,2},{4,5},{5,4},{6,7},{7,6},{8,9},{9,8},{10,11... | collective-permute-start | bytes 3145736 | tf_op jit(solution)/shard_map/ppermute | solution.py:35
  146.1 48.8 %collective-permute-start.10 = (bf16[256,2048]{1,0:T(8,128)(2,1)}, bf16[256,2048]{1,0:T(8,128)(2,1)}, u32[]{:S(2)}, u32[]{:S(2)}) collective-permute-start(bf16[256,2048]{1,0:T(8,128)(2,1)} %copy-done.15), channel_id=1, source_target_pairs={{0,16},{16,0},{8,24},{24,8},{1,17},{17,1},{9,25},{25,9},{2,18},{18... | collective-permute-start | bytes 3145736 | tf_op jit(solution)/shard_map/ppermute | solution.py:49
  152.2 50.1 %collective-permute-start.11 = (bf16[256,2816]{1,0:T(8,128)(2,1)}, bf16[256,2816]{1,0:T(8,128)(2,1)}, u32[]{:S(2)}, u32[]{:S(2)}) collective-permute-start(bf16[256,2816]{1,0:T(8,128)(2,1)} %pad_maximum_fusion.8), channel_id=1, source_target_pairs={{0,16},{16,0},{8,24},{24,8},{1,17},{17,1},{9,25},{25,9},{2,18},{18... | collective-permute-start | bytes 4325384 | tf_op jit(solution)/shard_map/ppermute | solution.py:49
  202.3 149.0 %reduce-scatter.9.cloned.1.call-start = ((), (), s32[]{:S(2)}) async-start(), calls=%async_computation.7 | async-start | bytes 7208960 | tf_op jit(solution)/shard_map/reduce_scatter | solution.py:469
  206.0 7.3 %collective-permute-start.15 = (bf16[512,2816]{1,0:T(8,128)(2,1)}, bf16[512,2816]{1,0:T(8,128)(2,1)}, u32[]{:S(2)}, u32[]{:S(2)}) collective-permute-start(bf16[512,2816]{1,0:T(8,128)(2,1)} %pad_maximum_fusion.1), channel_id=1, source_target_pairs={{0,8},{8,0},{16,24},{24,16},{1,9},{9,1},{17,25},{25,17},{2,10},{10... | collective-permute-start | bytes 8650760 | tf_op jit(solution)/shard_map/ppermute | solution.py:45
  211.2 13.7 %collective-permute-start.13 = (bf16[256,512]{1,0:T(8,128)(2,1)}, bf16[256,512]{1,0:T(8,128)(2,1)S(1)}, u32[]{:S(2)}, u32[]{:S(2)}) collective-permute-start(bf16[256,512]{1,0:T(8,128)(2,1)} %get-tuple-element.163), channel_id=1, source_target_pairs={{0,16},{16,0},{8,24},{24,8},{1,17},{17,1},{9,25},{25,9},{2,18},{18... | collective-permute-start | bytes 786440 | tf_op jit(solution)/shard_map/ppermute | solution.py:49
  212.7 29.5 %collective-permute-start.12 = (bf16[256,2048]{1,0:T(8,128)(2,1)}, bf16[256,2048]{1,0:T(8,128)(2,1)}, u32[]{:S(2)}, u32[]{:S(2)}) collective-permute-start(bf16[256,2048]{1,0:T(8,128)(2,1)} %copy-done.10), channel_id=1, source_target_pairs={{0,16},{16,0},{8,24},{24,8},{1,17},{17,1},{9,25},{25,9},{2,18},{18... | collective-permute-start | bytes 3145736 | tf_op jit(solution)/shard_map/ppermute | solution.py:49
  246.9 169.2 %reduce-scatter.11.cloned.1.call-start = ((), (), s32[]{:S(2)}) async-start(), calls=%async_computation.8 | async-start | bytes 3932160 | tf_op jit(solution)/shard_map/reduce_scatter | solution.py:304
  255.3 13.5 %collective-permute-start.24 = (bf16[256,1024]{1,0:T(8,128)(2,1)S(1)}, bf16[256,1024]{1,0:T(8,128)(2,1)S(1)}, u32[]{:S(2)}, u32[]{:S(2)}) collective-permute-start(bf16[256,1024]{1,0:T(8,128)(2,1)S(1)} %pad_maximum_fusion.12), channel_id=1, source_target_pairs={{0,16},{16,0},{8,24},{24,8},{1,17},{17,1},{9,25},{25,9},{2,18},{18... | collective-permute-start | bytes 1572872 | tf_op jit(solution)/shard_map/ppermute | solution.py:49
  258.2 14.1 %collective-permute-start.23 = (bf16[512,1024]{1,0:T(8,128)(2,1)S(1)}, bf16[512,1024]{1,0:T(8,128)(2,1)S(1)}, u32[]{:S(2)}, u32[]{:S(2)}) collective-permute-start(bf16[512,1024]{1,0:T(8,128)(2,1)S(1)} %get-tuple-element.147), channel_id=1, source_target_pairs={{0,8},{8,0},{16,24},{24,16},{1,9},{9,1},{17,25},{25,17},{2,10},{10... | collective-permute-start | bytes 3145736 | tf_op jit(solution)/shard_map/ppermute | solution.py:45
  355.1 181.6 %all-gather.10.cloned.1.call-start = ((), (), s32[]{:S(2)}) async-start(), calls=%async_computation.10 | async-start | bytes 24510464 | tf_op jit(solution)/shard_map/all_gather | solution.py:293
  355.7 306.9 %all-gather.8.cloned.1.call-start = ((), (), s32[]{:S(2)}) async-start(), calls=%async_computation.9 | async-start | bytes 25624576 | tf_op jit(solution)/shard_map/all_gather | solution.py:306
  427.2 14.9 %collective-permute-start.16 = (bf16[256,1024]{1,0:T(8,128)(2,1)S(1)}, bf16[256,1024]{1,0:T(8,128)(2,1)S(1)}, u32[]{:S(2)}, u32[]{:S(2)}) collective-permute-start(bf16[256,1024]{1,0:T(8,128)(2,1)S(1)} %dynamic-slice_convert_fusion), channel_id=1, source_target_pairs={{0,1},{1,0},{2,3},{3,2},{4,5},{5,4},{6,7},{7,6},{8,9},{9,8},{10,11... | collective-permute-start | bytes 1572872 | tf_op jit(solution)/shard_map/ppermute | solution.py:35
  434.9 16.5 %collective-permute-start.8 = (bf16[256,1024]{1,0:T(8,128)(2,1)S(1)}, bf16[256,1024]{1,0:T(8,128)(2,1)S(1)}, u32[]{:S(2)}, u32[]{:S(2)}) collective-permute-start(bf16[256,1024]{1,0:T(8,128)(2,1)S(1)} %dynamic-slice_convert_fusion.1), channel_id=1, source_target_pairs={{0,1},{1,0},{2,3},{3,2},{4,5},{5,4},{6,7},{7,6},{8,9},{9,8},{10,11... | collective-permute-start | bytes 1572872 | tf_op jit(solution)/shard_map/ppermute | solution.py:35
  (46 other events, 251.5 us)
Sparse Core Ops, SparseCore 0:
  18.5 48.6 all-gather.5
  144.7 55.5 reduce-scatter.4
  203.1 43.7 reduce-scatter.6
  249.7 101.5 reduce-scatter.8
  355.3 60.7 reduce-scatter.10
  417.6 119.0 all-gather.9
  539.0 123.6 all-gather.7

commit v6 on v5

--- a/solution.py
+++ b/solution.py
@@ -63,8 +63,19 @@
     return values * cos + pltpu.roll(values, HEAD_DIMENSION // 2, 1) * sin
 
 
-def key_value_kernel(x_ref, key_ref, value_ref, cos_ref, sin_ref, out_ref):
-    x = x_ref[...]
+def key_value_kernel(
+    x_ref, gain_ref, key_ref, value_ref, cos_ref, sin_ref, out_ref, normed_ref, scale_ref
+):
+    @pl.when(pl.program_id(0) == 0)
+    def _():
+        for start in range(0, x_ref.shape[0], 32):
+            rows = slice(start, start + 32)
+            raw = x_ref[rows, :].astype(F32)
+            scale = lax.rsqrt(jnp.mean(raw * raw, axis=-1, keepdims=True) + EPSILON)
+            scale_ref[rows, :] = scale
+            normed_ref[rows, :] = (raw * scale * gain_ref[...]).astype(BF)
+
+    x = normed_ref[...]
     keys = dot(x, key_ref[...])
     values = dot(x, value_ref[...]).astype(BF)
     for start in range(0, keys.shape[1], HEAD_DIMENSION):
@@ -74,7 +85,7 @@
         out_ref[:, 2 * start + HEAD_DIMENSION : 2 * (start + HEAD_DIMENSION)] = values[:, head]
 
 
-def keys_and_values(x, key_weight, value_weight, cos, sin):
+def keys_and_values(x, gain, key_weight, value_weight, cos, sin):
     rows, width = x.shape
     columns = key_weight.shape[1]
     block = 2 * HEAD_DIMENSION if columns % (2 * HEAD_DIMENSION) == 0 else HEAD_DIMENSION
@@ -85,15 +96,24 @@
         grid=(columns // block,),
         in_specs=[
             pl.BlockSpec((rows, width), whole),
+            pl.BlockSpec((1, width), whole),
             pl.BlockSpec((width, block), column),
             pl.BlockSpec((width, block), column),
             pl.BlockSpec((rows, HEAD_DIMENSION), whole),
             pl.BlockSpec((rows, HEAD_DIMENSION), whole),
         ],
-        out_specs=pl.BlockSpec((rows, 2 * block), column),
-        out_shape=jax.ShapeDtypeStruct((rows, 2 * columns), BF),
+        out_specs=[
+            pl.BlockSpec((rows, 2 * block), column),
+            pl.BlockSpec((rows, width), whole),
+            pl.BlockSpec((rows, 1), whole),
+        ],
+        out_shape=[
+            jax.ShapeDtypeStruct((rows, 2 * columns), BF),
+            jax.ShapeDtypeStruct((rows, width), BF),
+            jax.ShapeDtypeStruct((rows, 1), F32),
+        ],
         name="keys_and_values",
-    )(x, key_weight, value_weight, cos, sin)
+    )(x, gain, key_weight, value_weight, cos, sin)
 
 
 def query_kernel(x_ref, weight_ref, cos_ref, sin_ref, out_ref):
@@ -372,7 +392,6 @@
     x_in = inputs.reshape(rows, width)
     g_in = out_grad.reshape(rows, width)
     in_f = x_in.astype(F32)
-    active = jnp.repeat((1 - skip_mask[:, 0]).astype(F32), length)[:, None]
     offsets = jnp.arange(block_rows, dtype=jnp.int32)
     order = block_order[:, 0]
     key_pos = (order[:, :, None] * block_rows + offsets).reshape(micro, 1, -1)
@@ -380,11 +399,12 @@
     query_pos = (my_blocks[:, :, None] * block_rows + offsets).reshape(rows, 1)
     cos, sin = tables(query_pos[:, 0])
 
-    scale_one = lax.rsqrt(jnp.mean(in_f * in_f, axis=-1, keepdims=True) + EPSILON)
-    hn1 = (in_f * scale_one * gain_one).astype(BF)
+    kvb, hn1, scale_one = keys_and_values(
+        x_in, gain_one[None], key_weight, value_weight, cos, sin
+    )
+    kvb, hn1, g_in, skips = tie(kvb, hn1, g_in, skip_mask[:, 0])
+    active = jnp.repeat((1 - skips).astype(F32), length)[:, None]
     df = (active * g_in.astype(F32)).astype(BF)
-    kvb = keys_and_values(hn1, key_weight, value_weight, cos, sin)
-    kvb, hn1, df = tie(kvb, hn1, df)
 
     kv_all = lax.all_gather(kvb.reshape(micro, length, -1), "seq", axis=1, tiled=True)
     hn1_other = to_chip(hn1)

time: 698 us -> 695 us (level)
  no operation moved by 1% of the time
where the time goes in v6:
time: 695 us; the launch traced here: 690 us
  waiting for transfers between devices  430 us (62%)
  Pallas kernels  82 us (12%)
  matrix products  79.5 us (11%)
  other arithmetic  38.4 us (6%)
  starting transfers between devices  24.9 us (4%)
  local copies, waits for them, and re-layouts  20.6 us (3%)
  between operations  14.9 us (2%)
    all_gather x1, waiting for transfers between devices, share(): every = lax.all_gather(part, ('seq', 'dp'), axis=0, tiled=False)  104 us
    all_gather x1, waiting for transfers between devices, share(): gate_up = lax.all_gather(gate_up_part, ('seq', 'dp'), axis=0, tiled=False)  73.6 us
    reduce_scatter x1, waiting for transfers between devices, on_device(): lax.psum_scatter(gate_up_quarter, 'seq', scatter_dimension=0, tiled=True)  72.9 us
    reduce_scatter x1, waiting for transfers between devices, share(): part = lax.psum_scatter(joined, 'seq', scatter_dimension=0, tiled=False)  60.3 us
    pallas_call x2, Pallas kernels, write_whole(): pl.pallas_call(functools.partial(share_kernel, pieces=tuple(spans)), grid...  44.5 us
    ppermute x6, waiting for transfers between devices, swap_tensor(): return lax.ppermute(sent, 'tensor', [(0, 1), (1, 0)]).astype(F32)  39.2 us
    ppermute x9, waiting for transfers between devices, to_chip(): return lax.ppermute(sent, 'dp', ACROSS)  38.4 us
    dot_general x7, matrix products, dot_t(): lax.dot_general(a, b, (((1,), (1,)), ((), ())), preferred_element_type=F32)  30.3 us
  transfers between devices with their start and end apart: 33, of which 21 were waited for; matrix products, arithmetic and copies ran while one was open for 15% of the time, Pallas kernels for 8%

profile of v6, /device:TPU:0, one launch (start us, length us, event | category | flops | bytes accessed | tf_op | source)
XLA Modules:
  0.0 689.9 jit_solution(13779147933336956597)
XLA Ops:
  19.9 9.0 %fusion.65 = f32[256,2816]{1,0:T(8,128)} fusion(bf16[256,2048]{1,0:T(8,128)(2,1)S(1)} %fusion.19, bf16[2816,2048]{1,0:T(8,128)(2,1)} %param.24), kind=kOutput, calls=%fused_computation.149 | convolution fusion | flops 2952790016 | bytes 15466496 | tf_op jit(solution)/shard_map/dot_general | solution.py:25
  28.9 5.4 queries.1.q_ref
  36.4 27.9 %all-gather.6.cloned.1.call-done.kv_ref = bf16[2,512,1024]{2,1,0:T(8,128)(2,1)} async-done(((bf16[2,128,1024]{2,1,0:T(8,128)(2,1)}), bf16[2,512,1024]{2,1,0:T(8,128)(2,1)}) %all-gather.6.cloned.1.call-update) | async-done | bytes 2097168 | tf_op jit(solution)/shard_map/all_gather | solution.py:409
  64.4 5.2 attend.3
  74.9 5.2 attend.2
  89.9 8.6 %collective-permute-done = bf16[128,2048]{1,0:T(8,128)(2,1)S(1)} collective-permute-done((bf16[128,2048]{1,0:T(8,128)(2,1)S(1)}, bf16[128,2048]{1,0:T(8,128)(2,1)S(1)}, u32[]{:S(2)}, u32[]{:S(2)}) %collective-permute-start) | collective-permute-done | bytes 524320 | tf_op jit(solution)/shard_map/ppermute | solution.py:35
  108.1 9.1 %multiply_convert_fusion = (bf16[256,2816]{1,0:T(8,128)(2,1)S(1)}, bf16[256,2816]{1,0:T(8,128)(2,1)S(1)}, bf16[256,2816]{1,0:T(8,128)(2,1)S(1)}) fusion(f32[256,2816]{1,0:T(8,128)S(1)} %copy-done.32, f32[256,2816]{1,0:T(8,128)} %fusion.66, bf16[256,2048]{1,0:T(8,128)(2,1)S(1)} %get-tuple-element.92, bf16[2048,2816]{1,0:T(8,128)(2,1)} %param.22), kind=kOutput, calls=%fused_computation.17 | convolution fusion | flops 2963603456 | bytes 22675456 | tf_op jit(solution)/shard_map/dot_general | solution.py:21
  119.0 6.2 fusion.67
  125.3 8.4 %fusion.18 = bf16[256,2048]{1,0:T(8,128)(2,1)} fusion(f32[256,2048]{1,0:T(8,128)S(1)} %fusion.67, bf16[256,2816]{1,0:T(8,128)(2,1)S(1)} %get-tuple-element.94, bf16[2048,2816]{1,0:T(8,128)(2,1)} %param.23), kind=kOutput, calls=%fused_computation.27 | convolution fusion | flops 2953838592 | bytes 16121856 | tf_op jit(solution)/shard_map/dot_general | solution.py:25
  150.5 17.3 %collective-permute-done.9 = bf16[256,2048]{1,0:T(8,128)(2,1)S(1)} collective-permute-done((bf16[256,2048]{1,0:T(8,128)(2,1)}, bf16[256,2048]{1,0:T(8,128)(2,1)S(1)}, u32[]{:S(2)}, u32[]{:S(2)}) %collective-permute-start.9) | collective-permute-done | bytes 1048608 | tf_op jit(solution)/shard_map/ppermute | solution.py:35
  174.4 6.7 attend_back.3
  181.2 6.8 attend_back.2
  192.8 7.2 %collective-permute-done.11 = bf16[256,2816]{1,0:T(8,128)(2,1)} collective-permute-done((bf16[256,2816]{1,0:T(8,128)(2,1)}, bf16[256,2816]{1,0:T(8,128)(2,1)}, u32[]{:S(2)}, u32[]{:S(2)}) %collective-permute-start.11) | collective-permute-done | bytes 1441824 | tf_op jit(solution)/shard_map/ppermute | solution.py:49
  211.0 11.7 %fusion.8 = bf16[1024,2816]{1,0:T(8,128)(2,1)} fusion(bf16[512,2816]{1,0:T(8,128)(2,1)} %collective-permute-done.15, bf16[256,2816]{1,0:T(8,128)(2,1)} %collective-permute-done.11, bf16[256,1408]{1,0:T(8,128)(2,1)} %get-tuple-element.166, bf16[256,1408]{1,0:T(8,128)(2,1)} %get-tuple-element.164, bf16[512,1024]{1,0:T(8,128)(2,1)} %collective-permute-done.14, ...), kind=kOutput, calls=%fused_computation.8 | convolution fusion | flops 5935726592 | bytes 13631488 | tf_op jit(solution)/shard_map/dot_general | solution.py:29
  222.7 17.3 %collective-permute-done.12 = bf16[256,2048]{1,0:T(8,128)(2,1)} collective-permute-done((bf16[256,2048]{1,0:T(8,128)(2,1)}, bf16[256,2048]{1,0:T(8,128)(2,1)}, u32[]{:S(2)}, u32[]{:S(2)}) %collective-permute-start.12) | collective-permute-done | bytes 1048608 | tf_op jit(solution)/shard_map/ppermute | solution.py:49
  256.1 10.4 %collective-permute-done.24 = bf16[256,1024]{1,0:T(8,128)(2,1)S(1)} collective-permute-done((bf16[256,1024]{1,0:T(8,128)(2,1)S(1)}, bf16[256,1024]{1,0:T(8,128)(2,1)S(1)}, u32[]{:S(2)}, u32[]{:S(2)}) %collective-permute-start.24) | collective-permute-done | bytes 524320 | tf_op jit(solution)/shard_map/ppermute | solution.py:49
  276.2 72.9 %reduce-scatter.9.cloned.1.call-done = bf16[256,2816]{1,0:T(8,128)(2,1)} async-done(((bf16[1024,2816]{1,0:T(8,128)(2,1)}), bf16[256,2816]{1,0:T(8,128)(2,1)}) %reduce-scatter.9.cloned.1.call-update) | async-done | bytes 1441808 | tf_op jit(solution)/shard_map/reduce_scatter | solution.py:489
  353.6 60.3 %reduce-scatter.11.cloned.1.call-done = bf16[1,384,1024]{2,1,0:T(8,128)(2,1)} async-done(((bf16[4,384,1024]{2,1,0:T(8,128)(2,1)}), bf16[1,384,1024]{2,1,0:T(8,128)(2,1)}) %reduce-scatter.11.cloned.1.call-update) | async-done | bytes 786448 | tf_op jit(solution)/shard_map/reduce_scatter | solution.py:324
  426.4 6.4 fusion.68
  433.9 6.3 collective-permute-done.16
  460.9 73.6 %all-gather.10.cloned.1.call-done = bf16[4096,2816]{1,0:T(8,128)(2,1)} async-done(((bf16[256,2816]{1,0:T(8,128)(2,1)}), bf16[4096,2816]{1,0:T(8,128)(2,1)}) %all-gather.10.cloned.1.call-update) | async-done | bytes 23068688 | tf_op jit(solution)/shard_map/all_gather | solution.py:313
  534.5 22.0 %write_whole.3 = (f32[2048,2816]{1,0:T(8,128)}, f32[2048,2816]{1,0:T(8,128)}) custom-call(bf16[4,4,256,2816]{3,2,1,0:T(8,128)(2,1)} %bitcast.64), custom_call_target="tpu_custom_call" | custom-call | bytes 69206016 | tf_op jit(solution)/shard_map/write_whole/pallas_call | solution.py:297
  556.5 103.9 %all-gather.8.cloned.1.call-done = bf16[11776,1024]{1,0:T(8,128)(2,1)} async-done(((bf16[736,1024]{1,0:T(8,128)(2,1)}), bf16[11776,1024]{1,0:T(8,128)(2,1)}) %all-gather.8.cloned.1.call-update) | async-done | bytes 24117264 | tf_op jit(solution)/shard_map/all_gather | solution.py:326
  660.4 22.4 %write_whole.2 = (f32[2816,2048]{1,0:T(8,128)}, f32[1024,2048]{1,0:T(8,128)}, f32[2048,1024]{1,0:T(8,128)}, f32[2048,512]{1,0:T(8,128)}, f32[2048,512]{1,0:T(8,128)}) custom-call(bf16[4,4,736,1024]{3,2,1,0:T(8,128)(2,1)} %bitcast.63), custom_call_target="tpu_custom_call" | custom-call | bytes 72351744 | tf_op jit(solution)/shard_map/write_whole/pallas_call | solution.py:297
  (219 shorter events, 144.4 us)
Async XLA Ops:
  7.2 57.2 %all-gather.6.cloned.1.call-start = ((), (), s32[]{:S(2)}) async-start(), calls=%async_computation.4 | async-start | bytes 2621440 | tf_op jit(solution)/shard_map/all_gather | solution.py:409
  15.6 184.5 %reduce-scatter.5.cloned.1.call-start = ((), (), s32[]{:S(2)}) async-start(), calls=%async_computation.5 | async-start | bytes 3604480 | tf_op jit(solution)/shard_map/reduce_scatter | solution.py:461
  15.6 68.1 %collective-permute-start.2 = (bf16[256,2048]{1,0:T(8,128)(2,1)}, bf16[256,2048]{1,0:T(8,128)(2,1)}, u32[]{:S(2)}, u32[]{:S(2)}) collective-permute-start(bf16[256,2048]{1,0:T(8,128)(2,1)} %get-tuple-element.70.x_ref), channel_id=1, source_target_pairs={{0,16},{16,0},{8,24},{24,8},{1,17},{17,1},{9,25},{25,9},{2,18},{18... | collective-permute-start | bytes 3145736 | tf_op jit(solution)/shard_map/ppermute | solution.py:49
  19.0 64.8 %collective-permute-start.3 = (bf16[256,2048]{1,0:T(8,128)(2,1)S(1)}, bf16[256,2048]{1,0:T(8,128)(2,1)}, u32[]{:S(2)}, u32[]{:S(2)}) collective-permute-start(bf16[256,2048]{1,0:T(8,128)(2,1)S(1)} %fusion.19), channel_id=1, source_target_pairs={{0,16},{16,0},{8,24},{24,8},{1,17},{17,1},{9,25},{25,9},{2,18},{18... | collective-permute-start | bytes 3145736 | tf_op jit(solution)/shard_map/ppermute | solution.py:49
  73.4 15.1 %collective-permute-start.1 = (bf16[128,2048]{1,0:T(8,128)(2,1)}, bf16[128,2048]{1,0:T(8,128)(2,1)}, u32[]{:S(2)}, u32[]{:S(2)}) collective-permute-start(bf16[128,2048]{1,0:T(8,128)(2,1)} %convolution_convert_fusion.1), channel_id=1, source_target_pairs={{0,1},{1,0},{2,3},{3,2},{4,5},{5,4},{6,7},{7,6},{8,9},{9,8},{10,11... | collective-permute-start | bytes 1572872 | tf_op jit(solution)/shard_map/ppermute | solution.py:35
  83.1 15.4 %collective-permute-start = (bf16[128,2048]{1,0:T(8,128)(2,1)S(1)}, bf16[128,2048]{1,0:T(8,128)(2,1)S(1)}, u32[]{:S(2)}, u32[]{:S(2)}) collective-permute-start(bf16[128,2048]{1,0:T(8,128)(2,1)S(1)} %convolution_convert_fusion.2), channel_id=1, source_target_pairs={{0,1},{1,0},{2,3},{3,2},{4,5},{5,4},{6,7},{7,6},{8,9},{9,8},{10,11... | collective-permute-start | bytes 1572872 | tf_op jit(solution)/shard_map/ppermute | solution.py:35
  85.2 15.6 %collective-permute-start.4 = (bf16[512,1024]{1,0:T(8,128)(2,1)S(1)}, bf16[512,1024]{1,0:T(8,128)(2,1)S(1)}, u32[]{:S(2)}, u32[]{:S(2)}) collective-permute-start(bf16[512,1024]{1,0:T(8,128)(2,1)S(1)} %get-tuple-element.163), channel_id=1, source_target_pairs={{0,8},{8,0},{16,24},{24,16},{1,9},{9,1},{17,25},{25,17},{2,10},{10... | collective-permute-start | bytes 3145736 | tf_op jit(solution)/shard_map/ppermute | solution.py:45
  86.9 15.5 %collective-permute-start.5 = (bf16[512,1024]{1,0:T(8,128)(2,1)S(1)}, bf16[512,1024]{1,0:T(8,128)(2,1)S(1)}, u32[]{:S(2)}, u32[]{:S(2)}) collective-permute-start(bf16[512,1024]{1,0:T(8,128)(2,1)S(1)} %get-tuple-element.161), channel_id=1, source_target_pairs={{0,8},{8,0},{16,24},{24,16},{1,9},{9,1},{17,25},{25,17},{2,10},{10... | collective-permute-start | bytes 3145736 | tf_op jit(solution)/shard_map/ppermute | solution.py:45
  117.4 17.0 %collective-permute-start.6 = (bf16[256,1408]{1,0:T(8,128)(2,1)S(1)}, bf16[256,1408]{1,0:T(8,128)(2,1)S(1)}, u32[]{:S(2)}, u32[]{:S(2)}) collective-permute-start(bf16[256,1408]{1,0:T(8,128)(2,1)S(1)} %get-tuple-element.169), channel_id=1, source_target_pairs={{0,16},{16,0},{8,24},{24,8},{1,17},{17,1},{9,25},{25,9},{2,18},{18... | collective-permute-start | bytes 2162696 | tf_op jit(solution)/shard_map/ppermute | solution.py:49
  142.3 102.3 %reduce-scatter.7.cloned.1.call-start = ((), (), s32[]{:S(2)}) async-start(), calls=%async_computation.6 | async-start | bytes 2621440 | tf_op jit(solution)/shard_map/reduce_scatter | solution.py:482
  142.4 25.5 %collective-permute-start.9 = (bf16[256,2048]{1,0:T(8,128)(2,1)}, bf16[256,2048]{1,0:T(8,128)(2,1)S(1)}, u32[]{:S(2)}, u32[]{:S(2)}) collective-permute-start(bf16[256,2048]{1,0:T(8,128)(2,1)} %fusion.18), channel_id=1, source_target_pairs={{0,1},{1,0},{2,3},{3,2},{4,5},{5,4},{6,7},{7,6},{8,9},{9,8},{10,11... | collective-permute-start | bytes 3145736 | tf_op jit(solution)/shard_map/ppermute | solution.py:35
  143.9 48.9 %collective-permute-start.10 = (bf16[256,2048]{1,0:T(8,128)(2,1)}, bf16[256,2048]{1,0:T(8,128)(2,1)}, u32[]{:S(2)}, u32[]{:S(2)}) collective-permute-start(bf16[256,2048]{1,0:T(8,128)(2,1)} %copy-done.12), channel_id=1, source_target_pairs={{0,16},{16,0},{8,24},{24,8},{1,17},{17,1},{9,25},{25,9},{2,18},{18... | collective-permute-start | bytes 3145736 | tf_op jit(solution)/shard_map/ppermute | solution.py:49
  150.0 50.1 %collective-permute-start.11 = (bf16[256,2816]{1,0:T(8,128)(2,1)}, bf16[256,2816]{1,0:T(8,128)(2,1)}, u32[]{:S(2)}, u32[]{:S(2)}) collective-permute-start(bf16[256,2816]{1,0:T(8,128)(2,1)} %pad_maximum_fusion.8), channel_id=1, source_target_pairs={{0,16},{16,0},{8,24},{24,8},{1,17},{17,1},{9,25},{25,9},{2,18},{18... | collective-permute-start | bytes 4325384 | tf_op jit(solution)/shard_map/ppermute | solution.py:49
  200.1 149.0 %reduce-scatter.9.cloned.1.call-start = ((), (), s32[]{:S(2)}) async-start(), calls=%async_computation.7 | async-start | bytes 7208960 | tf_op jit(solution)/shard_map/reduce_scatter | solution.py:489
  203.8 7.3 %collective-permute-start.15 = (bf16[512,2816]{1,0:T(8,128)(2,1)}, bf16[512,2816]{1,0:T(8,128)(2,1)}, u32[]{:S(2)}, u32[]{:S(2)}) collective-permute-start(bf16[512,2816]{1,0:T(8,128)(2,1)} %pad_maximum_fusion.1), channel_id=1, source_target_pairs={{0,8},{8,0},{16,24},{24,16},{1,9},{9,1},{17,25},{25,17},{2,10},{10... | collective-permute-start | bytes 8650760 | tf_op jit(solution)/shard_map/ppermute | solution.py:45
  209.0 13.7 %collective-permute-start.13 = (bf16[256,512]{1,0:T(8,128)(2,1)}, bf16[256,512]{1,0:T(8,128)(2,1)S(1)}, u32[]{:S(2)}, u32[]{:S(2)}) collective-permute-start(bf16[256,512]{1,0:T(8,128)(2,1)} %get-tuple-element.173), channel_id=1, source_target_pairs={{0,16},{16,0},{8,24},{24,8},{1,17},{17,1},{9,25},{25,9},{2,18},{18... | collective-permute-start | bytes 786440 | tf_op jit(solution)/shard_map/ppermute | solution.py:49
  210.5 29.5 %collective-permute-start.12 = (bf16[256,2048]{1,0:T(8,128)(2,1)}, bf16[256,2048]{1,0:T(8,128)(2,1)}, u32[]{:S(2)}, u32[]{:S(2)}) collective-permute-start(bf16[256,2048]{1,0:T(8,128)(2,1)} %copy-done.7), channel_id=1, source_target_pairs={{0,16},{16,0},{8,24},{24,8},{1,17},{17,1},{9,25},{25,9},{2,18},{18... | collective-permute-start | bytes 3145736 | tf_op jit(solution)/shard_map/ppermute | solution.py:49
  244.7 169.2 %reduce-scatter.11.cloned.1.call-start = ((), (), s32[]{:S(2)}) async-start(), calls=%async_computation.8 | async-start | bytes 3932160 | tf_op jit(solution)/shard_map/reduce_scatter | solution.py:324
  253.1 13.5 %collective-permute-start.24 = (bf16[256,1024]{1,0:T(8,128)(2,1)S(1)}, bf16[256,1024]{1,0:T(8,128)(2,1)S(1)}, u32[]{:S(2)}, u32[]{:S(2)}) collective-permute-start(bf16[256,1024]{1,0:T(8,128)(2,1)S(1)} %pad_maximum_fusion.12), channel_id=1, source_target_pairs={{0,16},{16,0},{8,24},{24,8},{1,17},{17,1},{9,25},{25,9},{2,18},{18... | collective-permute-start | bytes 1572872 | tf_op jit(solution)/shard_map/ppermute | solution.py:49
  256.0 14.1 %collective-permute-start.23 = (bf16[512,1024]{1,0:T(8,128)(2,1)S(1)}, bf16[512,1024]{1,0:T(8,128)(2,1)S(1)}, u32[]{:S(2)}, u32[]{:S(2)}) collective-permute-start(bf16[512,1024]{1,0:T(8,128)(2,1)S(1)} %get-tuple-element.157), channel_id=1, source_target_pairs={{0,8},{8,0},{16,24},{24,16},{1,9},{9,1},{17,25},{25,17},{2,10},{10... | collective-permute-start | bytes 3145736 | tf_op jit(solution)/shard_map/ppermute | solution.py:45
  352.9 181.6 %all-gather.10.cloned.1.call-start = ((), (), s32[]{:S(2)}) async-start(), calls=%async_computation.10 | async-start | bytes 24510464 | tf_op jit(solution)/shard_map/all_gather | solution.py:313
  353.5 306.9 %all-gather.8.cloned.1.call-start = ((), (), s32[]{:S(2)}) async-start(), calls=%async_computation.9 | async-start | bytes 25624576 | tf_op jit(solution)/shard_map/all_gather | solution.py:326
  425.2 14.9 %collective-permute-start.16 = (bf16[256,1024]{1,0:T(8,128)(2,1)S(1)}, bf16[256,1024]{1,0:T(8,128)(2,1)S(1)}, u32[]{:S(2)}, u32[]{:S(2)}) collective-permute-start(bf16[256,1024]{1,0:T(8,128)(2,1)S(1)} %dynamic-slice_convert_fusion), channel_id=1, source_target_pairs={{0,1},{1,0},{2,3},{3,2},{4,5},{5,4},{6,7},{7,6},{8,9},{9,8},{10,11... | collective-permute-start | bytes 1572872 | tf_op jit(solution)/shard_map/ppermute | solution.py:35
  432.9 16.5 %collective-permute-start.8 = (bf16[256,1024]{1,0:T(8,128)(2,1)S(1)}, bf16[256,1024]{1,0:T(8,128)(2,1)S(1)}, u32[]{:S(2)}, u32[]{:S(2)}) collective-permute-start(bf16[256,1024]{1,0:T(8,128)(2,1)S(1)} %dynamic-slice_convert_fusion.1), channel_id=1, source_target_pairs={{0,1},{1,0},{2,3},{3,2},{4,5},{5,4},{6,7},{7,6},{8,9},{9,8},{10,11... | collective-permute-start | bytes 1572872 | tf_op jit(solution)/shard_map/ppermute | solution.py:35
  (45 other events, 264.3 us)
Sparse Core Ops, SparseCore 0:
  15.7 48.6 all-gather.5
  142.4 55.5 reduce-scatter.4
  200.9 43.7 reduce-scatter.6
  247.5 101.5 reduce-scatter.8
  353.1 60.7 reduce-scatter.10
  415.4 119.0 all-gather.9
  536.8 123.6 all-gather.7
